TPU v7x, 256 devices: a whole 4x4x8 slice. The times are simulated.
256 devices in a mesh: span: 8 (over x, y_hi), seq: 32 (over y_lo, z, core).
Axes of the slice: x: 4, y: 4 (y_hi: 2, y_lo: 2; y = y_hi * 2 + y_lo), z: 8, core: 2. Of those that a mesh axis runs over, the one named last changes fastest.
Arguments:
- hidden: bfloat16 [8, 1024, 3072], P('span', 'seq'), may hold values from -6 to 6
- levels: int32 [8], P('span'), may hold values from 0 to 15
- span_order: int32 [8], replicated, may hold values from 0 to 7, each once
- modulation: float32 [16, 3, 3072], replicated, may hold values from -1 to 4
- in_weight: bfloat16 [32, 3072, 384], P('seq'), may hold values from -1 to 1
- out_weight: bfloat16 [32, 128, 3072], P('seq'), may hold values from -0.109375 to 0.109375
- latent_weight: bfloat16 [3072, 64], replicated, may hold values from -0.109375 to 0.109375
- decoder_weight: bfloat16 [3, 3, 3, 16, 512], P(None, None, None, None, 'span'), may hold values from -0.3125 to 0.3125
Outputs:
- block_out: bfloat16 [8, 1024, 3072], P('span', 'seq')
- decoded: bfloat16 [32, 2, 64, 512], P('seq', None, None, 'span')
Inputs may be any that keep to these rules, and one draw needn't show every extreme that they name: `span_order`: each span has a different place in time.
All inputs are finite; a program needn't handle non-finite values.
Results may differ from a plain program's by a relative error of at most 0.03.
Values may be sent and summed in bfloat16 or wider, within the bound.
No kernel may reach another device: no remote copies, remote signals or barrier semaphores. Data moves between devices by JAX's collectives and lax.ppermute only.
A program may use at most 64 MiB of HBM per device.

v0:
```python
import functools
import math

import jax
import jax.numpy as jnp
from jax import lax
from jax.experimental import pallas as pl
from jax.experimental.pallas import tpu as pltpu
from jax.sharding import PartitionSpec as P

HEADS = 24
FR = 4
P_SIZE = 2
C = 16
HD = 128

EPSILON = 1e-06
NEG_LARGE = 1e30

NX, NH, NY, NZ, NC = 4, 2, 2, 8, 2
BLK = 32
QUARTER = NZ * BLK
TAIL = 16


def seq_at(y, z, c):
    return ((y % NY) * NZ + z % NZ) * NC + c % NC


def span_at(x, h):
    return (x % NX) * NH + h % NH


def seq_route(dy=0, dz=0, dc=0):
    return [
        (seq_at(y, z, c), seq_at(y + dy, z + dz, c + dc))
        for y in range(NY)
        for z in range(NZ)
        for c in range(NC)
    ]


def span_route(dx=0, dh=0):
    return [(span_at(x, h), span_at(x + dx, h + dh)) for x in range(NX) for h in range(NH)]


def move_z(a, d):
    return lax.ppermute(a, "seq", seq_route(dz=d))


def move_y(a):
    return lax.ppermute(a, "seq", seq_route(dy=1))


def move_core(a):
    return lax.ppermute(a, "seq", seq_route(dc=1))


def move_x(a, d):
    return lax.ppermute(a, "span", span_route(dx=d))


def move_hi(a):
    return lax.ppermute(a, "span", span_route(dh=1))


HALVES = (
    ((0, 0), (0, 1), (0, 2), (0, 6), (0, 7), (1, 0), (1, 1), (1, 7)),
    ((0, 3), (0, 4), (0, 5), (1, 2), (1, 3), (1, 4), (1, 5), (1, 6)),
)


def block_at(y_apart, core_apart, d):
    half = 0 if (y_apart, d) in HALVES[0] else 1
    return half * 2 * NZ + core_apart * NZ + HALVES[half].index((y_apart, d))


def block_of(at):
    half, core_apart, i = at // (2 * NZ), at // NZ % 2, at % NZ
    y_apart, d = HALVES[half][i]
    return y_apart, core_apart, d


def gather_class(b):
    up1, dn1, y0 = move_z(b, 1), move_z(b, -1), move_y(b)
    up2, dn2 = move_z(up1, 1), move_z(dn1, -1)
    yu1, yd1 = move_y(up1), move_y(dn1)
    up3, dn3 = move_z(up2, 1), move_z(dn2, -1)
    yu2, yd2 = move_y(up2), move_y(dn2)
    far = move_z(up3, 1)
    yu3, yd3 = move_z(yu2, 1), move_z(yd2, -1)
    yfar = lax.ppermute(dn3, "seq", seq_route(dy=1, dz=-1))
    return (b, dn1, dn2, up2, up1, y0, yd1, yu1), (dn3, far, up3, yd2, yd3, yfar, yu3, yu2)


EXP_SCALE = math.log2(math.e) / math.sqrt(HD)


def norm_kernel(level_ref, hidden_ref, mod_ref, out_ref, gate_ref):
    values = hidden_ref[...].astype(jnp.float32)
    row = pl.ds(level_ref[0] % MOD_ROWS, 1)
    center = values - jnp.mean(values, axis=-1, keepdims=True)
    spread = jnp.mean(center * center, axis=-1, keepdims=True)
    scaled = center * lax.rsqrt(spread + EPSILON)
    out_ref[...] = (scaled * (1.0 + mod_ref[1, row, :]) + mod_ref[0, row, :]).astype(jnp.bfloat16)
    gate_ref[...] = mod_ref[2, row, :]


MOD_ROWS = 8


def normalize(levels, rows, modulation):
    width = rows.shape[1]
    return pl.pallas_call(
        norm_kernel,
        grid_spec=pltpu.PrefetchScalarGridSpec(
            num_scalar_prefetch=1,
            grid=(1,),
            in_specs=[
                pl.BlockSpec(rows.shape, lambda i, s: (0, 0)),
                pl.BlockSpec((3, MOD_ROWS, width), lambda i, s: (0, s[0] // MOD_ROWS, 0)),
            ],
            out_specs=[
                pl.BlockSpec(rows.shape, lambda i, s: (0, 0)),
                pl.BlockSpec((1, width), lambda i, s: (0, 0)),
            ],
        ),
        out_shape=[
            jax.ShapeDtypeStruct(rows.shape, jnp.bfloat16),
            jax.ShapeDtypeStruct((1, width), jnp.float32),
        ],
        name="normalize",
    )(levels, rows, modulation.transpose(1, 0, 2))


def latent_kernel(w_ref, gate_ref, lw_ref, o_ref):
    gated = w_ref[...].astype(jnp.float32) * gate_ref[...]
    hi = gated.astype(jnp.bfloat16)
    lo = (gated - hi.astype(jnp.float32)).astype(jnp.bfloat16)
    out = dot_t(hi, lw_ref[...]) + dot_t(lo, lw_ref[...])
    top = out.astype(jnp.bfloat16)
    o_ref[: w_ref.shape[0], :] = top
    o_ref[w_ref.shape[0] :, :] = (out - top.astype(jnp.float32)).astype(jnp.bfloat16)


def latent_matrix(w, gate_row, latent_weight):
    pv = latent_weight.shape[1]
    return pl.pallas_call(
        latent_kernel,
        out_shape=jax.ShapeDtypeStruct((2 * w.shape[0], pv), jnp.bfloat16),
        compiler_params=pltpu.CompilerParams(vmem_limit_bytes=16 * 2**20),
        name="latent_matrix",
    )(w, gate_row, latent_weight.T)


def project_kernel(*refs):
    blocks, (own_ref, oth_ref, mine_ref, theirs_ref, rows) = refs[:NZ], refs[NZ:]
    for i, block in enumerate(blocks):
        rows[i * BLK : i * BLK + BLK, :] = block[...]
    for w_ref, o_ref in ((oth_ref, theirs_ref), (own_ref, mine_ref)):
        out = jnp.dot(rows[...], w_ref[...], preferred_element_type=jnp.float32)
        o_ref[:, :HD] = (out[:, :HD] * EXP_SCALE).astype(jnp.bfloat16)
        o_ref[:, HD:] = out[:, HD:].astype(jnp.bfloat16)


def project(blocks, w_own, w_oth):
    width, cols = w_own.shape
    rows = len(blocks) * BLK
    vmem = pl.BlockSpec(memory_space=pltpu.VMEM)
    return pl.pallas_call(
        project_kernel,
        in_specs=[vmem] * (len(blocks) + 2),
        out_specs=[vmem, vmem],
        out_shape=[jax.ShapeDtypeStruct((rows, cols), jnp.bfloat16)] * 2,
        scratch_shapes=[pltpu.VMEM((rows, width), jnp.bfloat16)],
        compiler_params=pltpu.CompilerParams(vmem_limit_bytes=16 * 2**20),
        cost_estimate=pl.CostEstimate(
            flops=4 * rows * width * cols,
            bytes_accessed=4 * width * cols + 2 * rows * width,
            transcendentals=0,
        ),
        name="project",
    )(*blocks, w_own, w_oth)


def dot_t(a, b):
    return lax.dot_general(a, b, (((1,), (1,)), ((), ())), preferred_element_type=jnp.float32)


TILE = 128


def used_slots(y, z):
    return (y * NZ + z) * NC < HEADS


def self_kernel(s_ref, q_ref, kv_ref, m_ref, o_ref, values):
    y, z, core = s_ref[1], s_ref[2], s_ref[3]
    used = used_slots(y, z)
    values[:, :HD] = kv_ref[:, HD:]
    values[:, HD:] = jnp.ones((values.shape[0], HD), jnp.bfloat16)
    for t in range(q_ref.shape[0] // TILE):
        s = dot_t(q_ref[t * TILE : t * TILE + TILE, :], kv_ref[:, :HD])
        p = jnp.exp2(s - jnp.max(s, axis=1, keepdims=True)).astype(jnp.bfloat16)
        acc = jnp.dot(p, values[...], preferred_element_type=jnp.float32)
        att = (acc[:, :HD] / acc[:, HD:]).astype(jnp.bfloat16)
        att = jnp.concatenate([att, att], axis=1)
        part = jnp.dot(att, m_ref[...], preferred_element_type=jnp.float32)
        part = jnp.where(used, part, 0.0).astype(jnp.bfloat16)
        for j in range(TILE // BLK):
            y_apart, core_apart, d = block_of(t * (TILE // BLK) + j)
            at = ((y ^ y_apart) * NZ + (z + d) % NZ) * NC + (core ^ core_apart)
            o_ref[at] = part[j * BLK : j * BLK + BLK]


def self_attention(place, q, kv, matrix):
    pv = matrix.shape[1]
    rows = q.shape[0]
    return pl.pallas_call(
        self_kernel,
        grid_spec=pltpu.PrefetchScalarGridSpec(
            num_scalar_prefetch=1,
            grid=(1,),
            in_specs=[pl.BlockSpec(a.shape, lambda i, s: (0, 0)) for a in (q, kv, matrix)],
            out_specs=pl.BlockSpec((rows // BLK, BLK, pv), lambda i, s: (0, 0, 0)),
            scratch_shapes=[pltpu.VMEM((rows, 2 * HD), jnp.bfloat16)],
        ),
        out_shape=jax.ShapeDtypeStruct((rows // BLK, BLK, pv), jnp.bfloat16),
        compiler_params=pltpu.CompilerParams(vmem_limit_bytes=16 * 2**20),
        cost_estimate=pl.CostEstimate(
            flops=6 * rows * rows * HD, bytes_accessed=2**20, transcendentals=rows * rows
        ),
        name="self_attention",
    )(place, q, kv, matrix)


def visit(kv_ref, q, values, acc, top):
    values[:, :HD] = kv_ref[:, HD:]
    values[:, HD:] = jnp.ones((values.shape[0], HD), jnp.bfloat16)
    for t in range(q.shape[0] // TILE):
        rows = slice(t * TILE, t * TILE + TILE)
        s = dot_t(q[rows, :], kv_ref[:, :HD])
        old = top[rows, :1]
        new = jnp.maximum(old, jnp.max(s, axis=1, keepdims=True))
        p = jnp.exp2(s - new).astype(jnp.bfloat16)
        acc[rows, :] = acc[rows, :] * jnp.exp2(old - new) + jnp.dot(
            p, values[...], preferred_element_type=jnp.float32
        )
        top[rows, :] = jnp.broadcast_to(new, (TILE, 128))


def sees(order_ref, s_ref, dh, dx):
    x, h = s_ref[4], s_ref[0]
    mine = order_ref[x * NH + (h ^ dh)]
    return order_ref[((x + dx) % NX) * NH + h] <= mine


def own_kernel(order_ref, s_ref, qa_ref, qb_ref, kv_ref, acc_ref, top_ref, q, values):
    dh = pl.program_id(0)
    q[...] = jnp.where(dh == 0, qa_ref[...], qb_ref[...])
    acc_ref[...] = jnp.zeros_like(acc_ref)
    top_ref[...] = jnp.full_like(top_ref, -NEG_LARGE)
    pl.when(sees(order_ref, s_ref, dh, 0))(
        functools.partial(visit, kv_ref, q, values, acc_ref.at[0], top_ref.at[0])
    )


def other_kernel(order_ref, s_ref, qa_ref, qb_ref, acc_in, top_in, k1, k2, k3, o_ref, *scratch):
    q, values, acc, top = scratch
    dh = pl.program_id(0)
    q[...] = jnp.where(dh == 0, qa_ref[...], qb_ref[...])
    acc[...] = acc_in[0]
    top[...] = top_in[0]
    for dx, ref in ((NX - 1, k1), (1, k2), (2, k3)):
        pl.when(sees(order_ref, s_ref, dh, dx))(
            functools.partial(visit, ref, q, values, acc, top)
        )
    y, core = s_ref[1], s_ref[3]
    for quarter in range(4):
        starts = [block_at(quarter // 2, quarter % 2, d) * BLK for d in range(NZ)]
        gather = lambda ref, cols: jnp.concatenate([ref[i : i + BLK, cols] for i in starts], axis=0)
        total = gather(acc, slice(HD, 2 * HD))
        some = total > 0.0
        safe = jnp.where(some, total, 1.0)
        at = quarter ^ (y * 2 + core)
        o_ref[at, :QUARTER, :] = (gather(acc, slice(0, HD)) / safe).astype(jnp.bfloat16)
        lse = jnp.where(some, gather(top, slice(0, 128)) + jnp.log2(safe), -NEG_LARGE)
        row = lse.T[0:1, :]
        row = jnp.concatenate([row[:, :128], row[:, 128:]], axis=0)
        hi = row.astype(jnp.bfloat16).astype(jnp.float32)
        rest = row - hi
        mid = rest.astype(jnp.bfloat16).astype(jnp.float32)
        pad = jnp.zeros((TAIL - 6, 128), jnp.float32)
        o_ref[at, QUARTER:, :] = jnp.concatenate([hi, mid, rest - mid, pad], axis=0).astype(
            jnp.bfloat16
        )


def whole(a):
    return pl.BlockSpec(a.shape, lambda i, *s: (0,) * a.ndim)


def attention_cost(units, rows):
    pairs = 2 * units * rows * rows
    return pl.CostEstimate(flops=6 * pairs * HD, bytes_accessed=4 * 2**20, transcendentals=pairs)


def own_attention(order, place, qa, qb, kv):
    rows = qa.shape[0]
    out = lambda cols: pl.BlockSpec((1, rows, cols), lambda i, *s: (i, 0, 0))
    return pl.pallas_call(
        own_kernel,
        grid_spec=pltpu.PrefetchScalarGridSpec(
            num_scalar_prefetch=2,
            grid=(NH,),
            in_specs=[whole(a) for a in (qa, qb, kv)],
            out_specs=[out(2 * HD), out(128)],
            scratch_shapes=[
                pltpu.VMEM((rows, HD), jnp.bfloat16),
                pltpu.VMEM((rows, 2 * HD), jnp.bfloat16),
            ],
        ),
        out_shape=[
            jax.ShapeDtypeStruct((NH, rows, 2 * HD), jnp.float32),
            jax.ShapeDtypeStruct((NH, rows, 128), jnp.float32),
        ],
        compiler_params=pltpu.CompilerParams(vmem_limit_bytes=20 * 2**20),
        cost_estimate=attention_cost(1, rows),
        name="own_attention",
    )(order, place, qa, qb, kv)


def other_attention(order, place, qa, qb, acc, top, blocks):
    rows = qa.shape[0]
    chunk = QUARTER + TAIL
    part = lambda a: pl.BlockSpec((1,) + a.shape[1:], lambda i, *s: (i, 0, 0))
    return pl.pallas_call(
        other_kernel,
        grid_spec=pltpu.PrefetchScalarGridSpec(
            num_scalar_prefetch=2,
            grid=(NH,),
            in_specs=[whole(qa), whole(qb), part(acc), part(top)] + [whole(b) for b in blocks],
            out_specs=pl.BlockSpec((4, chunk, HD), lambda i, o, s: (i ^ s[0], 0, 0)),
            scratch_shapes=[
                pltpu.VMEM((rows, HD), jnp.bfloat16),
                pltpu.VMEM((rows, 2 * HD), jnp.bfloat16),
                pltpu.VMEM((rows, 2 * HD), jnp.float32),
                pltpu.VMEM((rows, 128), jnp.float32),
            ],
        ),
        out_shape=jax.ShapeDtypeStruct((NH * 4, chunk, HD), jnp.bfloat16),
        compiler_params=pltpu.CompilerParams(vmem_limit_bytes=24 * 2**20),
        cost_estimate=attention_cost(3, rows),
        name="other_attention",
    )(order, place, qa, qb, acc, top, *blocks)


def join_kernel(s_ref, in_ref, w0_ref, w1_ref, w2_ref, w3_ref, o_ref, a_ref, w_ref):
    h, y, z, core = s_ref[0], s_ref[1], s_ref[2], s_ref[3]
    place = h * 4 + y * 2 + core

    @pl.when(pl.program_id(0) == 0)
    def _():
        for r in range(4):
            used = used_slots(y ^ (r // 2), z)
            parts = []
            for dh in range(NH):
                at = (dh * 4 + r) ^ place
                rows = in_ref[at, QUARTER:, :].astype(jnp.float32)
                parts.append((at, rows[0:2] + rows[2:4] + rows[4:6]))
            top = jnp.maximum(parts[0][1], parts[1][1])
            e = [jnp.exp2(lse - top) for _, lse in parts]
            norm = e[0] + e[1]
            for half in range(2):
                out = None
                for (at, _), weight in zip(parts, e):
                    w = jnp.where(used, weight / norm, 0.0)[half : half + 1, :]
                    col = jnp.broadcast_to(w, (128, 128)).T
                    term = in_ref[at, half * 128 : half * 128 + 128, :].astype(jnp.float32) * col
                    out = term if out is None else out + term
                out = out.astype(jnp.bfloat16)
                for j in range(4):
                    start = pl.multiple_of(((z + half * 4 + j) % NZ) * BLK, BLK)
                    a_ref[pl.ds(start, BLK), r * HD : r * HD + HD] = out[j * BLK : j * BLK + BLK]

    for r, ref in enumerate((w0_ref, w1_ref, w2_ref, w3_ref)):
        w_ref[r * HD : r * HD + HD, :] = ref[...]
    o_ref[...] = jnp.dot(a_ref[...], w_ref[...], preferred_element_type=jnp.float32).astype(
        jnp.bfloat16
    )


def join_heads(place, received, weights):
    width = weights[0].shape[1]
    step = width // 4
    return pl.pallas_call(
        join_kernel,
        grid_spec=pltpu.PrefetchScalarGridSpec(
            num_scalar_prefetch=1,
            grid=(4,),
            in_specs=[whole(received)] + [pl.BlockSpec((HD, step), lambda i, s: (0, i))] * 4,
            out_specs=pl.BlockSpec((QUARTER, step), lambda i, s: (0, i)),
            scratch_shapes=[
                pltpu.VMEM((QUARTER, 4 * HD), jnp.bfloat16),
                pltpu.VMEM((4 * HD, step), jnp.bfloat16),
            ],
        ),
        out_shape=jax.ShapeDtypeStruct((QUARTER, width), jnp.bfloat16),
        compiler_params=pltpu.CompilerParams(vmem_limit_bytes=16 * 2**20),
        name="join_heads",
    )(place, received, *weights)


def decode(latents, root_kernel):
    seq_count = latents.shape[0]
    row_patches = seq_count // FR
    me = lax.axis_index("seq")
    ringed = jnp.concatenate([latents[-1:], latents, latents[:1]], axis=0)
    position = (me - row_patches // 2 + seq_count) % seq_count
    patch_row = position % row_patches
    frame_index = position // row_patches
    row_ids = jnp.arange(P_SIZE + 2, dtype=jnp.int32)
    keep = jnp.where(
        row_ids == 0,
        patch_row > 0,
        jnp.where(row_ids == P_SIZE + 1, patch_row < row_patches - 1, True),
    )
    width_cols = BLK * P_SIZE
    windows = []
    for lag in range(3):
        start = (me - lag * row_patches + seq_count) % seq_count
        three = lax.dynamic_slice_in_dim(ringed, start, 3, axis=0)
        slab = (
            three.reshape(3, BLK, P_SIZE, P_SIZE, C)
            .transpose(0, 2, 1, 3, 4)
            .reshape(3 * P_SIZE, width_cols, C)
        )[P_SIZE - 1 : 2 * P_SIZE + 1]
        ok = keep & (frame_index >= lag)
        slab = jnp.where(ok[:, None, None], slab, jnp.zeros_like(slab))
        framed = jnp.pad(slab, ((0, 0), (1, 1), (0, 0)))
        for row_off in range(3):
            for col_off in range(3):
                windows.append(framed[row_off : row_off + P_SIZE, col_off : col_off + width_cols])
    stacked = jnp.concatenate(windows, axis=-1).reshape(P_SIZE * width_cols, 27 * C)
    decoded = jnp.dot(stacked, root_kernel, preferred_element_type=jnp.float32)
    return decoded.reshape(P_SIZE, width_cols, root_kernel.shape[1]).astype(jnp.bfloat16)[None]


def after(value, earlier):
    return lax.optimization_barrier((value, earlier))[0]


def per_device(
    hidden, levels, span_order, modulation, in_weight, out_weight, latent_weight, decoder_weight
):
    span_me = lax.axis_index("span")
    seq_me = lax.axis_index("seq")
    x, h = span_me // NH, span_me % NH
    y, z, core = seq_me // (NZ * NC), (seq_me // NC) % NZ, seq_me % NC
    place = jnp.stack([h, y, z, core, x])
    pv = latent_weight.shape[1]
    seq_count = NY * NZ * NC

    normed, gate_row = normalize(levels, hidden[0], modulation)
    w_own = in_weight[0]
    own_blocks, other_blocks = gather_class(normed)
    w_oth = move_core(w_own)
    mine_a, theirs_a = project(own_blocks, w_own, w_oth)
    mine_b, theirs_b = project(other_blocks, w_own, w_oth)
    triples = jnp.concatenate([mine_a, move_core(theirs_a), mine_b, move_core(theirs_b)], axis=0)
    q = triples[:, :HD]
    kv = triples[:, HD:]

    others = tuple(move_x(kv, d) for d in (1, NX - 1, 2))
    q_hi = move_hi(q)

    matrix = latent_matrix(after(out_weight[0], mine_b), gate_row, latent_weight)
    part = self_attention(place, q, kv, matrix)
    part = lax.all_to_all(part, "seq", 0, 0, tiled=True)

    out_w = after(out_weight[0], mine_b)
    w_core, w_far = move_core(out_w), move_y(out_w)
    weights = (out_w, w_core, w_far, move_core(w_far))

    acc, top = own_attention(span_order, place, q, q_hi, kv)
    acc = after(acc, part)
    chunks = other_attention(span_order, place, q, q_hi, acc, top, others)
    groups = [
        [
            span_at(i, hh) * seq_count + seq_at(yy, j, cc)
            for hh in range(NH)
            for yy in range(NY)
            for cc in range(NC)
        ]
        for i in range(NX)
        for j in range(NZ)
    ]
    received = lax.all_to_all(
        chunks, ("span", "seq"), 0, 0, tiled=True, axis_index_groups=groups
    )
    partial = join_heads(place, received, weights)
    z_groups = [[seq_at(yy, j, cc) for j in range(NZ)] for yy in range(NY) for cc in range(NC)]
    part = after(part, partial)
    summed = lax.psum_scatter(
        partial, "seq", scatter_dimension=0, tiled=True, axis_index_groups=z_groups
    ).astype(jnp.float32)
    block_out = (hidden[0].astype(jnp.float32) + gate_row * summed).astype(jnp.bfloat16)[None]

    own_latents = jnp.dot(hidden[0], latent_weight, preferred_element_type=jnp.float32)
    latents = (jnp.sum(part.astype(jnp.float32), axis=0) + own_latents).astype(jnp.bfloat16)
    group_ids = jnp.arange(span_order.shape[0], dtype=jnp.int32)
    root = jnp.sum(jnp.where(span_order == 0, group_ids, 0))
    spread = lax.all_to_all(
        jnp.broadcast_to(latents[None], (NX * NH, BLK, pv)), "span", 0, 0, tiled=True
    )
    latents = lax.dynamic_index_in_dim(spread, root, 0, keepdims=True)
    every = lax.all_to_all(
        jnp.broadcast_to(latents, (seq_count, BLK, pv)), "seq", 0, 0, tiled=True
    )
    decoded = decode(every, decoder_weight.reshape(27 * C, decoder_weight.shape[4]))
    return (block_out, decoded)


def solution(mesh):
    placed = (
        P("span", "seq", None),
        P("span"),
        P(),
        P(),
        P("seq", None, None),
        P("seq", None, None),
        P(),
        P(None, None, None, None, "span"),
    )
    return jax.shard_map(
        per_device,
        mesh=mesh,
        in_specs=placed,
        out_specs=(P("span", "seq", None), P("seq", None, None, "span")),
        check_vma=False,
    )
```

profile of v0, /device:TPU:10, one launch (start us, length us, event | category | flops | bytes accessed | tf_op | source)
XLA Modules:
  0.0 172.4 jit_solution(11018930821905394853)
XLA Ops:
  7.2 0.1 collective-permute-start.7
  7.9 2.0 %normalize.1 = (bf16[32,3072]{1,0:T(8,128)(2,1)}, f32[1,3072]{1,0:T(1,128)}) custom-call(s32[1]{0:T(128)S(6)} %copy.28.level_ref, bf16[32,3072]{1,0:T(8,128)(2,1)} %bitcast.48, f32[3,16,3072]{2,1,0:T(8,128)} %bitcast.49), custom_call_target="tpu_custom_call" | custom-call | tf_op jit(solution)/shard_map/normalize/pallas_call | solution.py:114
  10.0 1.9 %collective-permute-start.2 = (bf16[32,3072]{1,0:T(8,128)(2,1)}, bf16[32,3072]{1,0:T(8,128)(2,1)S(1)}, u32[]{:S(2)}, u32[]{:S(2)}) collective-permute-start(bf16[32,3072]{1,0:T(8,128)(2,1)} %get-tuple-element.14.refs_0_), channel_id=1, source_target_pairs={{0,2},{1,3},{2,4},{3,5},{4,6},{5,7},{6,8},{7,9},{8,10},{9,11},{10,... | collective-permute-start | bytes 589832 | tf_op jit(solution)/shard_map/ppermute | solution.py:48
  11.9 3.9 %collective-permute-start = (bf16[32,3072]{1,0:T(8,128)(2,1)}, bf16[32,3072]{1,0:T(8,128)(2,1)S(1)}, u32[]{:S(2)}, u32[]{:S(2)}) collective-permute-start(bf16[32,3072]{1,0:T(8,128)(2,1)} %get-tuple-element.14.refs_0_), channel_id=1, source_target_pairs={{0,14},{1,15},{2,0},{3,1},{4,2},{5,3},{6,4},{7,5},{8,6},{9,7},{10,... | collective-permute-start | bytes 589832 | tf_op jit(solution)/shard_map/ppermute | solution.py:48
  15.8 0.4 collective-permute-start.4
  16.3 5.3 %collective-permute-done.2.refs_4_ = bf16[32,3072]{1,0:T(8,128)(2,1)S(1)} collective-permute-done((bf16[32,3072]{1,0:T(8,128)(2,1)}, bf16[32,3072]{1,0:T(8,128)(2,1)S(1)}, u32[]{:S(2)}, u32[]{:S(2)}) %collective-permute-start.2) | collective-permute-done | bytes 196640 | tf_op jit(solution)/shard_map/ppermute | solution.py:48
  21.6 3.2 %collective-permute-start.1 = (bf16[32,3072]{1,0:T(8,128)(2,1)S(1)}, bf16[32,3072]{1,0:T(8,128)(2,1)S(1)}, u32[]{:S(2)}, u32[]{:S(2)}) collective-permute-start(bf16[32,3072]{1,0:T(8,128)(2,1)S(1)} %collective-permute-done.refs_1_), channel_id=1, source_target_pairs={{0,14},{1,15},{2,0},{3,1},{4,2},{5,3},{6,4},{7,5},{8,6},{9,7},{10,... | collective-permute-start | bytes 589832 | tf_op jit(solution)/shard_map/ppermute | solution.py:48
  24.8 0.4 collective-permute-start.5
  25.3 1.6 collective-permute-start.6
  26.9 2.7 %collective-permute-done.3.refs_3_ = bf16[32,3072]{1,0:T(8,128)(2,1)S(1)} collective-permute-done((bf16[32,3072]{1,0:T(8,128)(2,1)S(1)}, bf16[32,3072]{1,0:T(8,128)(2,1)S(1)}, u32[]{:S(2)}, u32[]{:S(2)}) %collective-permute-start.3) | collective-permute-done | bytes 196640 | tf_op jit(solution)/shard_map/ppermute | solution.py:48
  29.6 0.5 collective-permute-start.12
  30.0 2.7 %collective-permute-done.5.refs_6_ = bf16[32,3072]{1,0:T(8,128)(2,1)S(1)} collective-permute-done((bf16[32,3072]{1,0:T(8,128)(2,1)S(1)}, bf16[32,3072]{1,0:T(8,128)(2,1)S(1)}, u32[]{:S(2)}, u32[]{:S(2)}) %collective-permute-start.5) | collective-permute-done | bytes 196640 | tf_op jit(solution)/shard_map/ppermute | solution.py:52
  32.7 0.6 collective-permute-start.9
  33.2 3.7 %collective-permute-done.6.refs_7_ = bf16[32,3072]{1,0:T(8,128)(2,1)S(1)} collective-permute-done((bf16[32,3072]{1,0:T(8,128)(2,1)S(1)}, bf16[32,3072]{1,0:T(8,128)(2,1)S(1)}, u32[]{:S(2)}, u32[]{:S(2)}) %collective-permute-start.6) | collective-permute-done | bytes 196640 | tf_op jit(solution)/shard_map/ppermute | solution.py:52
  36.9 0.4 collective-permute-start.15
  37.4 3.8 %collective-permute-done.12.refs_3_ = bf16[32,3072]{1,0:T(8,128)(2,1)S(1)} collective-permute-done((bf16[32,3072]{1,0:T(8,128)(2,1)S(1)}, bf16[32,3072]{1,0:T(8,128)(2,1)S(1)}, u32[]{:S(2)}, u32[]{:S(2)}) %collective-permute-start.12) | collective-permute-done | bytes 196640 | tf_op jit(solution)/shard_map/ppermute | solution.py:52
  41.1 1.4 collective-permute-start.14
  42.5 3.2 %collective-permute-done.15.refs_7_ = bf16[32,3072]{1,0:T(8,128)(2,1)S(1)} collective-permute-done((bf16[32,3072]{1,0:T(8,128)(2,1)S(1)}, bf16[32,3072]{1,0:T(8,128)(2,1)S(1)}, u32[]{:S(2)}, u32[]{:S(2)}) %collective-permute-start.15) | collective-permute-done | bytes 196640 | tf_op jit(solution)/shard_map/ppermute | solution.py:52
  45.8 1.7 copy-done.1
  47.4 0.9 copy-done.5
  48.4 1.8 %project.2 = (bf16[256,384]{1,0:T(8,128)(2,1)S(1)}, bf16[256,384]{1,0:T(8,128)(2,1)S(1)}) custom-call(bf16[32,3072]{1,0:T(8,128)(2,1)S(1)} %copy-done.5, bf16[32,3072]{1,0:T(8,128)(2,1)S(1)} %collective-permute-done.refs_1_, bf16[32,3072]{1,0:T(8,128)(2,1)S(1)} %collective-permute-done.1.refs_2_, bf16[32,3072]{1,0:T(8,128)(2,1)S(1)} %collective-permute-done.3.refs_3_, ...), custom_call_target="tpu_custom_call" | custom-call | flops 1207959552 | bytes 6291456 | tf_op jit(solution)/shard_map/project/pallas_call | solution.py:170
  50.2 0.1 collective-permute-start.8
  50.3 2.3 %collective-permute-done.16.refs_6_ = bf16[32,3072]{1,0:T(8,128)(2,1)S(1)} collective-permute-done((bf16[32,3072]{1,0:T(8,128)(2,1)S(1)}, bf16[32,3072]{1,0:T(8,128)(2,1)S(1)}, u32[]{:S(2)}, u32[]{:S(2)}) %collective-permute-start.16) | collective-permute-done | bytes 196640 | tf_op jit(solution)/shard_map/ppermute | solution.py:48
  52.6 1.8 %project.3 = (bf16[256,384]{1,0:T(8,128)(2,1)S(1)}, bf16[256,384]{1,0:T(8,128)(2,1)S(1)}) custom-call(bf16[32,3072]{1,0:T(8,128)(2,1)S(1)} %collective-permute-done.9.refs_0_, bf16[32,3072]{1,0:T(8,128)(2,1)S(1)} %collective-permute-done.11.refs_1_, bf16[32,3072]{1,0:T(8,128)(2,1)S(1)} %collective-permute-done.10.refs_2_, ...), custom_call_target="tpu_custom_call" | custom-call | flops 1207959552 | bytes 6291456 | tf_op jit(solution)/shard_map/project/pallas_call | solution.py:170
  54.5 0.1 collective-permute-start.17
  54.6 0.1 collective-permute-start.23
  54.8 1.2 collective-permute-done.17
  56.1 1.6 collective-permute-start.19
  57.7 0.5 collective-permute-start.20
  58.2 2.1 %collective-permute-start.21 = (bf16[1024,256]{1,0:T(8,128)(2,1)S(1)}, bf16[1024,256]{1,0:T(8,128)(2,1)}, u32[]{:S(2)}, u32[]{:S(2)}) collective-permute-start(bf16[1024,256]{1,0:T(8,128)(2,1)S(1)} %slice.146.kv_ref), channel_id=1, source_target_pairs={{0,128},{32,160},{64,192},{96,224},{128,0},{160,32},{192,64},{224,... | collective-permute-start | bytes 1572872 | tf_op jit(solution)/shard_map/ppermute | solution.py:60
  60.3 0.1 stack.23.s_ref
  60.4 0.6 latent_matrix.1.m_ref
  61.0 1.0 slice.145.qa_ref.q_ref
  62.0 2.4 %collective-permute-start.18 = (bf16[1024,128]{1,0:T(8,128)(2,1)S(1)}, bf16[1024,128]{1,0:T(8,128)(2,1)S(1)}, u32[]{:S(2)}, u32[]{:S(2)}) collective-permute-start(bf16[1024,128]{1,0:T(8,128)(2,1)S(1)} %slice.145.qa_ref.q_ref), channel_id=1, source_target_pairs={{0,32},{32,0},{64,96},{96,64},{128,160},{160,128},{192,224},{224,1... | collective-permute-start | bytes 786440 | tf_op jit(solution)/shard_map/ppermute | solution.py:64
  64.4 5.1 %self_attention.1 = bf16[32,32,64]{2,1,0:T(8,128)(2,1)S(1)} custom-call(s32[5]{0:T(128)S(1)} %stack.23.s_ref, bf16[1024,128]{1,0:T(8,128)(2,1)S(1)} %slice.145.qa_ref.q_ref, bf16[1024,256]{1,0:T(8,128)(2,1)S(1)} %slice.146.kv_ref, bf16[256,64]{1,0:T(8,128)(2,1)S(1)} %latent_matrix.1.m_ref), custom_call_target="tpu_custom_call" | custom-call | flops 805306368 | bytes 1048576 | tf_op jit(solution)/shard_map/self_attention/pallas_call | solution.py:219
  69.5 0.8 reshape.53
  70.4 16.1 %all_to_all.20 = bf16[32,2,1024]{2,1,0:T(2,128)(2,1)S(1)} all-to-all(bf16[32,2,1024]{2,1,0:T(2,128)(2,1)} %reshape.53), channel_id=1, replica_groups=mesh['span'=8,'seq'=32] {'seq'}, dimensions={0} | all-to-all | bytes 262144 | tf_op jit(solution)/shard_map/all_to_all | solution.py:479
  86.5 0.9 reshape.54
  87.4 2.8 %own_attention.1 = (f32[2,1024,256]{2,1,0:T(8,128)S(1)}, f32[2,1024,128]{2,1,0:T(8,128)S(1)}) custom-call(s32[8]{0:T(128)S(1)} %copy-done.7, s32[5]{0:T(128)S(1)} %stack.23.s_ref, bf16[1024,128]{1,0:T(8,128)(2,1)S(1)} %slice.145.qa_ref.q_ref, bf16[1024,128]{1,0:T(8,128)(2,1)S(1)} %collective-permute-done.18.qb_ref, bf16[1024,256]{1,0:T(8,128)(2,1)S(1)} %slice.146.kv_ref), custom_call_target="tpu_custom_call" | custom-call | flops 1610612736 | bytes 4194304 | tf_op jit(solution)/shard_map/own_attention/pallas_call | solution.py:311
  90.2 0.6 collective-permute-start.24
  90.8 8.6 %other_attention.1 = bf16[8,272,128]{2,1,0:T(8,128)(2,1)} custom-call(s32[8]{0:T(128)S(1)} %copy-done.7, s32[5]{0:T(128)S(1)} %stack.23.s_ref, bf16[1024,128]{1,0:T(8,128)(2,1)S(1)} %slice.145.qa_ref.q_ref, bf16[1024,128]{1,0:T(8,128)(2,1)S(1)} %collective-permute-done.18.qb_ref, f32[2,1024,256]{2,1,0:T(8,128)S(1)} %get-tuple-element.21.acc_in, ...), custom_call_target="tpu_custom_call" | custom-call | flops 4831838208 | bytes 4194304 | tf_op jit(solution)/shard_map/other_attention/pallas_call | solution.py:337
  99.5 5.0 %all-to-all-start.1 = ((bf16[8,272,128]{2,1,0:T(8,128)(2,1)}), bf16[8,272,128]{2,1,0:T(8,128)(2,1)S(1)}, u32[]{:S(2)}, u32[]{:S(2)}) async-start(bf16[8,272,128]{2,1,0:T(8,128)(2,1)} %other_attention.1), calls=%async_computation.1 | async-start | bytes 1114112 | tf_op jit(solution)/shard_map/all_to_all | solution.py:498
  104.5 9.2 %all-to-all-done.1.in_ref = bf16[8,272,128]{2,1,0:T(8,128)(2,1)S(1)} async-done(((bf16[8,272,128]{2,1,0:T(8,128)(2,1)}), bf16[8,272,128]{2,1,0:T(8,128)(2,1)S(1)}, u32[]{:S(2)}, u32[]{:S(2)}) %all-to-all-start.1) | async-done | bytes 557088 | tf_op jit(solution)/shard_map/all_to_all | solution.py:498
  113.7 5.4 %join_heads.1 = bf16[256,3072]{1,0:T(8,128)(2,1)} custom-call(s32[5]{0:T(128)S(1)} %stack.23.s_ref, bf16[8,272,128]{2,1,0:T(8,128)(2,1)S(1)} %all-to-all-done.1.in_ref, bf16[128,3072]{1,0:T(8,128)(2,1)S(1)} %bitcast.45, bf16[128,3072]{1,0:T(8,128)(2,1)} %collective-permute-done.22.w1_ref, bf16[128,3072]{1,0:T(8,128)(2,1)S(1)} %collective-permute-done.23.w2_ref, ...), custom_call_target="tpu_custom_call" | custom-call | tf_op jit(solution)/shard_map/join_heads/pallas_call | solution.py:396
  119.2 0.2 fusion.1
  119.5 0.7 reshape.55
  120.2 12.6 %all-to-all-start.2 = ((bf16[8,2,1024]{2,1,0:T(2,128)(2,1)}), bf16[8,2,1024]{2,1,0:T(2,128)(2,1)S(1)}, u32[]{:S(2)}, u32[]{:S(2)}) async-start(bf16[8,2,1024]{2,1,0:T(2,128)(2,1)} %reshape.55), calls=%async_computation.3 | async-start | bytes 65536 | tf_op jit(solution)/shard_map/all_to_all | solution.py:513
  132.8 0.6 fusion.3
  135.4 3.7 %all-to-all-done.2 = bf16[8,2,1024]{2,1,0:T(2,128)(2,1)S(1)} async-done(((bf16[8,2,1024]{2,1,0:T(2,128)(2,1)}), bf16[8,2,1024]{2,1,0:T(2,128)(2,1)S(1)}, u32[]{:S(2)}, u32[]{:S(2)}) %all-to-all-start.2) | async-done | bytes 32800 | tf_op jit(solution)/shard_map/all_to_all | solution.py:513
  139.1 0.1 reshape.56
  139.2 0.8 reshape.57
  140.1 4.2 %all-to-all-start.3 = ((bf16[32,2,1024]{2,1,0:T(2,128)(2,1)}), bf16[32,2,1024]{2,1,0:T(2,128)(2,1)S(1)}, u32[]{:S(2)}, u32[]{:S(2)}) async-start(bf16[32,2,1024]{2,1,0:T(2,128)(2,1)} %reshape.57), calls=%async_computation.4 | async-start | bytes 262144 | tf_op jit(solution)/shard_map/all_to_all | solution.py:517
  144.4 9.6 %all-to-all-done.3 = bf16[32,2,1024]{2,1,0:T(2,128)(2,1)S(1)} async-done(((bf16[32,2,1024]{2,1,0:T(2,128)(2,1)}), bf16[32,2,1024]{2,1,0:T(2,128)(2,1)S(1)}, u32[]{:S(2)}, u32[]{:S(2)}) %all-to-all-start.3) | async-done | bytes 131104 | tf_op jit(solution)/shard_map/all_to_all | solution.py:517
  154.0 0.2 reshape.58
  154.2 0.3 copy.16
  154.5 0.1 pad_maximum_fusion
  154.7 0.1 copy.21
  154.8 0.1 copy.20
  154.9 0.1 copy.19
  155.0 0.1 slice_select_fusion
  155.4 0.3 concatenate.11
  155.8 0.8 fusion
  156.6 7.3 %reduce-scatter.2.cloned.1.call-done = bf16[32,3072]{1,0:T(8,128)(2,1)} async-done(((bf16[256,3072]{1,0:T(8,128)(2,1)}), bf16[32,3072]{1,0:T(8,128)(2,1)}) %reduce-scatter.2.cloned.1.call-update) | async-done | bytes 196624 | tf_op jit(solution)/shard_map/reduce_scatter | solution.py:504
  163.9 1.7 fusion.2
  (63 shorter events, 0.8 us)
Async XLA Ops:
  7.2 148.6 %copy-start = (bf16[3,3,3,16,64]{4,3,2,1,0:T(8,128)(2,1)S(1)}, bf16[3,3,3,16,64]{4,3,2,1,0:T(8,128)(2,1)}, u32[]{:S(2)}) copy-start(bf16[3,3,3,16,64]{4,3,2,1,0:T(8,128)(2,1)} %param.15) | copy-start | bytes 165892
  7.2 38.6 %collective-permute-start.7 = (bf16[3072,384]{1,0:T(8,128)(2,1)}, bf16[3072,384]{1,0:T(8,128)(2,1)S(1)}, u32[]{:S(2)}, u32[]{:S(2)}) collective-permute-start(bf16[3072,384]{1,0:T(8,128)(2,1)} %bitcast.39), channel_id=1, source_target_pairs={{0,1},{1,0},{2,3},{3,2},{4,5},{5,4},{6,7},{7,6},{8,9},{9,8},{10,11... | collective-permute-start | bytes 7077896 | tf_op jit(solution)/shard_map/ppermute | solution.py:56
  10.0 11.6 %collective-permute-start.2 = (bf16[32,3072]{1,0:T(8,128)(2,1)}, bf16[32,3072]{1,0:T(8,128)(2,1)S(1)}, u32[]{:S(2)}, u32[]{:S(2)}) collective-permute-start(bf16[32,3072]{1,0:T(8,128)(2,1)} %get-tuple-element.14.refs_0_), channel_id=1, source_target_pairs={{0,2},{1,3},{2,4},{3,5},{4,6},{5,7},{6,8},{7,9},{8,10},{9,11},{10,... | collective-permute-start | bytes 589832 | tf_op jit(solution)/shard_map/ppermute | solution.py:48
  11.9 9.7 %collective-permute-start = (bf16[32,3072]{1,0:T(8,128)(2,1)}, bf16[32,3072]{1,0:T(8,128)(2,1)S(1)}, u32[]{:S(2)}, u32[]{:S(2)}) collective-permute-start(bf16[32,3072]{1,0:T(8,128)(2,1)} %get-tuple-element.14.refs_0_), channel_id=1, source_target_pairs={{0,14},{1,15},{2,0},{3,1},{4,2},{5,3},{6,4},{7,5},{8,6},{9,7},{10,... | collective-permute-start | bytes 589832 | tf_op jit(solution)/shard_map/ppermute | solution.py:48
  15.8 9.5 %collective-permute-start.4 = (bf16[32,3072]{1,0:T(8,128)(2,1)}, bf16[32,3072]{1,0:T(8,128)(2,1)S(1)}, u32[]{:S(2)}, u32[]{:S(2)}) collective-permute-start(bf16[32,3072]{1,0:T(8,128)(2,1)} %get-tuple-element.14.refs_0_), channel_id=1, source_target_pairs={{0,16},{1,17},{2,18},{3,19},{4,20},{5,21},{6,22},{7,23},{8,24},{9,... | collective-permute-start | bytes 589832 | tf_op jit(solution)/shard_map/ppermute | solution.py:52
  21.6 7.9 %collective-permute-start.3 = (bf16[32,3072]{1,0:T(8,128)(2,1)S(1)}, bf16[32,3072]{1,0:T(8,128)(2,1)S(1)}, u32[]{:S(2)}, u32[]{:S(2)}) collective-permute-start(bf16[32,3072]{1,0:T(8,128)(2,1)S(1)} %collective-permute-done.2.refs_4_), channel_id=1, source_target_pairs={{0,2},{1,3},{2,4},{3,5},{4,6},{5,7},{6,8},{7,9},{8,10},{9,11},{10,... | collective-permute-start | bytes 589832 | tf_op jit(solution)/shard_map/ppermute | solution.py:48
  21.6 7.9 %collective-permute-start.1 = (bf16[32,3072]{1,0:T(8,128)(2,1)S(1)}, bf16[32,3072]{1,0:T(8,128)(2,1)S(1)}, u32[]{:S(2)}, u32[]{:S(2)}) collective-permute-start(bf16[32,3072]{1,0:T(8,128)(2,1)S(1)} %collective-permute-done.refs_1_), channel_id=1, source_target_pairs={{0,14},{1,15},{2,0},{3,1},{4,2},{5,3},{6,4},{7,5},{8,6},{9,7},{10,... | collective-permute-start | bytes 589832 | tf_op jit(solution)/shard_map/ppermute | solution.py:48
  24.8 7.8 %collective-permute-start.5 = (bf16[32,3072]{1,0:T(8,128)(2,1)S(1)}, bf16[32,3072]{1,0:T(8,128)(2,1)S(1)}, u32[]{:S(2)}, u32[]{:S(2)}) collective-permute-start(bf16[32,3072]{1,0:T(8,128)(2,1)S(1)} %collective-permute-done.refs_1_), channel_id=1, source_target_pairs={{0,16},{1,17},{2,18},{3,19},{4,20},{5,21},{6,22},{7,23},{8,24},{9,... | collective-permute-start | bytes 589832 | tf_op jit(solution)/shard_map/ppermute | solution.py:52
  25.3 11.6 %collective-permute-start.6 = (bf16[32,3072]{1,0:T(8,128)(2,1)S(1)}, bf16[32,3072]{1,0:T(8,128)(2,1)S(1)}, u32[]{:S(2)}, u32[]{:S(2)}) collective-permute-start(bf16[32,3072]{1,0:T(8,128)(2,1)S(1)} %collective-permute-done.2.refs_4_), channel_id=1, source_target_pairs={{0,16},{1,17},{2,18},{3,19},{4,20},{5,21},{6,22},{7,23},{8,24},{9,... | collective-permute-start | bytes 589832 | tf_op jit(solution)/shard_map/ppermute | solution.py:52
  29.5 7.8 %collective-permute-start.10 = (bf16[32,3072]{1,0:T(8,128)(2,1)S(1)}, bf16[32,3072]{1,0:T(8,128)(2,1)S(1)}, u32[]{:S(2)}, u32[]{:S(2)}) collective-permute-start(bf16[32,3072]{1,0:T(8,128)(2,1)S(1)} %collective-permute-done.3.refs_3_), channel_id=1, source_target_pairs={{0,2},{1,3},{2,4},{3,5},{4,6},{5,7},{6,8},{7,9},{8,10},{9,11},{10,... | collective-permute-start | bytes 589832 | tf_op jit(solution)/shard_map/ppermute | solution.py:48
  29.6 11.6 %collective-permute-start.12 = (bf16[32,3072]{1,0:T(8,128)(2,1)S(1)}, bf16[32,3072]{1,0:T(8,128)(2,1)S(1)}, u32[]{:S(2)}, u32[]{:S(2)}) collective-permute-start(bf16[32,3072]{1,0:T(8,128)(2,1)S(1)} %collective-permute-done.1.refs_2_), channel_id=1, source_target_pairs={{0,16},{1,17},{2,18},{3,19},{4,20},{5,21},{6,22},{7,23},{8,24},{9,... | collective-permute-start | bytes 589832 | tf_op jit(solution)/shard_map/ppermute | solution.py:52
  32.7 8.4 %collective-permute-start.9 = (bf16[32,3072]{1,0:T(8,128)(2,1)S(1)}, bf16[32,3072]{1,0:T(8,128)(2,1)S(1)}, u32[]{:S(2)}, u32[]{:S(2)}) collective-permute-start(bf16[32,3072]{1,0:T(8,128)(2,1)S(1)} %collective-permute-done.1.refs_2_), channel_id=1, source_target_pairs={{0,14},{1,15},{2,0},{3,1},{4,2},{5,3},{6,4},{7,5},{8,6},{9,7},{10,... | collective-permute-start | bytes 589832 | tf_op jit(solution)/shard_map/ppermute | solution.py:48
  36.9 8.9 %collective-permute-start.15 = (bf16[32,3072]{1,0:T(8,128)(2,1)S(1)}, bf16[32,3072]{1,0:T(8,128)(2,1)S(1)}, u32[]{:S(2)}, u32[]{:S(2)}) collective-permute-start(bf16[32,3072]{1,0:T(8,128)(2,1)S(1)} %collective-permute-done.3.refs_3_), channel_id=1, source_target_pairs={{0,16},{1,17},{2,18},{3,19},{4,20},{5,21},{6,22},{7,23},{8,24},{9,... | collective-permute-start | bytes 589832 | tf_op jit(solution)/shard_map/ppermute | solution.py:52
  37.4 12.9 %collective-permute-start.11 = (bf16[32,3072]{1,0:T(8,128)(2,1)S(1)}, bf16[32,3072]{1,0:T(8,128)(2,1)S(1)}, u32[]{:S(2)}, u32[]{:S(2)}) collective-permute-start(bf16[32,3072]{1,0:T(8,128)(2,1)S(1)} %collective-permute-done.10.refs_2_), channel_id=1, source_target_pairs={{0,2},{1,3},{2,4},{3,5},{4,6},{5,7},{6,8},{7,9},{8,10},{9,11},{10,... | collective-permute-start | bytes 589832 | tf_op jit(solution)/shard_map/ppermute | solution.py:48
  41.1 9.2 %collective-permute-start.13 = (bf16[32,3072]{1,0:T(8,128)(2,1)S(1)}, bf16[32,3072]{1,0:T(8,128)(2,1)S(1)}, u32[]{:S(2)}, u32[]{:S(2)}) collective-permute-start(bf16[32,3072]{1,0:T(8,128)(2,1)S(1)} %collective-permute-done.12.refs_3_), channel_id=1, source_target_pairs={{0,14},{1,15},{2,0},{3,1},{4,2},{5,3},{6,4},{7,5},{8,6},{9,7},{10,... | collective-permute-start | bytes 589832 | tf_op jit(solution)/shard_map/ppermute | solution.py:48
  41.1 9.2 %collective-permute-start.14 = (bf16[32,3072]{1,0:T(8,128)(2,1)S(1)}, bf16[32,3072]{1,0:T(8,128)(2,1)S(1)}, u32[]{:S(2)}, u32[]{:S(2)}) collective-permute-start(bf16[32,3072]{1,0:T(8,128)(2,1)S(1)} %collective-permute-done.9.refs_0_), channel_id=1, source_target_pairs={{0,30},{1,31},{2,16},{3,17},{4,18},{5,19},{6,20},{7,21},{8,22},{9,... | collective-permute-start | bytes 589832 | tf_op jit(solution)/shard_map/ppermute | solution.py:92
  45.8 6.9 %collective-permute-start.16 = (bf16[32,3072]{1,0:T(8,128)(2,1)S(1)}, bf16[32,3072]{1,0:T(8,128)(2,1)S(1)}, u32[]{:S(2)}, u32[]{:S(2)}) collective-permute-start(bf16[32,3072]{1,0:T(8,128)(2,1)S(1)} %collective-permute-done.15.refs_7_), channel_id=1, source_target_pairs={{0,2},{1,3},{2,4},{3,5},{4,6},{5,7},{6,8},{7,9},{8,10},{9,11},{10,... | collective-permute-start | bytes 589832 | tf_op jit(solution)/shard_map/ppermute | solution.py:48
  45.8 1.7 copy-start.1
  47.4 0.9 copy-start.5
  48.4 4.3 %copy-start.2 = (bf16[1,3072,384]{2,1,0:T(8,128)(2,1)S(1)}, bf16[1,3072,384]{2,1,0:T(8,128)(2,1)}, u32[]{:S(2)}) copy-start(bf16[1,3072,384]{2,1,0:T(8,128)(2,1)} %param.12) | copy-start | bytes 7077892
  50.2 4.4 %copy-start.3 = (bf16[1,128,3072]{2,1,0:T(8,128)(2,1)S(1)}, bf16[1,128,3072]{2,1,0:T(8,128)(2,1)}, u32[]{:S(2)}) copy-start(bf16[1,128,3072]{2,1,0:T(8,128)(2,1)} %param.13) | copy-start | bytes 2359300
  50.2 4.5 %collective-permute-start.8 = (bf16[256,384]{1,0:T(8,128)(2,1)S(1)}, bf16[256,384]{1,0:T(8,128)(2,1)S(1)}, u32[]{:S(2)}, u32[]{:S(2)}) collective-permute-start(bf16[256,384]{1,0:T(8,128)(2,1)S(1)} %get-tuple-element.16), channel_id=1, source_target_pairs={{0,1},{1,0},{2,3},{3,2},{4,5},{5,4},{6,7},{7,6},{8,9},{9,8},{10,11... | collective-permute-start | bytes 589832 | tf_op jit(solution)/shard_map/ppermute | solution.py:56
  54.5 6.0 %copy-start.4 = (bf16[3072,64]{0,1:T(8,128)(2,1)S(1)}, bf16[3072,64]{0,1:T(8,128)(2,1)}, u32[]{:S(2)}) copy-start(bf16[3072,64]{0,1:T(8,128)(2,1)} %param.14) | copy-start | bytes 1179652
  54.5 6.0 %copy-start.6 = (f32[1,3072]{1,0:T(1,128)S(1)}, f32[1,3072]{1,0:T(1,128)}, u32[]{:S(2)}) copy-start(f32[1,3072]{1,0:T(1,128)} %get-tuple-element.13.gate_ref) | copy-start | bytes 36868
  54.5 1.5 collective-permute-start.17
  54.6 35.6 %collective-permute-start.23 = (bf16[128,3072]{1,0:T(8,128)(2,1)S(1)}, bf16[128,3072]{1,0:T(8,128)(2,1)S(1)}, u32[]{:S(2)}, u32[]{:S(2)}) collective-permute-start(bf16[128,3072]{1,0:T(8,128)(2,1)S(1)} %bitcast.42), channel_id=1, source_target_pairs={{0,16},{1,17},{2,18},{3,19},{4,20},{5,21},{6,22},{7,23},{8,24},{9,... | collective-permute-start | bytes 2359304 | tf_op jit(solution)/shard_map/ppermute | solution.py:52
  56.0 1.6 copy-start.9
  56.1 34.7 %collective-permute-start.19 = (bf16[1024,256]{1,0:T(8,128)(2,1)S(1)}, bf16[1024,256]{1,0:T(8,128)(2,1)}, u32[]{:S(2)}, u32[]{:S(2)}) collective-permute-start(bf16[1024,256]{1,0:T(8,128)(2,1)S(1)} %slice.146.kv_ref), channel_id=1, source_target_pairs={{0,64},{32,96},{64,128},{96,160},{128,192},{160,224},{192,0},{224,... | collective-permute-start | bytes 1572872 | tf_op jit(solution)/shard_map/ppermute | solution.py:60
  57.7 33.1 %collective-permute-start.20 = (bf16[1024,256]{1,0:T(8,128)(2,1)S(1)}, bf16[1024,256]{1,0:T(8,128)(2,1)}, u32[]{:S(2)}, u32[]{:S(2)}) collective-permute-start(bf16[1024,256]{1,0:T(8,128)(2,1)S(1)} %slice.146.kv_ref), channel_id=1, source_target_pairs={{0,192},{32,224},{64,0},{96,32},{128,64},{160,96},{192,128},{224,1... | collective-permute-start | bytes 1572872 | tf_op jit(solution)/shard_map/ppermute | solution.py:60
  58.2 32.6 %collective-permute-start.21 = (bf16[1024,256]{1,0:T(8,128)(2,1)S(1)}, bf16[1024,256]{1,0:T(8,128)(2,1)}, u32[]{:S(2)}, u32[]{:S(2)}) collective-permute-start(bf16[1024,256]{1,0:T(8,128)(2,1)S(1)} %slice.146.kv_ref), channel_id=1, source_target_pairs={{0,128},{32,160},{64,192},{96,224},{128,0},{160,32},{192,64},{224,... | collective-permute-start | bytes 1572872 | tf_op jit(solution)/shard_map/ppermute | solution.py:60
  61.0 26.4 %copy-start.7 = (s32[8]{0:T(128)S(1)}, s32[8]{0:T(128)}, u32[]{:S(2)}) copy-start(s32[8]{0:T(128)} %order_ref.3) | copy-start | bytes 100
  62.0 25.4 %collective-permute-start.18 = (bf16[1024,128]{1,0:T(8,128)(2,1)S(1)}, bf16[1024,128]{1,0:T(8,128)(2,1)S(1)}, u32[]{:S(2)}, u32[]{:S(2)}) collective-permute-start(bf16[1024,128]{1,0:T(8,128)(2,1)S(1)} %slice.145.qa_ref.q_ref), channel_id=1, source_target_pairs={{0,32},{32,0},{64,96},{96,64},{128,160},{160,128},{192,224},{224,1... | collective-permute-start | bytes 786440 | tf_op jit(solution)/shard_map/ppermute | solution.py:64
  87.4 17.1 %collective-permute-start.22 = (bf16[128,3072]{1,0:T(8,128)(2,1)S(1)}, bf16[128,3072]{1,0:T(8,128)(2,1)}, u32[]{:S(2)}, u32[]{:S(2)}) collective-permute-start(bf16[128,3072]{1,0:T(8,128)(2,1)S(1)} %bitcast.44), channel_id=1, source_target_pairs={{0,1},{1,0},{2,3},{3,2},{4,5},{5,4},{6,7},{7,6},{8,9},{9,8},{10,11... | collective-permute-start | bytes 2359304 | tf_op jit(solution)/shard_map/ppermute | solution.py:56
  90.2 23.5 %collective-permute-start.24 = (bf16[128,3072]{1,0:T(8,128)(2,1)S(1)}, bf16[128,3072]{1,0:T(8,128)(2,1)}, u32[]{:S(2)}, u32[]{:S(2)}) collective-permute-start(bf16[128,3072]{1,0:T(8,128)(2,1)S(1)} %collective-permute-done.23.w2_ref), channel_id=1, source_target_pairs={{0,1},{1,0},{2,3},{3,2},{4,5},{5,4},{6,7},{7,6},{8,9},{9,8},{10,11... | collective-permute-start | bytes 2359304 | tf_op jit(solution)/shard_map/ppermute | solution.py:56
  99.5 14.3 %all-to-all-start.1 = ((bf16[8,272,128]{2,1,0:T(8,128)(2,1)}), bf16[8,272,128]{2,1,0:T(8,128)(2,1)S(1)}, u32[]{:S(2)}, u32[]{:S(2)}) async-start(bf16[8,272,128]{2,1,0:T(8,128)(2,1)} %other_attention.1), calls=%async_computation.1 | async-start | bytes 1114112 | tf_op jit(solution)/shard_map/all_to_all | solution.py:498
  104.4 14.7 %copy-start.10 = (bf16[32,32,64]{2,1,0:T(8,128)(2,1)S(1)}, bf16[32,32,64]{2,1,0:T(8,128)(2,1)}, u32[]{:S(2)}) copy-start(bf16[32,32,64]{2,1,0:T(8,128)(2,1)} %reshape.54) | copy-start | bytes 393220
  104.4 14.7 %copy-start.8 = (bf16[1,32,3072]{2,1,0:T(8,128)(2,1)S(1)}, bf16[1,32,3072]{2,1,0:T(8,128)(2,1)}, u32[]{:S(2)}) copy-start(bf16[1,32,3072]{2,1,0:T(8,128)(2,1)} %param.8) | copy-start | bytes 589828
  104.4 59.4 %reduce-scatter.2.cloned.1.call-start = ((), (), s32[]{:S(2)}) async-start(), calls=%async_computation.5 | async-start | bytes 1769472 | tf_op jit(solution)/shard_map/reduce_scatter | solution.py:504
  120.2 18.9 %all-to-all-start.2 = ((bf16[8,2,1024]{2,1,0:T(2,128)(2,1)}), bf16[8,2,1024]{2,1,0:T(2,128)(2,1)S(1)}, u32[]{:S(2)}, u32[]{:S(2)}) async-start(bf16[8,2,1024]{2,1,0:T(2,128)(2,1)} %reshape.55), calls=%async_computation.3 | async-start | bytes 65536 | tf_op jit(solution)/shard_map/all_to_all | solution.py:513
  140.1 13.9 %all-to-all-start.3 = ((bf16[32,2,1024]{2,1,0:T(2,128)(2,1)}), bf16[32,2,1024]{2,1,0:T(2,128)(2,1)S(1)}, u32[]{:S(2)}, u32[]{:S(2)}) async-start(bf16[32,2,1024]{2,1,0:T(2,128)(2,1)} %reshape.57), calls=%async_computation.4 | async-start | bytes 262144 | tf_op jit(solution)/shard_map/all_to_all | solution.py:517
Sparse Core Ops, SparseCore 0:
  119.2 44.5 reduce-scatter.1
where the time goes:
time: 172 us
  waiting for transfers between devices  54.6 us (32%)
  starting transfers between devices  43.9 us (26%)
  Pallas kernels  28.2 us (16%)
  between operations  17.1 us (10%)
  blocking collectives  16.1 us (9%)
  local copies, waits for them, and re-layouts  8.71 us (5%)
  other arithmetic  2.74 us (2%)
    all_to_all x1, blocking collectives, per_device(): part = lax.all_to_all(part, 'seq', 0, 0, tiled=True)  16.1 us
    ppermute x6, waiting for transfers between devices, move_y(): return lax.ppermute(a, 'seq', seq_route(dy=1))  13.3 us
    all_to_all x1, starting transfers between devices, per_device(): lax.all_to_all(jnp.broadcast_to(latents[None], (NX * NH, BLK, pv)), 'span...  12.6 us
    ppermute x9, waiting for transfers between devices, move_z(): return lax.ppermute(a, 'seq', seq_route(dz=d))  10.3 us
    ppermute x9, starting transfers between devices, move_z(): return lax.ppermute(a, 'seq', seq_route(dz=d))  9.66 us
    all_to_all x1, waiting for transfers between devices, per_device(): lax.all_to_all(jnp.broadcast_to(latents, (seq_count, BLK, pv)), 'seq', 0,...  9.56 us
    all_to_all x1, waiting for transfers between devices, per_device(): lax.all_to_all(chunks, ('span', 'seq'), 0, 0, tiled=True, axis_index_grou...  9.21 us
    pallas_call x1, Pallas kernels, other_attention(): pl.pallas_call(other_kernel, grid_spec=pltpu.PrefetchScalarGridSpec(num_s...  8.63 us
  transfers between devices with their start and end apart: 29, of which 12 were waited for; matrix products, arithmetic and copies ran while one was open for 5% of the time, Pallas kernels for 13%

commit v1 on v0

--- a/solution.py
+++ b/solution.py
@@ -194,15 +194,18 @@
     return (y * NZ + z) * NC < HEADS
 
 
-def self_kernel(s_ref, q_ref, kv_ref, m_ref, o_ref, values):
+def self_kernel(s_ref, q_ref, kv_ref, m_ref, o_ref, acc_ref, top_ref, values):
     y, z, core = s_ref[1], s_ref[2], s_ref[3]
     used = used_slots(y, z)
     values[:, :HD] = kv_ref[:, HD:]
     values[:, HD:] = jnp.ones((values.shape[0], HD), jnp.bfloat16)
     for t in range(q_ref.shape[0] // TILE):
         s = dot_t(q_ref[t * TILE : t * TILE + TILE, :], kv_ref[:, :HD])
-        p = jnp.exp2(s - jnp.max(s, axis=1, keepdims=True)).astype(jnp.bfloat16)
+        top = jnp.max(s, axis=1, keepdims=True)
+        p = jnp.exp2(s - top).astype(jnp.bfloat16)
         acc = jnp.dot(p, values[...], preferred_element_type=jnp.float32)
+        acc_ref[t * TILE : t * TILE + TILE, :] = acc
+        top_ref[t * TILE : t * TILE + TILE, :] = jnp.broadcast_to(top, (TILE, 128))
         att = (acc[:, :HD] / acc[:, HD:]).astype(jnp.bfloat16)
         att = jnp.concatenate([att, att], axis=1)
         part = jnp.dot(att, m_ref[...], preferred_element_type=jnp.float32)
@@ -210,7 +213,10 @@
         for j in range(TILE // BLK):
             y_apart, core_apart, d = block_of(t * (TILE // BLK) + j)
             at = ((y ^ y_apart) * NZ + (z + d) % NZ) * NC + (core ^ core_apart)
-            o_ref[at] = part[j * BLK : j * BLK + BLK]
+            low, high = j * BLK, j * BLK + BLK // 2
+            o_ref[at] = jnp.concatenate(
+                [part[low:high, :], part[high : high + BLK // 2, :]], axis=1
+            )
 
 
 def self_attention(place, q, kv, matrix):
@@ -222,10 +228,18 @@
             num_scalar_prefetch=1,
             grid=(1,),
             in_specs=[pl.BlockSpec(a.shape, lambda i, s: (0, 0)) for a in (q, kv, matrix)],
-            out_specs=pl.BlockSpec((rows // BLK, BLK, pv), lambda i, s: (0, 0, 0)),
+            out_specs=[
+                pl.BlockSpec((rows // BLK, BLK // 2, 2 * pv), lambda i, s: (0, 0, 0)),
+                pl.BlockSpec((rows, 2 * HD), lambda i, s: (0, 0)),
+                pl.BlockSpec((rows, 128), lambda i, s: (0, 0)),
+            ],
             scratch_shapes=[pltpu.VMEM((rows, 2 * HD), jnp.bfloat16)],
         ),
-        out_shape=jax.ShapeDtypeStruct((rows // BLK, BLK, pv), jnp.bfloat16),
+        out_shape=[
+            jax.ShapeDtypeStruct((rows // BLK, BLK // 2, 2 * pv), jnp.bfloat16),
+            jax.ShapeDtypeStruct((rows, 2 * HD), jnp.float32),
+            jax.ShapeDtypeStruct((rows, 128), jnp.float32),
+        ],
         compiler_params=pltpu.CompilerParams(vmem_limit_bytes=16 * 2**20),
         cost_estimate=pl.CostEstimate(
             flops=6 * rows * rows * HD, bytes_accessed=2**20, transcendentals=rows * rows
@@ -255,22 +269,24 @@
     return order_ref[((x + dx) % NX) * NH + h] <= mine
 
 
-def own_kernel(order_ref, s_ref, qa_ref, qb_ref, kv_ref, acc_ref, top_ref, q, values):
-    dh = pl.program_id(0)
-    q[...] = jnp.where(dh == 0, qa_ref[...], qb_ref[...])
-    acc_ref[...] = jnp.zeros_like(acc_ref)
-    top_ref[...] = jnp.full_like(top_ref, -NEG_LARGE)
-    pl.when(sees(order_ref, s_ref, dh, 0))(
-        functools.partial(visit, kv_ref, q, values, acc_ref.at[0], top_ref.at[0])
-    )
-
-
-def other_kernel(order_ref, s_ref, qa_ref, qb_ref, acc_in, top_in, k1, k2, k3, o_ref, *scratch):
+def other_kernel(order_ref, s_ref, qa_ref, qb_ref, acc_in, top_in, k0, k1, k2, k3, o_ref, *scratch):
     q, values, acc, top = scratch
     dh = pl.program_id(0)
     q[...] = jnp.where(dh == 0, qa_ref[...], qb_ref[...])
-    acc[...] = acc_in[0]
-    top[...] = top_in[0]
+
+    @pl.when(dh == 0)
+    def _():
+        acc[...] = acc_in[...]
+        top[...] = top_in[...]
+
+    @pl.when(dh == 1)
+    def _():
+        acc[...] = jnp.zeros_like(acc)
+        top[...] = jnp.full_like(top, -NEG_LARGE)
+
+    pl.when((dh == 1) & sees(order_ref, s_ref, dh, 0))(
+        functools.partial(visit, k0, q, values, acc, top)
+    )
     for dx, ref in ((NX - 1, k1), (1, k2), (2, k3)):
         pl.when(sees(order_ref, s_ref, dh, dx))(
             functools.partial(visit, ref, q, values, acc, top)
@@ -305,41 +321,15 @@
     return pl.CostEstimate(flops=6 * pairs * HD, bytes_accessed=4 * 2**20, transcendentals=pairs)
 
 
-def own_attention(order, place, qa, qb, kv):
-    rows = qa.shape[0]
-    out = lambda cols: pl.BlockSpec((1, rows, cols), lambda i, *s: (i, 0, 0))
-    return pl.pallas_call(
-        own_kernel,
-        grid_spec=pltpu.PrefetchScalarGridSpec(
-            num_scalar_prefetch=2,
-            grid=(NH,),
-            in_specs=[whole(a) for a in (qa, qb, kv)],
-            out_specs=[out(2 * HD), out(128)],
-            scratch_shapes=[
-                pltpu.VMEM((rows, HD), jnp.bfloat16),
-                pltpu.VMEM((rows, 2 * HD), jnp.bfloat16),
-            ],
-        ),
-        out_shape=[
-            jax.ShapeDtypeStruct((NH, rows, 2 * HD), jnp.float32),
-            jax.ShapeDtypeStruct((NH, rows, 128), jnp.float32),
-        ],
-        compiler_params=pltpu.CompilerParams(vmem_limit_bytes=20 * 2**20),
-        cost_estimate=attention_cost(1, rows),
-        name="own_attention",
-    )(order, place, qa, qb, kv)
-
-
 def other_attention(order, place, qa, qb, acc, top, blocks):
     rows = qa.shape[0]
     chunk = QUARTER + TAIL
-    part = lambda a: pl.BlockSpec((1,) + a.shape[1:], lambda i, *s: (i, 0, 0))
     return pl.pallas_call(
         other_kernel,
         grid_spec=pltpu.PrefetchScalarGridSpec(
             num_scalar_prefetch=2,
             grid=(NH,),
-            in_specs=[whole(qa), whole(qb), part(acc), part(top)] + [whole(b) for b in blocks],
+            in_specs=[whole(a) for a in (qa, qb, acc, top, *blocks)],
             out_specs=pl.BlockSpec((4, chunk, HD), lambda i, o, s: (i ^ s[0], 0, 0)),
             scratch_shapes=[
                 pltpu.VMEM((rows, HD), jnp.bfloat16),
@@ -430,6 +420,8 @@
     for lag in range(3):
         start = (me - lag * row_patches + seq_count) % seq_count
         three = lax.dynamic_slice_in_dim(ringed, start, 3, axis=0)
+        pv = three.shape[2] // 2
+        three = jnp.concatenate([three[:, :, :pv], three[:, :, pv:]], axis=1)
         slab = (
             three.reshape(3, BLK, P_SIZE, P_SIZE, C)
             .transpose(0, 2, 1, 3, 4)
@@ -458,7 +450,6 @@
     x, h = span_me // NH, span_me % NH
     y, z, core = seq_me // (NZ * NC), (seq_me // NC) % NZ, seq_me % NC
     place = jnp.stack([h, y, z, core, x])
-    pv = latent_weight.shape[1]
     seq_count = NY * NZ * NC
 
     normed, gate_row = normalize(levels, hidden[0], modulation)
@@ -475,16 +466,15 @@
     q_hi = move_hi(q)
 
     matrix = latent_matrix(after(out_weight[0], mine_b), gate_row, latent_weight)
-    part = self_attention(place, q, kv, matrix)
+    part, acc, top = self_attention(place, q, kv, matrix)
     part = lax.all_to_all(part, "seq", 0, 0, tiled=True)
 
     out_w = after(out_weight[0], mine_b)
     w_core, w_far = move_core(out_w), move_y(out_w)
     weights = (out_w, w_core, w_far, move_core(w_far))
 
-    acc, top = own_attention(span_order, place, q, q_hi, kv)
     acc = after(acc, part)
-    chunks = other_attention(span_order, place, q, q_hi, acc, top, others)
+    chunks = other_attention(span_order, place, q, q_hi, acc, top, (kv, *others))
     groups = [
         [
             span_at(i, hh) * seq_count + seq_at(yy, j, cc)
@@ -507,15 +497,16 @@
     block_out = (hidden[0].astype(jnp.float32) + gate_row * summed).astype(jnp.bfloat16)[None]
 
     own_latents = jnp.dot(hidden[0], latent_weight, preferred_element_type=jnp.float32)
+    own_latents = jnp.concatenate([own_latents[: BLK // 2], own_latents[BLK // 2 :]], axis=1)
     latents = (jnp.sum(part.astype(jnp.float32), axis=0) + own_latents).astype(jnp.bfloat16)
     group_ids = jnp.arange(span_order.shape[0], dtype=jnp.int32)
     root = jnp.sum(jnp.where(span_order == 0, group_ids, 0))
     spread = lax.all_to_all(
-        jnp.broadcast_to(latents[None], (NX * NH, BLK, pv)), "span", 0, 0, tiled=True
+        jnp.broadcast_to(latents[None], (NX * NH,) + latents.shape), "span", 0, 0, tiled=True
     )
     latents = lax.dynamic_index_in_dim(spread, root, 0, keepdims=True)
     every = lax.all_to_all(
-        jnp.broadcast_to(latents, (seq_count, BLK, pv)), "seq", 0, 0, tiled=True
+        jnp.broadcast_to(latents, (seq_count,) + latents.shape[1:]), "seq", 0, 0, tiled=True
     )
     decoded = decode(every, decoder_weight.reshape(27 * C, decoder_weight.shape[4]))
     return (block_out, decoded)

time: 172 us -> 166 us (0.965); the launches traced: 172 us -> 164 us
  starting transfers between devices: 43.9 us -> 38.5 us
  local copies, waits for them, and re-layouts: 8.71 us -> 6.68 us
    all_to_all x2, starting transfers between devices: 16.8 us -> 10.2 us  [the longest x1 5.13 us: per_device(): lax.all_to_all(jnp.broadcast_to(latents[None], (NX * NH,) + latents.shape...]
    pallas_call x1 -> x0, Pallas kernels: 2.78 us -> none  [own_attention(): pl.pallas_call(own_kernel, grid_spec=pltpu.PrefetchScalarGridSpec(num_sca...]
    unnamed x30 -> x29, local copies, waits for them, and re-layouts: 5.48 us -> 3.34 us
    pallas_call x1, Pallas kernels: 8.63 us -> 10.5 us  [other_attention(): pl.pallas_call(other_kernel, grid_spec=pltpu.PrefetchScalarGridSpec(num_s...]
  transfers between devices with their start and end apart: 29 -> 29, of which waited for: 12 -> 12; matrix products, arithmetic and copies ran while one was open for 5% -> 4% of each run, Pallas kernels for 13% -> 13%
where the time goes in v1:
time: 166 us; the launch traced here: 164 us
  waiting for transfers between devices  54.5 us (33%)
  starting transfers between devices  38.5 us (23%)
  Pallas kernels  27.3 us (16%)
  between operations  17.1 us (10%)
  blocking collectives  15.9 us (10%)
  local copies, waits for them, and re-layouts  6.68 us (4%)
  other arithmetic  2.97 us (2%)
    all_to_all x1, blocking collectives, per_device(): part = lax.all_to_all(part, 'seq', 0, 0, tiled=True)  15.9 us
    ppermute x6, waiting for transfers between devices, move_y(): return lax.ppermute(a, 'seq', seq_route(dy=1))  13.3 us
    pallas_call x1, Pallas kernels, other_attention(): pl.pallas_call(other_kernel, grid_spec=pltpu.PrefetchScalarGridSpec(num_s...  10.5 us
    ppermute x9, waiting for transfers between devices, move_z(): return lax.ppermute(a, 'seq', seq_route(dz=d))  10.3 us
    all_to_all x1, waiting for transfers between devices, per_device(): lax.all_to_all(jnp.broadcast_to(latents, (seq_count,) + latents.shape[1:]...  10.3 us
    ppermute x9, starting transfers between devices, move_z(): return lax.ppermute(a, 'seq', seq_route(dz=d))  9.66 us
    all_to_all x1, waiting for transfers between devices, per_device(): lax.all_to_all(chunks, ('span', 'seq'), 0, 0, tiled=True, axis_index_grou...  9 us
    reduce_scatter x1, waiting for transfers between devices, per_device(): lax.psum_scatter(partial, 'seq', scatter_dimension=0, tiled=True, axis_in...  6.63 us
  transfers between devices with their start and end apart: 29, of which 12 were waited for; matrix products, arithmetic and copies ran while one was open for 4% of the time, Pallas kernels for 13%

profile of v1, /device:TPU:10, one launch (start us, length us, event | category | flops | bytes accessed | tf_op | source)
XLA Modules:
  0.0 163.9 jit_solution(1630453207012327387)
XLA Ops:
  7.2 0.1 collective-permute-start.7
  7.9 2.0 %normalize.1 = (bf16[32,3072]{1,0:T(8,128)(2,1)}, f32[1,3072]{1,0:T(1,128)}) custom-call(s32[1]{0:T(128)S(6)} %copy.37.level_ref, bf16[32,3072]{1,0:T(8,128)(2,1)} %bitcast.48, f32[3,16,3072]{2,1,0:T(8,128)} %bitcast.49), custom_call_target="tpu_custom_call" | custom-call | tf_op jit(solution)/shard_map/normalize/pallas_call | solution.py:114
  10.0 1.9 %collective-permute-start.2 = (bf16[32,3072]{1,0:T(8,128)(2,1)}, bf16[32,3072]{1,0:T(8,128)(2,1)S(1)}, u32[]{:S(2)}, u32[]{:S(2)}) collective-permute-start(bf16[32,3072]{1,0:T(8,128)(2,1)} %get-tuple-element.15.refs_0_), channel_id=1, source_target_pairs={{0,2},{1,3},{2,4},{3,5},{4,6},{5,7},{6,8},{7,9},{8,10},{9,11},{10,... | collective-permute-start | bytes 589832 | tf_op jit(solution)/shard_map/ppermute | solution.py:48
  11.9 3.9 %collective-permute-start = (bf16[32,3072]{1,0:T(8,128)(2,1)}, bf16[32,3072]{1,0:T(8,128)(2,1)S(1)}, u32[]{:S(2)}, u32[]{:S(2)}) collective-permute-start(bf16[32,3072]{1,0:T(8,128)(2,1)} %get-tuple-element.15.refs_0_), channel_id=1, source_target_pairs={{0,14},{1,15},{2,0},{3,1},{4,2},{5,3},{6,4},{7,5},{8,6},{9,7},{10,... | collective-permute-start | bytes 589832 | tf_op jit(solution)/shard_map/ppermute | solution.py:48
  15.8 0.4 collective-permute-start.4
  16.3 5.3 %collective-permute-done.2.refs_4_ = bf16[32,3072]{1,0:T(8,128)(2,1)S(1)} collective-permute-done((bf16[32,3072]{1,0:T(8,128)(2,1)}, bf16[32,3072]{1,0:T(8,128)(2,1)S(1)}, u32[]{:S(2)}, u32[]{:S(2)}) %collective-permute-start.2) | collective-permute-done | bytes 196640 | tf_op jit(solution)/shard_map/ppermute | solution.py:48
  21.6 3.2 %collective-permute-start.1 = (bf16[32,3072]{1,0:T(8,128)(2,1)S(1)}, bf16[32,3072]{1,0:T(8,128)(2,1)S(1)}, u32[]{:S(2)}, u32[]{:S(2)}) collective-permute-start(bf16[32,3072]{1,0:T(8,128)(2,1)S(1)} %collective-permute-done.refs_1_), channel_id=1, source_target_pairs={{0,14},{1,15},{2,0},{3,1},{4,2},{5,3},{6,4},{7,5},{8,6},{9,7},{10,... | collective-permute-start | bytes 589832 | tf_op jit(solution)/shard_map/ppermute | solution.py:48
  24.8 0.4 collective-permute-start.5
  25.3 1.6 collective-permute-start.6
  26.9 2.7 %collective-permute-done.3.refs_3_ = bf16[32,3072]{1,0:T(8,128)(2,1)S(1)} collective-permute-done((bf16[32,3072]{1,0:T(8,128)(2,1)S(1)}, bf16[32,3072]{1,0:T(8,128)(2,1)S(1)}, u32[]{:S(2)}, u32[]{:S(2)}) %collective-permute-start.3) | collective-permute-done | bytes 196640 | tf_op jit(solution)/shard_map/ppermute | solution.py:48
  29.6 0.5 collective-permute-start.12
  30.0 2.7 %collective-permute-done.5.refs_6_ = bf16[32,3072]{1,0:T(8,128)(2,1)S(1)} collective-permute-done((bf16[32,3072]{1,0:T(8,128)(2,1)S(1)}, bf16[32,3072]{1,0:T(8,128)(2,1)S(1)}, u32[]{:S(2)}, u32[]{:S(2)}) %collective-permute-start.5) | collective-permute-done | bytes 196640 | tf_op jit(solution)/shard_map/ppermute | solution.py:52
  32.7 0.6 collective-permute-start.9
  33.2 3.7 %collective-permute-done.6.refs_7_ = bf16[32,3072]{1,0:T(8,128)(2,1)S(1)} collective-permute-done((bf16[32,3072]{1,0:T(8,128)(2,1)S(1)}, bf16[32,3072]{1,0:T(8,128)(2,1)S(1)}, u32[]{:S(2)}, u32[]{:S(2)}) %collective-permute-start.6) | collective-permute-done | bytes 196640 | tf_op jit(solution)/shard_map/ppermute | solution.py:52
  36.9 0.4 collective-permute-start.15
  37.4 3.8 %collective-permute-done.12.refs_3_ = bf16[32,3072]{1,0:T(8,128)(2,1)S(1)} collective-permute-done((bf16[32,3072]{1,0:T(8,128)(2,1)S(1)}, bf16[32,3072]{1,0:T(8,128)(2,1)S(1)}, u32[]{:S(2)}, u32[]{:S(2)}) %collective-permute-start.12) | collective-permute-done | bytes 196640 | tf_op jit(solution)/shard_map/ppermute | solution.py:52
  41.1 1.4 collective-permute-start.14
  42.5 3.2 %collective-permute-done.15.refs_7_ = bf16[32,3072]{1,0:T(8,128)(2,1)S(1)} collective-permute-done((bf16[32,3072]{1,0:T(8,128)(2,1)S(1)}, bf16[32,3072]{1,0:T(8,128)(2,1)S(1)}, u32[]{:S(2)}, u32[]{:S(2)}) %collective-permute-start.15) | collective-permute-done | bytes 196640 | tf_op jit(solution)/shard_map/ppermute | solution.py:52
  45.8 1.7 %copy-done.1 = bf16[1,3072,384]{2,1,0:T(8,128)(2,1)S(1)} copy-done((bf16[1,3072,384]{2,1,0:T(8,128)(2,1)S(1)}, bf16[1,3072,384]{2,1,0:T(8,128)(2,1)}, u32[]{:S(2)}) %copy-start.1) | copy-done | bytes 2359320
  47.4 0.9 copy-done.5
  48.4 1.8 %project.2 = (bf16[256,384]{1,0:T(8,128)(2,1)S(1)}, bf16[256,384]{1,0:T(8,128)(2,1)S(1)}) custom-call(bf16[32,3072]{1,0:T(8,128)(2,1)S(1)} %copy-done.5, bf16[32,3072]{1,0:T(8,128)(2,1)S(1)} %collective-permute-done.refs_1_, bf16[32,3072]{1,0:T(8,128)(2,1)S(1)} %collective-permute-done.1.refs_2_, bf16[32,3072]{1,0:T(8,128)(2,1)S(1)} %collective-permute-done.3.refs_3_, ...), custom_call_target="tpu_custom_call" | custom-call | flops 1207959552 | bytes 6291456 | tf_op jit(solution)/shard_map/project/pallas_call | solution.py:170
  50.2 0.1 collective-permute-start.8
  50.3 2.3 %collective-permute-done.16.refs_6_ = bf16[32,3072]{1,0:T(8,128)(2,1)S(1)} collective-permute-done((bf16[32,3072]{1,0:T(8,128)(2,1)S(1)}, bf16[32,3072]{1,0:T(8,128)(2,1)S(1)}, u32[]{:S(2)}, u32[]{:S(2)}) %collective-permute-start.16) | collective-permute-done | bytes 196640 | tf_op jit(solution)/shard_map/ppermute | solution.py:48
  52.6 1.8 %project.3 = (bf16[256,384]{1,0:T(8,128)(2,1)S(1)}, bf16[256,384]{1,0:T(8,128)(2,1)S(1)}) custom-call(bf16[32,3072]{1,0:T(8,128)(2,1)S(1)} %collective-permute-done.9.refs_0_, bf16[32,3072]{1,0:T(8,128)(2,1)S(1)} %collective-permute-done.11.refs_1_, bf16[32,3072]{1,0:T(8,128)(2,1)S(1)} %collective-permute-done.10.refs_2_, ...), custom_call_target="tpu_custom_call" | custom-call | flops 1207959552 | bytes 6291456 | tf_op jit(solution)/shard_map/project/pallas_call | solution.py:170
  54.5 0.1 collective-permute-start.17
  54.6 0.1 collective-permute-start.23
  54.8 1.2 collective-permute-done.17
  56.1 1.6 collective-permute-start.19
  57.7 0.5 collective-permute-start.20
  58.2 2.1 %collective-permute-start.21 = (bf16[1024,256]{1,0:T(8,128)(2,1)S(1)}, bf16[1024,256]{1,0:T(8,128)(2,1)}, u32[]{:S(2)}, u32[]{:S(2)}) collective-permute-start(bf16[1024,256]{1,0:T(8,128)(2,1)S(1)} %slice.178.kv_ref.k0), channel_id=1, source_target_pairs={{0,128},{32,160},{64,192},{96,224},{128,0},{160,32},{192,64},{224,... | collective-permute-start | bytes 1572872 | tf_op jit(solution)/shard_map/ppermute | solution.py:60
  60.4 0.6 latent_matrix.1.m_ref
  61.0 1.0 slice.177.q_ref.qa_ref
  62.0 2.4 %collective-permute-start.18 = (bf16[1024,128]{1,0:T(8,128)(2,1)S(1)}, bf16[1024,128]{1,0:T(8,128)(2,1)S(1)}, u32[]{:S(2)}, u32[]{:S(2)}) collective-permute-start(bf16[1024,128]{1,0:T(8,128)(2,1)S(1)} %slice.177.q_ref.qa_ref), channel_id=1, source_target_pairs={{0,32},{32,0},{64,96},{96,64},{128,160},{160,128},{192,224},{224,1... | collective-permute-start | bytes 786440 | tf_op jit(solution)/shard_map/ppermute | solution.py:64
  64.4 5.2 %self_attention.1 = (bf16[32,16,128]{2,1,0:T(8,128)(2,1)S(1)}, f32[1024,256]{1,0:T(8,128)S(1)}, f32[1024,128]{1,0:T(8,128)S(1)}) custom-call(s32[5]{0:T(128)S(1)} %stack.23.s_ref, bf16[1024,128]{1,0:T(8,128)(2,1)S(1)} %slice.177.q_ref.qa_ref, bf16[1024,256]{1,0:T(8,128)(2,1)S(1)} %slice.178.kv_ref.k0, bf16[256,64]{1,0:T(8,128)(2,1)S(1)} %latent_matrix.1.m_ref), custom_call_target="tpu_custom_call" | custom-call | flops 805306368 | bytes 1048576 | tf_op jit(solution)/shard_map/self_attention/pallas_call | solution.py:225
  69.6 15.9 %all_to_all.20 = bf16[32,16,128]{2,1,0:T(8,128)(2,1)S(1)} all-to-all(bf16[32,16,128]{2,1,0:T(8,128)(2,1)S(1)} %get-tuple-element.22), channel_id=1, replica_groups=mesh['span'=8,'seq'=32] {'seq'}, dimensions={0} | all-to-all | bytes 262144 | tf_op jit(solution)/shard_map/all_to_all | solution.py:470
  85.5 0.5 collective-permute-start.24
  86.1 10.5 %other_attention.1 = bf16[8,272,128]{2,1,0:T(8,128)(2,1)} custom-call(s32[8]{0:T(128)S(1)} %copy-done.7, s32[5]{0:T(128)S(1)} %stack.23.s_ref, bf16[1024,128]{1,0:T(8,128)(2,1)S(1)} %slice.177.q_ref.qa_ref, bf16[1024,128]{1,0:T(8,128)(2,1)S(1)} %collective-permute-done.18.qb_ref, f32[1024,256]{1,0:T(8,128)S(1)} %get-tuple-element.23.acc_in, ...), custom_call_target="tpu_custom_call" | custom-call | flops 4831838208 | bytes 4194304 | tf_op jit(solution)/shard_map/other_attention/pallas_call | solution.py:327
  96.5 6.3 %all-to-all-start.1 = ((bf16[8,272,128]{2,1,0:T(8,128)(2,1)}), bf16[8,272,128]{2,1,0:T(8,128)(2,1)S(1)}, u32[]{:S(2)}, u32[]{:S(2)}) async-start(bf16[8,272,128]{2,1,0:T(8,128)(2,1)} %other_attention.1), calls=%async_computation.1 | async-start | bytes 1114112 | tf_op jit(solution)/shard_map/all_to_all | solution.py:488
  102.9 0.2 fusion.4
  103.1 9.0 %all-to-all-done.1.in_ref = bf16[8,272,128]{2,1,0:T(8,128)(2,1)S(1)} async-done(((bf16[8,272,128]{2,1,0:T(8,128)(2,1)}), bf16[8,272,128]{2,1,0:T(8,128)(2,1)S(1)}, u32[]{:S(2)}, u32[]{:S(2)}) %all-to-all-start.1) | async-done | bytes 557088 | tf_op jit(solution)/shard_map/all_to_all | solution.py:488
  112.1 5.4 %join_heads.1 = bf16[256,3072]{1,0:T(8,128)(2,1)} custom-call(s32[5]{0:T(128)S(1)} %stack.23.s_ref, bf16[8,272,128]{2,1,0:T(8,128)(2,1)S(1)} %all-to-all-done.1.in_ref, bf16[128,3072]{1,0:T(8,128)(2,1)S(1)} %bitcast.45, bf16[128,3072]{1,0:T(8,128)(2,1)} %collective-permute-done.22.w1_ref, bf16[128,3072]{1,0:T(8,128)(2,1)S(1)} %collective-permute-done.23.w2_ref, ...), custom_call_target="tpu_custom_call" | custom-call | tf_op jit(solution)/shard_map/join_heads/pallas_call | solution.py:386
  117.7 0.6 broadcast_in_dim.59
  118.3 5.1 %all-to-all-start.2 = ((bf16[8,16,128]{2,1,0:T(8,128)(2,1)}), bf16[8,16,128]{2,1,0:T(8,128)(2,1)S(1)}, u32[]{:S(2)}, u32[]{:S(2)}) async-start(bf16[8,16,128]{2,1,0:T(8,128)(2,1)} %broadcast_in_dim.59), calls=%async_computation.3 | async-start | bytes 65536 | tf_op jit(solution)/shard_map/all_to_all | solution.py:504
  123.4 0.6 fusion.3
  126.0 3.7 %all-to-all-done.2 = bf16[8,16,128]{2,1,0:T(8,128)(2,1)S(1)} async-done(((bf16[8,16,128]{2,1,0:T(8,128)(2,1)}), bf16[8,16,128]{2,1,0:T(8,128)(2,1)S(1)}, u32[]{:S(2)}, u32[]{:S(2)}) %all-to-all-start.2) | async-done | bytes 32800 | tf_op jit(solution)/shard_map/all_to_all | solution.py:504
  129.7 0.7 broadcast_in_dim.61
  130.4 5.0 %all-to-all-start.3 = ((bf16[32,16,128]{2,1,0:T(8,128)(2,1)}), bf16[32,16,128]{2,1,0:T(8,128)(2,1)S(1)}, u32[]{:S(2)}, u32[]{:S(2)}) async-start(bf16[32,16,128]{2,1,0:T(8,128)(2,1)} %broadcast_in_dim.61), calls=%async_computation.4 | async-start | bytes 262144 | tf_op jit(solution)/shard_map/all_to_all | solution.py:508
  135.5 10.3 %all-to-all-done.3 = bf16[32,16,128]{2,1,0:T(8,128)(2,1)S(1)} async-done(((bf16[32,16,128]{2,1,0:T(8,128)(2,1)}), bf16[32,16,128]{2,1,0:T(8,128)(2,1)S(1)}, u32[]{:S(2)}, u32[]{:S(2)}) %all-to-all-start.3) | async-done | bytes 131104 | tf_op jit(solution)/shard_map/all_to_all | solution.py:508
  145.9 0.1 copy.32
  146.0 0.1 copy.33
  146.1 0.1 pad_maximum_fusion.3
  146.2 0.1 copy.21
  146.3 0.1 copy.29
  146.4 0.1 copy.30
  146.5 0.1 pad_maximum_fusion.2
  146.6 0.1 copy.19
  146.8 0.1 copy.26
  146.9 0.1 copy.27
  147.0 0.1 pad_maximum_fusion.1
  147.1 0.1 copy.17
  147.6 0.4 concatenate.31
  148.0 0.8 fusion
  148.8 6.6 %reduce-scatter.2.cloned.1.call-done = bf16[32,3072]{1,0:T(8,128)(2,1)} async-done(((bf16[256,3072]{1,0:T(8,128)(2,1)}), bf16[32,3072]{1,0:T(8,128)(2,1)}) %reduce-scatter.2.cloned.1.call-update) | async-done | bytes 196624 | tf_op jit(solution)/shard_map/reduce_scatter | solution.py:494
  155.4 1.7 %fusion.1 = bf16[1,32,3072]{2,1,0:T(8,128)(2,1)} fusion(bf16[32,3072]{1,0:T(8,128)(2,1)} %reduce-scatter.2.cloned.1.call-done, f32[3072]{0:T(1024)S(1)} %bitcast.47, bf16[1,32,3072]{2,1,0:T(8,128)(2,1)S(1)} %copy-done.8), kind=kLoop, calls=%fused_computation.4 | loop fusion | flops 491520 | bytes 602112 | tf_op jit(solution)/shard_map/broadcast_in_dim | solution.py:497
  (64 shorter events, 1.0 us)
Async XLA Ops:
  7.2 140.8 %copy-start = (bf16[3,3,3,16,64]{4,3,2,1,0:T(8,128)(2,1)S(1)}, bf16[3,3,3,16,64]{4,3,2,1,0:T(8,128)(2,1)}, u32[]{:S(2)}) copy-start(bf16[3,3,3,16,64]{4,3,2,1,0:T(8,128)(2,1)} %param.15) | copy-start | bytes 165892
  7.2 38.6 %collective-permute-start.7 = (bf16[3072,384]{1,0:T(8,128)(2,1)}, bf16[3072,384]{1,0:T(8,128)(2,1)S(1)}, u32[]{:S(2)}, u32[]{:S(2)}) collective-permute-start(bf16[3072,384]{1,0:T(8,128)(2,1)} %bitcast.39), channel_id=1, source_target_pairs={{0,1},{1,0},{2,3},{3,2},{4,5},{5,4},{6,7},{7,6},{8,9},{9,8},{10,11... | collective-permute-start | bytes 7077896 | tf_op jit(solution)/shard_map/ppermute | solution.py:56
  10.0 11.6 %collective-permute-start.2 = (bf16[32,3072]{1,0:T(8,128)(2,1)}, bf16[32,3072]{1,0:T(8,128)(2,1)S(1)}, u32[]{:S(2)}, u32[]{:S(2)}) collective-permute-start(bf16[32,3072]{1,0:T(8,128)(2,1)} %get-tuple-element.15.refs_0_), channel_id=1, source_target_pairs={{0,2},{1,3},{2,4},{3,5},{4,6},{5,7},{6,8},{7,9},{8,10},{9,11},{10,... | collective-permute-start | bytes 589832 | tf_op jit(solution)/shard_map/ppermute | solution.py:48
  11.9 9.7 %collective-permute-start = (bf16[32,3072]{1,0:T(8,128)(2,1)}, bf16[32,3072]{1,0:T(8,128)(2,1)S(1)}, u32[]{:S(2)}, u32[]{:S(2)}) collective-permute-start(bf16[32,3072]{1,0:T(8,128)(2,1)} %get-tuple-element.15.refs_0_), channel_id=1, source_target_pairs={{0,14},{1,15},{2,0},{3,1},{4,2},{5,3},{6,4},{7,5},{8,6},{9,7},{10,... | collective-permute-start | bytes 589832 | tf_op jit(solution)/shard_map/ppermute | solution.py:48
  15.8 9.5 %collective-permute-start.4 = (bf16[32,3072]{1,0:T(8,128)(2,1)}, bf16[32,3072]{1,0:T(8,128)(2,1)S(1)}, u32[]{:S(2)}, u32[]{:S(2)}) collective-permute-start(bf16[32,3072]{1,0:T(8,128)(2,1)} %get-tuple-element.15.refs_0_), channel_id=1, source_target_pairs={{0,16},{1,17},{2,18},{3,19},{4,20},{5,21},{6,22},{7,23},{8,24},{9,... | collective-permute-start | bytes 589832 | tf_op jit(solution)/shard_map/ppermute | solution.py:52
  21.6 7.9 %collective-permute-start.3 = (bf16[32,3072]{1,0:T(8,128)(2,1)S(1)}, bf16[32,3072]{1,0:T(8,128)(2,1)S(1)}, u32[]{:S(2)}, u32[]{:S(2)}) collective-permute-start(bf16[32,3072]{1,0:T(8,128)(2,1)S(1)} %collective-permute-done.2.refs_4_), channel_id=1, source_target_pairs={{0,2},{1,3},{2,4},{3,5},{4,6},{5,7},{6,8},{7,9},{8,10},{9,11},{10,... | collective-permute-start | bytes 589832 | tf_op jit(solution)/shard_map/ppermute | solution.py:48
  21.6 7.9 %collective-permute-start.1 = (bf16[32,3072]{1,0:T(8,128)(2,1)S(1)}, bf16[32,3072]{1,0:T(8,128)(2,1)S(1)}, u32[]{:S(2)}, u32[]{:S(2)}) collective-permute-start(bf16[32,3072]{1,0:T(8,128)(2,1)S(1)} %collective-permute-done.refs_1_), channel_id=1, source_target_pairs={{0,14},{1,15},{2,0},{3,1},{4,2},{5,3},{6,4},{7,5},{8,6},{9,7},{10,... | collective-permute-start | bytes 589832 | tf_op jit(solution)/shard_map/ppermute | solution.py:48
  24.8 7.8 %collective-permute-start.5 = (bf16[32,3072]{1,0:T(8,128)(2,1)S(1)}, bf16[32,3072]{1,0:T(8,128)(2,1)S(1)}, u32[]{:S(2)}, u32[]{:S(2)}) collective-permute-start(bf16[32,3072]{1,0:T(8,128)(2,1)S(1)} %collective-permute-done.refs_1_), channel_id=1, source_target_pairs={{0,16},{1,17},{2,18},{3,19},{4,20},{5,21},{6,22},{7,23},{8,24},{9,... | collective-permute-start | bytes 589832 | tf_op jit(solution)/shard_map/ppermute | solution.py:52
  25.3 11.6 %collective-permute-start.6 = (bf16[32,3072]{1,0:T(8,128)(2,1)S(1)}, bf16[32,3072]{1,0:T(8,128)(2,1)S(1)}, u32[]{:S(2)}, u32[]{:S(2)}) collective-permute-start(bf16[32,3072]{1,0:T(8,128)(2,1)S(1)} %collective-permute-done.2.refs_4_), channel_id=1, source_target_pairs={{0,16},{1,17},{2,18},{3,19},{4,20},{5,21},{6,22},{7,23},{8,24},{9,... | collective-permute-start | bytes 589832 | tf_op jit(solution)/shard_map/ppermute | solution.py:52
  29.5 7.8 %collective-permute-start.10 = (bf16[32,3072]{1,0:T(8,128)(2,1)S(1)}, bf16[32,3072]{1,0:T(8,128)(2,1)S(1)}, u32[]{:S(2)}, u32[]{:S(2)}) collective-permute-start(bf16[32,3072]{1,0:T(8,128)(2,1)S(1)} %collective-permute-done.3.refs_3_), channel_id=1, source_target_pairs={{0,2},{1,3},{2,4},{3,5},{4,6},{5,7},{6,8},{7,9},{8,10},{9,11},{10,... | collective-permute-start | bytes 589832 | tf_op jit(solution)/shard_map/ppermute | solution.py:48
  29.6 11.6 %collective-permute-start.12 = (bf16[32,3072]{1,0:T(8,128)(2,1)S(1)}, bf16[32,3072]{1,0:T(8,128)(2,1)S(1)}, u32[]{:S(2)}, u32[]{:S(2)}) collective-permute-start(bf16[32,3072]{1,0:T(8,128)(2,1)S(1)} %collective-permute-done.1.refs_2_), channel_id=1, source_target_pairs={{0,16},{1,17},{2,18},{3,19},{4,20},{5,21},{6,22},{7,23},{8,24},{9,... | collective-permute-start | bytes 589832 | tf_op jit(solution)/shard_map/ppermute | solution.py:52
  32.7 8.4 %collective-permute-start.9 = (bf16[32,3072]{1,0:T(8,128)(2,1)S(1)}, bf16[32,3072]{1,0:T(8,128)(2,1)S(1)}, u32[]{:S(2)}, u32[]{:S(2)}) collective-permute-start(bf16[32,3072]{1,0:T(8,128)(2,1)S(1)} %collective-permute-done.1.refs_2_), channel_id=1, source_target_pairs={{0,14},{1,15},{2,0},{3,1},{4,2},{5,3},{6,4},{7,5},{8,6},{9,7},{10,... | collective-permute-start | bytes 589832 | tf_op jit(solution)/shard_map/ppermute | solution.py:48
  36.9 8.9 %collective-permute-start.15 = (bf16[32,3072]{1,0:T(8,128)(2,1)S(1)}, bf16[32,3072]{1,0:T(8,128)(2,1)S(1)}, u32[]{:S(2)}, u32[]{:S(2)}) collective-permute-start(bf16[32,3072]{1,0:T(8,128)(2,1)S(1)} %collective-permute-done.3.refs_3_), channel_id=1, source_target_pairs={{0,16},{1,17},{2,18},{3,19},{4,20},{5,21},{6,22},{7,23},{8,24},{9,... | collective-permute-start | bytes 589832 | tf_op jit(solution)/shard_map/ppermute | solution.py:52
  37.4 12.9 %collective-permute-start.11 = (bf16[32,3072]{1,0:T(8,128)(2,1)S(1)}, bf16[32,3072]{1,0:T(8,128)(2,1)S(1)}, u32[]{:S(2)}, u32[]{:S(2)}) collective-permute-start(bf16[32,3072]{1,0:T(8,128)(2,1)S(1)} %collective-permute-done.10.refs_2_), channel_id=1, source_target_pairs={{0,2},{1,3},{2,4},{3,5},{4,6},{5,7},{6,8},{7,9},{8,10},{9,11},{10,... | collective-permute-start | bytes 589832 | tf_op jit(solution)/shard_map/ppermute | solution.py:48
  41.1 9.2 %collective-permute-start.13 = (bf16[32,3072]{1,0:T(8,128)(2,1)S(1)}, bf16[32,3072]{1,0:T(8,128)(2,1)S(1)}, u32[]{:S(2)}, u32[]{:S(2)}) collective-permute-start(bf16[32,3072]{1,0:T(8,128)(2,1)S(1)} %collective-permute-done.12.refs_3_), channel_id=1, source_target_pairs={{0,14},{1,15},{2,0},{3,1},{4,2},{5,3},{6,4},{7,5},{8,6},{9,7},{10,... | collective-permute-start | bytes 589832 | tf_op jit(solution)/shard_map/ppermute | solution.py:48
  41.1 9.2 %collective-permute-start.14 = (bf16[32,3072]{1,0:T(8,128)(2,1)S(1)}, bf16[32,3072]{1,0:T(8,128)(2,1)S(1)}, u32[]{:S(2)}, u32[]{:S(2)}) collective-permute-start(bf16[32,3072]{1,0:T(8,128)(2,1)S(1)} %collective-permute-done.9.refs_0_), channel_id=1, source_target_pairs={{0,30},{1,31},{2,16},{3,17},{4,18},{5,19},{6,20},{7,21},{8,22},{9,... | collective-permute-start | bytes 589832 | tf_op jit(solution)/shard_map/ppermute | solution.py:92
  45.8 6.9 %collective-permute-start.16 = (bf16[32,3072]{1,0:T(8,128)(2,1)S(1)}, bf16[32,3072]{1,0:T(8,128)(2,1)S(1)}, u32[]{:S(2)}, u32[]{:S(2)}) collective-permute-start(bf16[32,3072]{1,0:T(8,128)(2,1)S(1)} %collective-permute-done.15.refs_7_), channel_id=1, source_target_pairs={{0,2},{1,3},{2,4},{3,5},{4,6},{5,7},{6,8},{7,9},{8,10},{9,11},{10,... | collective-permute-start | bytes 589832 | tf_op jit(solution)/shard_map/ppermute | solution.py:48
  45.8 1.7 %copy-start.1 = (bf16[1,3072,384]{2,1,0:T(8,128)(2,1)S(1)}, bf16[1,3072,384]{2,1,0:T(8,128)(2,1)}, u32[]{:S(2)}) copy-start(bf16[1,3072,384]{2,1,0:T(8,128)(2,1)} %param.12) | copy-start | bytes 7077892
  47.4 0.9 copy-start.5
  48.4 4.3 %copy-start.2 = (bf16[1,3072,384]{2,1,0:T(8,128)(2,1)S(1)}, bf16[1,3072,384]{2,1,0:T(8,128)(2,1)}, u32[]{:S(2)}) copy-start(bf16[1,3072,384]{2,1,0:T(8,128)(2,1)} %param.12) | copy-start | bytes 7077892
  50.2 4.4 %copy-start.3 = (bf16[1,128,3072]{2,1,0:T(8,128)(2,1)S(1)}, bf16[1,128,3072]{2,1,0:T(8,128)(2,1)}, u32[]{:S(2)}) copy-start(bf16[1,128,3072]{2,1,0:T(8,128)(2,1)} %param.13) | copy-start | bytes 2359300
  50.2 4.5 %collective-permute-start.8 = (bf16[256,384]{1,0:T(8,128)(2,1)S(1)}, bf16[256,384]{1,0:T(8,128)(2,1)S(1)}, u32[]{:S(2)}, u32[]{:S(2)}) collective-permute-start(bf16[256,384]{1,0:T(8,128)(2,1)S(1)} %get-tuple-element.17), channel_id=1, source_target_pairs={{0,1},{1,0},{2,3},{3,2},{4,5},{5,4},{6,7},{7,6},{8,9},{9,8},{10,11... | collective-permute-start | bytes 589832 | tf_op jit(solution)/shard_map/ppermute | solution.py:56
  54.5 6.0 %copy-start.4 = (bf16[3072,64]{0,1:T(8,128)(2,1)S(1)}, bf16[3072,64]{0,1:T(8,128)(2,1)}, u32[]{:S(2)}) copy-start(bf16[3072,64]{0,1:T(8,128)(2,1)} %param.14) | copy-start | bytes 1179652
  54.5 6.0 %copy-start.6 = (f32[1,3072]{1,0:T(1,128)S(1)}, f32[1,3072]{1,0:T(1,128)}, u32[]{:S(2)}) copy-start(f32[1,3072]{1,0:T(1,128)} %get-tuple-element.14.gate_ref) | copy-start | bytes 36868
  54.5 1.5 collective-permute-start.17
  54.6 30.9 %collective-permute-start.23 = (bf16[128,3072]{1,0:T(8,128)(2,1)S(1)}, bf16[128,3072]{1,0:T(8,128)(2,1)S(1)}, u32[]{:S(2)}, u32[]{:S(2)}) collective-permute-start(bf16[128,3072]{1,0:T(8,128)(2,1)S(1)} %bitcast.42), channel_id=1, source_target_pairs={{0,16},{1,17},{2,18},{3,19},{4,20},{5,21},{6,22},{7,23},{8,24},{9,... | collective-permute-start | bytes 2359304 | tf_op jit(solution)/shard_map/ppermute | solution.py:52
  56.0 1.6 copy-start.9
  56.1 29.9 %collective-permute-start.19 = (bf16[1024,256]{1,0:T(8,128)(2,1)S(1)}, bf16[1024,256]{1,0:T(8,128)(2,1)}, u32[]{:S(2)}, u32[]{:S(2)}) collective-permute-start(bf16[1024,256]{1,0:T(8,128)(2,1)S(1)} %slice.178.kv_ref.k0), channel_id=1, source_target_pairs={{0,64},{32,96},{64,128},{96,160},{128,192},{160,224},{192,0},{224,... | collective-permute-start | bytes 1572872 | tf_op jit(solution)/shard_map/ppermute | solution.py:60
  57.7 28.4 %collective-permute-start.20 = (bf16[1024,256]{1,0:T(8,128)(2,1)S(1)}, bf16[1024,256]{1,0:T(8,128)(2,1)}, u32[]{:S(2)}, u32[]{:S(2)}) collective-permute-start(bf16[1024,256]{1,0:T(8,128)(2,1)S(1)} %slice.178.kv_ref.k0), channel_id=1, source_target_pairs={{0,192},{32,224},{64,0},{96,32},{128,64},{160,96},{192,128},{224,1... | collective-permute-start | bytes 1572872 | tf_op jit(solution)/shard_map/ppermute | solution.py:60
  58.2 27.8 %collective-permute-start.21 = (bf16[1024,256]{1,0:T(8,128)(2,1)S(1)}, bf16[1024,256]{1,0:T(8,128)(2,1)}, u32[]{:S(2)}, u32[]{:S(2)}) collective-permute-start(bf16[1024,256]{1,0:T(8,128)(2,1)S(1)} %slice.178.kv_ref.k0), channel_id=1, source_target_pairs={{0,128},{32,160},{64,192},{96,224},{128,0},{160,32},{192,64},{224,... | collective-permute-start | bytes 1572872 | tf_op jit(solution)/shard_map/ppermute | solution.py:60
  60.4 25.6 %copy-start.7 = (s32[8]{0:T(128)S(1)}, s32[8]{0:T(128)}, u32[]{:S(2)}) copy-start(s32[8]{0:T(128)} %order_ref.1) | copy-start | bytes 100
  62.0 23.5 %collective-permute-start.18 = (bf16[1024,128]{1,0:T(8,128)(2,1)S(1)}, bf16[1024,128]{1,0:T(8,128)(2,1)S(1)}, u32[]{:S(2)}, u32[]{:S(2)}) collective-permute-start(bf16[1024,128]{1,0:T(8,128)(2,1)S(1)} %slice.177.q_ref.qa_ref), channel_id=1, source_target_pairs={{0,32},{32,0},{64,96},{96,64},{128,160},{160,128},{192,224},{224,1... | collective-permute-start | bytes 786440 | tf_op jit(solution)/shard_map/ppermute | solution.py:64
  85.5 17.6 %collective-permute-start.22 = (bf16[128,3072]{1,0:T(8,128)(2,1)S(1)}, bf16[128,3072]{1,0:T(8,128)(2,1)}, u32[]{:S(2)}, u32[]{:S(2)}) collective-permute-start(bf16[128,3072]{1,0:T(8,128)(2,1)S(1)} %bitcast.44), channel_id=1, source_target_pairs={{0,1},{1,0},{2,3},{3,2},{4,5},{5,4},{6,7},{7,6},{8,9},{9,8},{10,11... | collective-permute-start | bytes 2359304 | tf_op jit(solution)/shard_map/ppermute | solution.py:56
  85.5 26.6 %collective-permute-start.24 = (bf16[128,3072]{1,0:T(8,128)(2,1)S(1)}, bf16[128,3072]{1,0:T(8,128)(2,1)}, u32[]{:S(2)}, u32[]{:S(2)}) collective-permute-start(bf16[128,3072]{1,0:T(8,128)(2,1)S(1)} %collective-permute-done.23.w2_ref), channel_id=1, source_target_pairs={{0,1},{1,0},{2,3},{3,2},{4,5},{5,4},{6,7},{7,6},{8,9},{9,8},{10,11... | collective-permute-start | bytes 2359304 | tf_op jit(solution)/shard_map/ppermute | solution.py:56
  86.0 16.8 %copy-start.8 = (bf16[1,32,3072]{2,1,0:T(8,128)(2,1)S(1)}, bf16[1,32,3072]{2,1,0:T(8,128)(2,1)}, u32[]{:S(2)}) copy-start(bf16[1,32,3072]{2,1,0:T(8,128)(2,1)} %param.8) | copy-start | bytes 589828
  96.5 15.6 %all-to-all-start.1 = ((bf16[8,272,128]{2,1,0:T(8,128)(2,1)}), bf16[8,272,128]{2,1,0:T(8,128)(2,1)S(1)}, u32[]{:S(2)}, u32[]{:S(2)}) async-start(bf16[8,272,128]{2,1,0:T(8,128)(2,1)} %other_attention.1), calls=%async_computation.1 | async-start | bytes 1114112 | tf_op jit(solution)/shard_map/all_to_all | solution.py:488
  102.9 52.5 %reduce-scatter.2.cloned.1.call-start = ((), (), s32[]{:S(2)}) async-start(), calls=%async_computation.5 | async-start | bytes 1769472 | tf_op jit(solution)/shard_map/reduce_scatter | solution.py:494
  118.3 11.4 %all-to-all-start.2 = ((bf16[8,16,128]{2,1,0:T(8,128)(2,1)}), bf16[8,16,128]{2,1,0:T(8,128)(2,1)S(1)}, u32[]{:S(2)}, u32[]{:S(2)}) async-start(bf16[8,16,128]{2,1,0:T(8,128)(2,1)} %broadcast_in_dim.59), calls=%async_computation.3 | async-start | bytes 65536 | tf_op jit(solution)/shard_map/all_to_all | solution.py:504
  130.4 15.4 %all-to-all-start.3 = ((bf16[32,16,128]{2,1,0:T(8,128)(2,1)}), bf16[32,16,128]{2,1,0:T(8,128)(2,1)S(1)}, u32[]{:S(2)}, u32[]{:S(2)}) async-start(bf16[32,16,128]{2,1,0:T(8,128)(2,1)} %broadcast_in_dim.61), calls=%async_computation.4 | async-start | bytes 262144 | tf_op jit(solution)/shard_map/all_to_all | solution.py:508
Sparse Core Ops, SparseCore 0:
  117.6 37.7 reduce-scatter.1

commit v2 on v1

--- a/solution.py
+++ b/solution.py
@@ -248,15 +248,20 @@
     )(place, q, kv, matrix)
 
 
-def visit(kv_ref, q, values, acc, top):
-    values[:, :HD] = kv_ref[:, HD:]
+def visit(refs, q, values, acc, top):
+    at = 0
+    for ref in refs:
+        values[at : at + ref.shape[0], :HD] = ref[:, HD:]
+        at += ref.shape[0]
     values[:, HD:] = jnp.ones((values.shape[0], HD), jnp.bfloat16)
     for t in range(q.shape[0] // TILE):
         rows = slice(t * TILE, t * TILE + TILE)
-        s = dot_t(q[rows, :], kv_ref[:, :HD])
+        parts = [dot_t(q[rows, :], ref[:, :HD]) for ref in refs]
         old = top[rows, :1]
-        new = jnp.maximum(old, jnp.max(s, axis=1, keepdims=True))
-        p = jnp.exp2(s - new).astype(jnp.bfloat16)
+        new = old
+        for s in parts:
+            new = jnp.maximum(new, jnp.max(s, axis=1, keepdims=True))
+        p = jnp.concatenate([jnp.exp2(s - new).astype(jnp.bfloat16) for s in parts], axis=1)
         acc[rows, :] = acc[rows, :] * jnp.exp2(old - new) + jnp.dot(
             p, values[...], preferred_element_type=jnp.float32
         )
@@ -269,28 +274,36 @@
     return order_ref[((x + dx) % NX) * NH + h] <= mine
 
 
-def other_kernel(order_ref, s_ref, qa_ref, qb_ref, acc_in, top_in, k0, k1, k2, k3, o_ref, *scratch):
+def near_kernel(order_ref, s_ref, qa_ref, qb_ref, acc_in, top_in, k0, k1, k2, *refs):
+    acc_ref, top_ref, q, values = refs
+    dh = pl.program_id(0)
+    q[...] = jnp.where(dh == 0, qa_ref[...], qb_ref[...])
+
+    @pl.when(dh == 0)
+    def _():
+        acc_ref[0] = acc_in[...]
+        top_ref[0] = top_in[...]
+
+    @pl.when(dh == 1)
+    def _():
+        acc_ref[...] = jnp.zeros_like(acc_ref)
+        top_ref[...] = jnp.full_like(top_ref, -NEG_LARGE)
+
+    add = lambda ref: functools.partial(visit, (ref,), q, values, acc_ref.at[0], top_ref.at[0])
+    pl.when((dh == 1) & sees(order_ref, s_ref, dh, 0))(add(k0))
+    pl.when(sees(order_ref, s_ref, dh, NX - 1))(add(k1))
+    pl.when(sees(order_ref, s_ref, dh, 1))(add(k2))
+
+
+def far_kernel(order_ref, s_ref, qa_ref, qb_ref, acc_in, top_in, k3a, k3b, o_ref, *scratch):
     q, values, acc, top = scratch
     dh = pl.program_id(0)
     q[...] = jnp.where(dh == 0, qa_ref[...], qb_ref[...])
-
-    @pl.when(dh == 0)
-    def _():
-        acc[...] = acc_in[...]
-        top[...] = top_in[...]
-
-    @pl.when(dh == 1)
-    def _():
-        acc[...] = jnp.zeros_like(acc)
-        top[...] = jnp.full_like(top, -NEG_LARGE)
-
-    pl.when((dh == 1) & sees(order_ref, s_ref, dh, 0))(
-        functools.partial(visit, k0, q, values, acc, top)
-    )
-    for dx, ref in ((NX - 1, k1), (1, k2), (2, k3)):
-        pl.when(sees(order_ref, s_ref, dh, dx))(
-            functools.partial(visit, ref, q, values, acc, top)
-        )
+    acc[...] = acc_in[0]
+    top[...] = top_in[0]
+    pl.when(sees(order_ref, s_ref, dh, 2))(
+        functools.partial(visit, (k3a, k3b), q, values, acc, top)
+    )
     y, core = s_ref[1], s_ref[3]
     for quarter in range(4):
         starts = [block_at(quarter // 2, quarter % 2, d) * BLK for d in range(NZ)]
@@ -321,15 +334,41 @@
     return pl.CostEstimate(flops=6 * pairs * HD, bytes_accessed=4 * 2**20, transcendentals=pairs)
 
 
-def other_attention(order, place, qa, qb, acc, top, blocks):
+def near_attention(order, place, qa, qb, acc, top, blocks):
     rows = qa.shape[0]
-    chunk = QUARTER + TAIL
-    return pl.pallas_call(
-        other_kernel,
+    out = lambda cols: pl.BlockSpec((1, rows, cols), lambda i, *s: (i, 0, 0))
+    return pl.pallas_call(
+        near_kernel,
         grid_spec=pltpu.PrefetchScalarGridSpec(
             num_scalar_prefetch=2,
             grid=(NH,),
             in_specs=[whole(a) for a in (qa, qb, acc, top, *blocks)],
+            out_specs=[out(2 * HD), out(128)],
+            scratch_shapes=[
+                pltpu.VMEM((rows, HD), jnp.bfloat16),
+                pltpu.VMEM((rows, 2 * HD), jnp.bfloat16),
+            ],
+        ),
+        out_shape=[
+            jax.ShapeDtypeStruct((NH, rows, 2 * HD), jnp.float32),
+            jax.ShapeDtypeStruct((NH, rows, 128), jnp.float32),
+        ],
+        compiler_params=pltpu.CompilerParams(vmem_limit_bytes=20 * 2**20),
+        cost_estimate=attention_cost(3, rows),
+        name="near_attention",
+    )(order, place, qa, qb, acc, top, *blocks)
+
+
+def far_attention(order, place, qa, qb, acc, top, blocks):
+    rows = qa.shape[0]
+    chunk = QUARTER + TAIL
+    part = lambda a: pl.BlockSpec((1,) + a.shape[1:], lambda i, *s: (i, 0, 0))
+    return pl.pallas_call(
+        far_kernel,
+        grid_spec=pltpu.PrefetchScalarGridSpec(
+            num_scalar_prefetch=2,
+            grid=(NH,),
+            in_specs=[whole(qa), whole(qb), part(acc), part(top)] + [whole(b) for b in blocks],
             out_specs=pl.BlockSpec((4, chunk, HD), lambda i, o, s: (i ^ s[0], 0, 0)),
             scratch_shapes=[
                 pltpu.VMEM((rows, HD), jnp.bfloat16),
@@ -339,9 +378,9 @@
             ],
         ),
         out_shape=jax.ShapeDtypeStruct((NH * 4, chunk, HD), jnp.bfloat16),
-        compiler_params=pltpu.CompilerParams(vmem_limit_bytes=24 * 2**20),
-        cost_estimate=attention_cost(3, rows),
-        name="other_attention",
+        compiler_params=pltpu.CompilerParams(vmem_limit_bytes=20 * 2**20),
+        cost_estimate=attention_cost(1, rows),
+        name="far_attention",
     )(order, place, qa, qb, acc, top, *blocks)
 
 
@@ -462,8 +501,10 @@
     q = triples[:, :HD]
     kv = triples[:, HD:]
 
-    others = tuple(move_x(kv, d) for d in (1, NX - 1, 2))
+    half = kv.shape[0] // 2
+    kv_up, kv_dn = move_x(kv, 1), move_x(kv, -1)
     q_hi = move_hi(q)
+    kv_far = (move_x(kv_up[:half], 1), move_x(kv_dn[half:], -1))
 
     matrix = latent_matrix(after(out_weight[0], mine_b), gate_row, latent_weight)
     part, acc, top = self_attention(place, q, kv, matrix)
@@ -473,8 +514,9 @@
     w_core, w_far = move_core(out_w), move_y(out_w)
     weights = (out_w, w_core, w_far, move_core(w_far))
 
+    acc, top = near_attention(span_order, place, q, q_hi, acc, top, (kv, kv_up, kv_dn))
     acc = after(acc, part)
-    chunks = other_attention(span_order, place, q, q_hi, acc, top, (kv, *others))
+    chunks = far_attention(span_order, place, q, q_hi, acc, top, kv_far)
     groups = [
         [
             span_at(i, hh) * seq_count + seq_at(yy, j, cc)

time: 166 us -> 177 us (1.066)
  the two profiles are of different devices: /device:TPU:10 before, /device:TPU:22 now
where the time goes in v2:
time: 177 us; the launch traced here: 175 us
  starting transfers between devices  57.5 us (32%)
  waiting for transfers between devices  49.6 us (28%)
  Pallas kernels  28.1 us (16%)
  local copies, waits for them, and re-layouts  18.3 us (10%)
  between operations  17.1 us (10%)
  other arithmetic  2.97 us (2%)
    unnamed x43, local copies, waits for them, and re-layouts  12.5 us
    all_to_all x1, waiting for transfers between devices, per_device(): lax.all_to_all(jnp.broadcast_to(latents, (seq_count,) + latents.shape[1:]...  11.6 us
    all_to_all x1, starting transfers between devices, per_device(): lax.all_to_all(jnp.broadcast_to(latents[None], (NX * NH,) + latents.shape...  11 us
    ppermute x9, starting transfers between devices, move_z(): return lax.ppermute(a, 'seq', seq_route(dz=d))  10.8 us
    ppermute x6, waiting for transfers between devices, move_y(): return lax.ppermute(a, 'seq', seq_route(dy=1))  10 us
    reduce_scatter x1, waiting for transfers between devices, per_device(): lax.psum_scatter(partial, 'seq', scatter_dimension=0, tiled=True, axis_in...  9.58 us
    ppermute x9, waiting for transfers between devices, move_z(): return lax.ppermute(a, 'seq', seq_route(dz=d))  9.48 us
    all_to_all x1, starting transfers between devices, per_device(): lax.all_to_all(jnp.broadcast_to(latents, (seq_count,) + latents.shape[1:]...  7.51 us
  transfers between devices with their start and end apart: 31, of which 12 were waited for; matrix products, arithmetic and copies ran while one was open for 5% of the time, Pallas kernels for 13%

profile of v2, /device:TPU:22, one launch (start us, length us, event | category | flops | bytes accessed | tf_op | source)
XLA Modules:
  0.0 174.6 jit_solution(14489556510383827641)
XLA Ops:
  7.9 2.0 %normalize.1 = (bf16[32,3072]{1,0:T(8,128)(2,1)}, f32[1,3072]{1,0:T(1,128)}) custom-call(s32[1]{0:T(128)S(6)} %copy.37.level_ref, bf16[32,3072]{1,0:T(8,128)(2,1)} %bitcast.48, f32[3,16,3072]{2,1,0:T(8,128)} %bitcast.49), custom_call_target="tpu_custom_call" | custom-call | tf_op jit(solution)/shard_map/normalize/pallas_call | solution.py:114
  10.0 1.9 %collective-permute-start.2 = (bf16[32,3072]{1,0:T(8,128)(2,1)}, bf16[32,3072]{1,0:T(8,128)(2,1)S(1)}, u32[]{:S(2)}, u32[]{:S(2)}) collective-permute-start(bf16[32,3072]{1,0:T(8,128)(2,1)} %get-tuple-element.17.refs_0_), channel_id=1, source_target_pairs={{0,2},{1,3},{2,4},{3,5},{4,6},{5,7},{6,8},{7,9},{8,10},{9,11},{10,... | collective-permute-start | bytes 589832 | tf_op jit(solution)/shard_map/ppermute | solution.py:48
  11.9 3.9 %collective-permute-start = (bf16[32,3072]{1,0:T(8,128)(2,1)}, bf16[32,3072]{1,0:T(8,128)(2,1)S(1)}, u32[]{:S(2)}, u32[]{:S(2)}) collective-permute-start(bf16[32,3072]{1,0:T(8,128)(2,1)} %get-tuple-element.17.refs_0_), channel_id=1, source_target_pairs={{0,14},{1,15},{2,0},{3,1},{4,2},{5,3},{6,4},{7,5},{8,6},{9,7},{10,... | collective-permute-start | bytes 589832 | tf_op jit(solution)/shard_map/ppermute | solution.py:48
  15.8 1.3 collective-permute-start.4
  17.1 4.5 %collective-permute-done.2.refs_4_ = bf16[32,3072]{1,0:T(8,128)(2,1)S(1)} collective-permute-done((bf16[32,3072]{1,0:T(8,128)(2,1)}, bf16[32,3072]{1,0:T(8,128)(2,1)S(1)}, u32[]{:S(2)}, u32[]{:S(2)}) %collective-permute-start.2) | collective-permute-done | bytes 196640 | tf_op jit(solution)/shard_map/ppermute | solution.py:48
  21.6 3.2 %collective-permute-start.1 = (bf16[32,3072]{1,0:T(8,128)(2,1)S(1)}, bf16[32,3072]{1,0:T(8,128)(2,1)S(1)}, u32[]{:S(2)}, u32[]{:S(2)}) collective-permute-start(bf16[32,3072]{1,0:T(8,128)(2,1)S(1)} %collective-permute-done.refs_1_), channel_id=1, source_target_pairs={{0,14},{1,15},{2,0},{3,1},{4,2},{5,3},{6,4},{7,5},{8,6},{9,7},{10,... | collective-permute-start | bytes 589832 | tf_op jit(solution)/shard_map/ppermute | solution.py:48
  24.8 1.3 collective-permute-start.5
  26.1 0.8 collective-permute-start.6
  26.9 2.7 %collective-permute-done.3.refs_3_ = bf16[32,3072]{1,0:T(8,128)(2,1)S(1)} collective-permute-done((bf16[32,3072]{1,0:T(8,128)(2,1)S(1)}, bf16[32,3072]{1,0:T(8,128)(2,1)S(1)}, u32[]{:S(2)}, u32[]{:S(2)}) %collective-permute-start.3) | collective-permute-done | bytes 196640 | tf_op jit(solution)/shard_map/ppermute | solution.py:48
  29.6 1.3 collective-permute-start.12
  30.8 1.9 %collective-permute-done.5.refs_6_ = bf16[32,3072]{1,0:T(8,128)(2,1)S(1)} collective-permute-done((bf16[32,3072]{1,0:T(8,128)(2,1)S(1)}, bf16[32,3072]{1,0:T(8,128)(2,1)S(1)}, u32[]{:S(2)}, u32[]{:S(2)}) %collective-permute-start.5) | collective-permute-done | bytes 196640 | tf_op jit(solution)/shard_map/ppermute | solution.py:52
  32.7 1.4 collective-permute-start.9
  34.1 2.8 %collective-permute-done.6.refs_7_ = bf16[32,3072]{1,0:T(8,128)(2,1)S(1)} collective-permute-done((bf16[32,3072]{1,0:T(8,128)(2,1)S(1)}, bf16[32,3072]{1,0:T(8,128)(2,1)S(1)}, u32[]{:S(2)}, u32[]{:S(2)}) %collective-permute-start.6) | collective-permute-done | bytes 196640 | tf_op jit(solution)/shard_map/ppermute | solution.py:52
  36.9 1.3 collective-permute-start.15
  38.2 2.9 %collective-permute-done.12.refs_3_ = bf16[32,3072]{1,0:T(8,128)(2,1)S(1)} collective-permute-done((bf16[32,3072]{1,0:T(8,128)(2,1)S(1)}, bf16[32,3072]{1,0:T(8,128)(2,1)S(1)}, u32[]{:S(2)}, u32[]{:S(2)}) %collective-permute-start.12) | collective-permute-done | bytes 196640 | tf_op jit(solution)/shard_map/ppermute | solution.py:52
  41.1 0.3 collective-permute-start.13
  41.4 1.9 %collective-permute-start.14 = (bf16[32,3072]{1,0:T(8,128)(2,1)S(1)}, bf16[32,3072]{1,0:T(8,128)(2,1)S(1)}, u32[]{:S(2)}, u32[]{:S(2)}) collective-permute-start(bf16[32,3072]{1,0:T(8,128)(2,1)S(1)} %collective-permute-done.9.refs_0_), channel_id=1, source_target_pairs={{0,30},{1,31},{2,16},{3,17},{4,18},{5,19},{6,20},{7,21},{8,22},{9,... | collective-permute-start | bytes 589832 | tf_op jit(solution)/shard_map/ppermute | solution.py:92
  43.4 2.4 %collective-permute-done.15.refs_7_ = bf16[32,3072]{1,0:T(8,128)(2,1)S(1)} collective-permute-done((bf16[32,3072]{1,0:T(8,128)(2,1)S(1)}, bf16[32,3072]{1,0:T(8,128)(2,1)S(1)}, u32[]{:S(2)}, u32[]{:S(2)}) %collective-permute-start.15) | collective-permute-done | bytes 196640 | tf_op jit(solution)/shard_map/ppermute | solution.py:52
  45.8 1.7 copy-done.1
  47.4 0.9 copy-done.5
  48.4 1.8 %project.2 = (bf16[256,384]{1,0:T(8,128)(2,1)S(1)}, bf16[256,384]{1,0:T(8,128)(2,1)S(1)}) custom-call(bf16[32,3072]{1,0:T(8,128)(2,1)S(1)} %copy-done.5, bf16[32,3072]{1,0:T(8,128)(2,1)S(1)} %collective-permute-done.refs_1_, bf16[32,3072]{1,0:T(8,128)(2,1)S(1)} %collective-permute-done.1.refs_2_, bf16[32,3072]{1,0:T(8,128)(2,1)S(1)} %collective-permute-done.3.refs_3_, ...), custom_call_target="tpu_custom_call" | custom-call | flops 1207959552 | bytes 6291456 | tf_op jit(solution)/shard_map/project/pallas_call | solution.py:170
  50.3 2.3 %collective-permute-done.16.refs_6_ = bf16[32,3072]{1,0:T(8,128)(2,1)S(1)} collective-permute-done((bf16[32,3072]{1,0:T(8,128)(2,1)S(1)}, bf16[32,3072]{1,0:T(8,128)(2,1)S(1)}, u32[]{:S(2)}, u32[]{:S(2)}) %collective-permute-start.16) | collective-permute-done | bytes 196640 | tf_op jit(solution)/shard_map/ppermute | solution.py:48
  52.6 1.8 %project.3 = (bf16[256,384]{1,0:T(8,128)(2,1)S(1)}, bf16[256,384]{1,0:T(8,128)(2,1)S(1)}) custom-call(bf16[32,3072]{1,0:T(8,128)(2,1)S(1)} %collective-permute-done.9.refs_0_, bf16[32,3072]{1,0:T(8,128)(2,1)S(1)} %collective-permute-done.11.refs_1_, bf16[32,3072]{1,0:T(8,128)(2,1)S(1)} %collective-permute-done.10.refs_2_, ...), custom_call_target="tpu_custom_call" | custom-call | flops 1207959552 | bytes 6291456 | tf_op jit(solution)/shard_map/project/pallas_call | solution.py:170
  54.6 1.4 collective-permute-start.24
  56.2 0.6 collective-permute-start.19
  56.7 1.5 collective-permute-start.20
  58.3 0.7 collective-permute-start.18
  59.2 0.6 latent_matrix.1.m_ref
  59.7 5.9 %self_attention.1 = (bf16[32,16,128]{2,1,0:T(8,128)(2,1)}, f32[1024,256]{1,0:T(8,128)S(1)}, f32[1024,128]{1,0:T(8,128)S(1)}) custom-call(s32[5]{0:T(128)S(1)} %stack.23.s_ref, bf16[1024,128]{1,0:T(8,128)(2,1)S(1)} %slice.185.q_ref.qa_ref, bf16[1024,256]{1,0:T(8,128)(2,1)S(1)} %slice.186.kv_ref.k0, bf16[256,64]{1,0:T(8,128)(2,1)S(1)} %latent_matrix.1.m_ref), custom_call_target="tpu_custom_call" | custom-call | flops 805306368 | bytes 1048576 | tf_op jit(solution)/shard_map/self_attention/pallas_call | solution.py:225
  65.6 1.0 copy-done.12
  66.7 0.8 copy-done.14
  67.4 7.1 %all-to-all-start = ((bf16[32,16,128]{2,1,0:T(8,128)(2,1)}), bf16[32,16,128]{2,1,0:T(8,128)(2,1)S(1)}, u32[]{:S(2)}, u32[]{:S(2)}) async-start(bf16[32,16,128]{2,1,0:T(8,128)(2,1)} %get-tuple-element.26), calls=%async_computation | async-start | bytes 262144 | tf_op jit(solution)/shard_map/all_to_all | solution.py:511
  74.5 1.7 slice.187
  76.2 1.7 collective-permute-start.21
  77.9 1.7 slice.188
  79.6 0.3 collective-permute-start.22
  79.9 0.7 collective-permute-done.18.qb_ref
  80.6 1.2 copy-done.13
  81.9 1.0 copy-done.15
  82.9 5.9 %near_attention.1 = (f32[2,1024,256]{2,1,0:T(8,128)S(1)}, f32[2,1024,128]{2,1,0:T(8,128)S(1)}) custom-call(s32[8]{0:T(128)S(1)} %copy-done.7, s32[5]{0:T(128)S(1)} %stack.23.s_ref, bf16[1024,128]{1,0:T(8,128)(2,1)S(1)} %slice.185.q_ref.qa_ref, bf16[1024,128]{1,0:T(8,128)(2,1)S(1)} %collective-permute-done.18.qb_ref, f32[1024,256]{1,0:T(8,128)S(1)} %copy-done.13, ...), custom_call_target="tpu_custom_call" | custom-call | flops 4831838208 | bytes 4194304 | tf_op jit(solution)/shard_map/near_attention/pallas_call | solution.py:340
  88.9 1.3 copy-done.8
  90.2 1.0 copy-done.10
  91.2 1.6 copy-done.9
  92.8 1.2 copy-done.11
  94.0 4.7 %far_attention.1 = bf16[8,272,128]{2,1,0:T(8,128)(2,1)} custom-call(s32[8]{0:T(128)S(1)} %copy-done.7, s32[5]{0:T(128)S(1)} %stack.23.s_ref, bf16[1024,128]{1,0:T(8,128)(2,1)S(1)} %slice.185.q_ref.qa_ref, bf16[1024,128]{1,0:T(8,128)(2,1)S(1)} %collective-permute-done.18.qb_ref, f32[2,1024,256]{2,1,0:T(8,128)S(1)} %copy-done.9, ...), custom_call_target="tpu_custom_call" | custom-call | flops 1610612736 | bytes 4194304 | tf_op jit(solution)/shard_map/far_attention/pallas_call | solution.py:366
  98.7 6.8 %all-to-all-start.1 = ((bf16[8,272,128]{2,1,0:T(8,128)(2,1)}), bf16[8,272,128]{2,1,0:T(8,128)(2,1)S(1)}, u32[]{:S(2)}, u32[]{:S(2)}) async-start(bf16[8,272,128]{2,1,0:T(8,128)(2,1)} %far_attention.1), calls=%async_computation.1 | async-start | bytes 1114112 | tf_op jit(solution)/shard_map/all_to_all | solution.py:530
  105.5 0.2 fusion.4
  105.7 7.3 %all-to-all-done.1.in_ref = bf16[8,272,128]{2,1,0:T(8,128)(2,1)S(1)} async-done(((bf16[8,272,128]{2,1,0:T(8,128)(2,1)}), bf16[8,272,128]{2,1,0:T(8,128)(2,1)S(1)}, u32[]{:S(2)}, u32[]{:S(2)}) %all-to-all-start.1) | async-done | bytes 557088 | tf_op jit(solution)/shard_map/all_to_all | solution.py:530
  113.0 5.4 %join_heads.1 = bf16[256,3072]{1,0:T(8,128)(2,1)} custom-call(s32[5]{0:T(128)S(1)} %stack.23.s_ref, bf16[8,272,128]{2,1,0:T(8,128)(2,1)S(1)} %all-to-all-done.1.in_ref, bf16[128,3072]{1,0:T(8,128)(2,1)S(1)} %bitcast.45, bf16[128,3072]{1,0:T(8,128)(2,1)} %collective-permute-done.23.w1_ref, bf16[128,3072]{1,0:T(8,128)(2,1)S(1)} %collective-permute-done.24.w2_ref, ...), custom_call_target="tpu_custom_call" | custom-call | tf_op jit(solution)/shard_map/join_heads/pallas_call | solution.py:425
  118.6 0.6 broadcast_in_dim.59
  119.2 11.0 %all-to-all-start.2 = ((bf16[8,16,128]{2,1,0:T(8,128)(2,1)}), bf16[8,16,128]{2,1,0:T(8,128)(2,1)S(1)}, u32[]{:S(2)}, u32[]{:S(2)}) async-start(bf16[8,16,128]{2,1,0:T(8,128)(2,1)} %broadcast_in_dim.59), calls=%async_computation.3 | async-start | bytes 65536 | tf_op jit(solution)/shard_map/all_to_all | solution.py:546
  130.2 0.6 fusion.3
  132.8 0.8 all-to-all-done.2
  133.6 0.7 broadcast_in_dim.61
  134.3 7.5 %all-to-all-start.3 = ((bf16[32,16,128]{2,1,0:T(8,128)(2,1)}), bf16[32,16,128]{2,1,0:T(8,128)(2,1)S(1)}, u32[]{:S(2)}, u32[]{:S(2)}) async-start(bf16[32,16,128]{2,1,0:T(8,128)(2,1)} %broadcast_in_dim.61), calls=%async_computation.4 | async-start | bytes 262144 | tf_op jit(solution)/shard_map/all_to_all | solution.py:550
  141.9 11.6 %all-to-all-done.3 = bf16[32,16,128]{2,1,0:T(8,128)(2,1)S(1)} async-done(((bf16[32,16,128]{2,1,0:T(8,128)(2,1)}), bf16[32,16,128]{2,1,0:T(8,128)(2,1)S(1)}, u32[]{:S(2)}, u32[]{:S(2)}) %all-to-all-start.3) | async-done | bytes 131104 | tf_op jit(solution)/shard_map/all_to_all | solution.py:550
  154.0 0.1 copy.21
  154.1 0.1 copy.29
  154.4 0.1 copy.19
  154.8 0.1 copy.17
  155.3 0.4 concatenate.31
  155.7 0.8 fusion
  156.5 9.6 %reduce-scatter.2.cloned.1.call-done = bf16[32,3072]{1,0:T(8,128)(2,1)} async-done(((bf16[256,3072]{1,0:T(8,128)(2,1)}), bf16[32,3072]{1,0:T(8,128)(2,1)}) %reduce-scatter.2.cloned.1.call-update) | async-done | bytes 196624 | tf_op jit(solution)/shard_map/reduce_scatter | solution.py:536
  166.1 1.7 fusion.1
  (84 shorter events, 2.1 us)
Async XLA Ops:
  7.2 148.5 %copy-start = (bf16[3,3,3,16,64]{4,3,2,1,0:T(8,128)(2,1)S(1)}, bf16[3,3,3,16,64]{4,3,2,1,0:T(8,128)(2,1)}, u32[]{:S(2)}) copy-start(bf16[3,3,3,16,64]{4,3,2,1,0:T(8,128)(2,1)} %param.15) | copy-start | bytes 165892
  7.2 38.6 %collective-permute-start.7 = (bf16[3072,384]{1,0:T(8,128)(2,1)}, bf16[3072,384]{1,0:T(8,128)(2,1)S(1)}, u32[]{:S(2)}, u32[]{:S(2)}) collective-permute-start(bf16[3072,384]{1,0:T(8,128)(2,1)} %bitcast.39), channel_id=1, source_target_pairs={{0,1},{1,0},{2,3},{3,2},{4,5},{5,4},{6,7},{7,6},{8,9},{9,8},{10,11... | collective-permute-start | bytes 7077896 | tf_op jit(solution)/shard_map/ppermute | solution.py:56
  10.0 11.6 %collective-permute-start.2 = (bf16[32,3072]{1,0:T(8,128)(2,1)}, bf16[32,3072]{1,0:T(8,128)(2,1)S(1)}, u32[]{:S(2)}, u32[]{:S(2)}) collective-permute-start(bf16[32,3072]{1,0:T(8,128)(2,1)} %get-tuple-element.17.refs_0_), channel_id=1, source_target_pairs={{0,2},{1,3},{2,4},{3,5},{4,6},{5,7},{6,8},{7,9},{8,10},{9,11},{10,... | collective-permute-start | bytes 589832 | tf_op jit(solution)/shard_map/ppermute | solution.py:48
  11.9 9.7 %collective-permute-start = (bf16[32,3072]{1,0:T(8,128)(2,1)}, bf16[32,3072]{1,0:T(8,128)(2,1)S(1)}, u32[]{:S(2)}, u32[]{:S(2)}) collective-permute-start(bf16[32,3072]{1,0:T(8,128)(2,1)} %get-tuple-element.17.refs_0_), channel_id=1, source_target_pairs={{0,14},{1,15},{2,0},{3,1},{4,2},{5,3},{6,4},{7,5},{8,6},{9,7},{10,... | collective-permute-start | bytes 589832 | tf_op jit(solution)/shard_map/ppermute | solution.py:48
  15.8 10.3 %collective-permute-start.4 = (bf16[32,3072]{1,0:T(8,128)(2,1)}, bf16[32,3072]{1,0:T(8,128)(2,1)S(1)}, u32[]{:S(2)}, u32[]{:S(2)}) collective-permute-start(bf16[32,3072]{1,0:T(8,128)(2,1)} %get-tuple-element.17.refs_0_), channel_id=1, source_target_pairs={{0,16},{1,17},{2,18},{3,19},{4,20},{5,21},{6,22},{7,23},{8,24},{9,... | collective-permute-start | bytes 589832 | tf_op jit(solution)/shard_map/ppermute | solution.py:52
  21.6 7.9 %collective-permute-start.3 = (bf16[32,3072]{1,0:T(8,128)(2,1)S(1)}, bf16[32,3072]{1,0:T(8,128)(2,1)S(1)}, u32[]{:S(2)}, u32[]{:S(2)}) collective-permute-start(bf16[32,3072]{1,0:T(8,128)(2,1)S(1)} %collective-permute-done.2.refs_4_), channel_id=1, source_target_pairs={{0,2},{1,3},{2,4},{3,5},{4,6},{5,7},{6,8},{7,9},{8,10},{9,11},{10,... | collective-permute-start | bytes 589832 | tf_op jit(solution)/shard_map/ppermute | solution.py:48
  21.6 7.9 %collective-permute-start.1 = (bf16[32,3072]{1,0:T(8,128)(2,1)S(1)}, bf16[32,3072]{1,0:T(8,128)(2,1)S(1)}, u32[]{:S(2)}, u32[]{:S(2)}) collective-permute-start(bf16[32,3072]{1,0:T(8,128)(2,1)S(1)} %collective-permute-done.refs_1_), channel_id=1, source_target_pairs={{0,14},{1,15},{2,0},{3,1},{4,2},{5,3},{6,4},{7,5},{8,6},{9,7},{10,... | collective-permute-start | bytes 589832 | tf_op jit(solution)/shard_map/ppermute | solution.py:48
  24.8 7.9 %collective-permute-start.5 = (bf16[32,3072]{1,0:T(8,128)(2,1)S(1)}, bf16[32,3072]{1,0:T(8,128)(2,1)S(1)}, u32[]{:S(2)}, u32[]{:S(2)}) collective-permute-start(bf16[32,3072]{1,0:T(8,128)(2,1)S(1)} %collective-permute-done.refs_1_), channel_id=1, source_target_pairs={{0,16},{1,17},{2,18},{3,19},{4,20},{5,21},{6,22},{7,23},{8,24},{9,... | collective-permute-start | bytes 589832 | tf_op jit(solution)/shard_map/ppermute | solution.py:52
  26.1 10.8 %collective-permute-start.6 = (bf16[32,3072]{1,0:T(8,128)(2,1)S(1)}, bf16[32,3072]{1,0:T(8,128)(2,1)S(1)}, u32[]{:S(2)}, u32[]{:S(2)}) collective-permute-start(bf16[32,3072]{1,0:T(8,128)(2,1)S(1)} %collective-permute-done.2.refs_4_), channel_id=1, source_target_pairs={{0,16},{1,17},{2,18},{3,19},{4,20},{5,21},{6,22},{7,23},{8,24},{9,... | collective-permute-start | bytes 589832 | tf_op jit(solution)/shard_map/ppermute | solution.py:52
  29.5 8.6 %collective-permute-start.10 = (bf16[32,3072]{1,0:T(8,128)(2,1)S(1)}, bf16[32,3072]{1,0:T(8,128)(2,1)S(1)}, u32[]{:S(2)}, u32[]{:S(2)}) collective-permute-start(bf16[32,3072]{1,0:T(8,128)(2,1)S(1)} %collective-permute-done.3.refs_3_), channel_id=1, source_target_pairs={{0,2},{1,3},{2,4},{3,5},{4,6},{5,7},{6,8},{7,9},{8,10},{9,11},{10,... | collective-permute-start | bytes 589832 | tf_op jit(solution)/shard_map/ppermute | solution.py:48
  29.6 11.6 %collective-permute-start.12 = (bf16[32,3072]{1,0:T(8,128)(2,1)S(1)}, bf16[32,3072]{1,0:T(8,128)(2,1)S(1)}, u32[]{:S(2)}, u32[]{:S(2)}) collective-permute-start(bf16[32,3072]{1,0:T(8,128)(2,1)S(1)} %collective-permute-done.1.refs_2_), channel_id=1, source_target_pairs={{0,16},{1,17},{2,18},{3,19},{4,20},{5,21},{6,22},{7,23},{8,24},{9,... | collective-permute-start | bytes 589832 | tf_op jit(solution)/shard_map/ppermute | solution.py:52
  32.7 8.7 %collective-permute-start.9 = (bf16[32,3072]{1,0:T(8,128)(2,1)S(1)}, bf16[32,3072]{1,0:T(8,128)(2,1)S(1)}, u32[]{:S(2)}, u32[]{:S(2)}) collective-permute-start(bf16[32,3072]{1,0:T(8,128)(2,1)S(1)} %collective-permute-done.1.refs_2_), channel_id=1, source_target_pairs={{0,14},{1,15},{2,0},{3,1},{4,2},{5,3},{6,4},{7,5},{8,6},{9,7},{10,... | collective-permute-start | bytes 589832 | tf_op jit(solution)/shard_map/ppermute | solution.py:48
  36.9 8.8 %collective-permute-start.15 = (bf16[32,3072]{1,0:T(8,128)(2,1)S(1)}, bf16[32,3072]{1,0:T(8,128)(2,1)S(1)}, u32[]{:S(2)}, u32[]{:S(2)}) collective-permute-start(bf16[32,3072]{1,0:T(8,128)(2,1)S(1)} %collective-permute-done.3.refs_3_), channel_id=1, source_target_pairs={{0,16},{1,17},{2,18},{3,19},{4,20},{5,21},{6,22},{7,23},{8,24},{9,... | collective-permute-start | bytes 589832 | tf_op jit(solution)/shard_map/ppermute | solution.py:52
  38.2 12.1 %collective-permute-start.11 = (bf16[32,3072]{1,0:T(8,128)(2,1)S(1)}, bf16[32,3072]{1,0:T(8,128)(2,1)S(1)}, u32[]{:S(2)}, u32[]{:S(2)}) collective-permute-start(bf16[32,3072]{1,0:T(8,128)(2,1)S(1)} %collective-permute-done.10.refs_2_), channel_id=1, source_target_pairs={{0,2},{1,3},{2,4},{3,5},{4,6},{5,7},{6,8},{7,9},{8,10},{9,11},{10,... | collective-permute-start | bytes 589832 | tf_op jit(solution)/shard_map/ppermute | solution.py:48
  41.1 9.2 %collective-permute-start.13 = (bf16[32,3072]{1,0:T(8,128)(2,1)S(1)}, bf16[32,3072]{1,0:T(8,128)(2,1)S(1)}, u32[]{:S(2)}, u32[]{:S(2)}) collective-permute-start(bf16[32,3072]{1,0:T(8,128)(2,1)S(1)} %collective-permute-done.12.refs_3_), channel_id=1, source_target_pairs={{0,14},{1,15},{2,0},{3,1},{4,2},{5,3},{6,4},{7,5},{8,6},{9,7},{10,... | collective-permute-start | bytes 589832 | tf_op jit(solution)/shard_map/ppermute | solution.py:48
  41.4 8.9 %collective-permute-start.14 = (bf16[32,3072]{1,0:T(8,128)(2,1)S(1)}, bf16[32,3072]{1,0:T(8,128)(2,1)S(1)}, u32[]{:S(2)}, u32[]{:S(2)}) collective-permute-start(bf16[32,3072]{1,0:T(8,128)(2,1)S(1)} %collective-permute-done.9.refs_0_), channel_id=1, source_target_pairs={{0,30},{1,31},{2,16},{3,17},{4,18},{5,19},{6,20},{7,21},{8,22},{9,... | collective-permute-start | bytes 589832 | tf_op jit(solution)/shard_map/ppermute | solution.py:92
  45.8 6.9 %collective-permute-start.16 = (bf16[32,3072]{1,0:T(8,128)(2,1)S(1)}, bf16[32,3072]{1,0:T(8,128)(2,1)S(1)}, u32[]{:S(2)}, u32[]{:S(2)}) collective-permute-start(bf16[32,3072]{1,0:T(8,128)(2,1)S(1)} %collective-permute-done.15.refs_7_), channel_id=1, source_target_pairs={{0,2},{1,3},{2,4},{3,5},{4,6},{5,7},{6,8},{7,9},{8,10},{9,11},{10,... | collective-permute-start | bytes 589832 | tf_op jit(solution)/shard_map/ppermute | solution.py:48
  45.8 1.7 copy-start.1
  47.4 0.9 copy-start.5
  48.4 4.3 %copy-start.2 = (bf16[1,3072,384]{2,1,0:T(8,128)(2,1)S(1)}, bf16[1,3072,384]{2,1,0:T(8,128)(2,1)}, u32[]{:S(2)}) copy-start(bf16[1,3072,384]{2,1,0:T(8,128)(2,1)} %param.12) | copy-start | bytes 7077892
  50.2 4.4 %copy-start.3 = (bf16[1,128,3072]{2,1,0:T(8,128)(2,1)S(1)}, bf16[1,128,3072]{2,1,0:T(8,128)(2,1)}, u32[]{:S(2)}) copy-start(bf16[1,128,3072]{2,1,0:T(8,128)(2,1)} %param.13) | copy-start | bytes 2359300
  50.2 5.8 %collective-permute-start.8 = (bf16[256,384]{1,0:T(8,128)(2,1)S(1)}, bf16[256,384]{1,0:T(8,128)(2,1)S(1)}, u32[]{:S(2)}, u32[]{:S(2)}) collective-permute-start(bf16[256,384]{1,0:T(8,128)(2,1)S(1)} %get-tuple-element.19), channel_id=1, source_target_pairs={{0,1},{1,0},{2,3},{3,2},{4,5},{5,4},{6,7},{7,6},{8,9},{9,8},{10,11... | collective-permute-start | bytes 589832 | tf_op jit(solution)/shard_map/ppermute | solution.py:56
  54.5 4.7 %copy-start.4 = (bf16[3072,64]{0,1:T(8,128)(2,1)S(1)}, bf16[3072,64]{0,1:T(8,128)(2,1)}, u32[]{:S(2)}) copy-start(bf16[3072,64]{0,1:T(8,128)(2,1)} %param.14) | copy-start | bytes 1179652
  54.5 4.7 %copy-start.6 = (f32[1,3072]{1,0:T(1,128)S(1)}, f32[1,3072]{1,0:T(1,128)}, u32[]{:S(2)}) copy-start(f32[1,3072]{1,0:T(1,128)} %get-tuple-element.16.gate_ref) | copy-start | bytes 36868
  54.5 1.6 collective-permute-start.17
  54.6 25.3 %collective-permute-start.24 = (bf16[128,3072]{1,0:T(8,128)(2,1)S(1)}, bf16[128,3072]{1,0:T(8,128)(2,1)S(1)}, u32[]{:S(2)}, u32[]{:S(2)}) collective-permute-start(bf16[128,3072]{1,0:T(8,128)(2,1)S(1)} %bitcast.42), channel_id=1, source_target_pairs={{0,16},{1,17},{2,18},{3,19},{4,20},{5,21},{6,22},{7,23},{8,24},{9,... | collective-permute-start | bytes 2359304 | tf_op jit(solution)/shard_map/ppermute | solution.py:52
  56.2 18.4 %collective-permute-start.19 = (bf16[1024,256]{1,0:T(8,128)(2,1)S(1)}, bf16[1024,256]{1,0:T(8,128)(2,1)}, u32[]{:S(2)}, u32[]{:S(2)}) collective-permute-start(bf16[1024,256]{1,0:T(8,128)(2,1)S(1)} %slice.186.kv_ref.k0), channel_id=1, source_target_pairs={{0,64},{32,96},{64,128},{96,160},{128,192},{160,224},{192,0},{224,... | collective-permute-start | bytes 1572872 | tf_op jit(solution)/shard_map/ppermute | solution.py:60
  56.7 21.2 %collective-permute-start.20 = (bf16[1024,256]{1,0:T(8,128)(2,1)S(1)}, bf16[1024,256]{1,0:T(8,128)(2,1)}, u32[]{:S(2)}, u32[]{:S(2)}) collective-permute-start(bf16[1024,256]{1,0:T(8,128)(2,1)S(1)} %slice.186.kv_ref.k0), channel_id=1, source_target_pairs={{0,192},{32,224},{64,0},{96,32},{128,64},{160,96},{192,128},{224,1... | collective-permute-start | bytes 1572872 | tf_op jit(solution)/shard_map/ppermute | solution.py:60
  58.3 22.3 %collective-permute-start.18 = (bf16[1024,128]{1,0:T(8,128)(2,1)S(1)}, bf16[1024,128]{1,0:T(8,128)(2,1)S(1)}, u32[]{:S(2)}, u32[]{:S(2)}) collective-permute-start(bf16[1024,128]{1,0:T(8,128)(2,1)S(1)} %slice.185.q_ref.qa_ref), channel_id=1, source_target_pairs={{0,32},{32,0},{64,96},{96,64},{128,160},{160,128},{192,224},{224,1... | collective-permute-start | bytes 786440 | tf_op jit(solution)/shard_map/ppermute | solution.py:64
  59.1 46.6 %collective-permute-start.23 = (bf16[128,3072]{1,0:T(8,128)(2,1)S(1)}, bf16[128,3072]{1,0:T(8,128)(2,1)}, u32[]{:S(2)}, u32[]{:S(2)}) collective-permute-start(bf16[128,3072]{1,0:T(8,128)(2,1)S(1)} %bitcast.43), channel_id=1, source_target_pairs={{0,1},{1,0},{2,3},{3,2},{4,5},{5,4},{6,7},{7,6},{8,9},{9,8},{10,11... | collective-permute-start | bytes 2359304 | tf_op jit(solution)/shard_map/ppermute | solution.py:56
  59.7 20.9 %copy-start.7 = (s32[8]{0:T(128)S(1)}, s32[8]{0:T(128)}, u32[]{:S(2)}) copy-start(s32[8]{0:T(128)} %order_ref.3) | copy-start | bytes 100
  65.6 1.0 copy-start.12
  66.7 0.8 copy-start.14
  67.4 23.7 %all-to-all-start = ((bf16[32,16,128]{2,1,0:T(8,128)(2,1)}), bf16[32,16,128]{2,1,0:T(8,128)(2,1)S(1)}, u32[]{:S(2)}, u32[]{:S(2)}) async-start(bf16[32,16,128]{2,1,0:T(8,128)(2,1)} %get-tuple-element.26), calls=%async_computation | async-start | bytes 262144 | tf_op jit(solution)/shard_map/all_to_all | solution.py:511
  76.2 15.0 %collective-permute-start.21 = (bf16[512,256]{1,0:T(8,128)(2,1)}, bf16[512,256]{1,0:T(8,128)(2,1)S(1)}, u32[]{:S(2)}, u32[]{:S(2)}) collective-permute-start(bf16[512,256]{1,0:T(8,128)(2,1)} %slice.187), channel_id=1, source_target_pairs={{0,64},{32,96},{64,128},{96,160},{128,192},{160,224},{192,0},{224,... | collective-permute-start | bytes 786440 | tf_op jit(solution)/shard_map/ppermute | solution.py:60
  79.6 11.6 %collective-permute-start.22 = (bf16[512,256]{1,0:T(8,128)(2,1)}, bf16[512,256]{1,0:T(8,128)(2,1)}, u32[]{:S(2)}, u32[]{:S(2)}) collective-permute-start(bf16[512,256]{1,0:T(8,128)(2,1)} %slice.188), channel_id=1, source_target_pairs={{0,192},{32,224},{64,0},{96,32},{128,64},{160,96},{192,128},{224,1... | collective-permute-start | bytes 786440 | tf_op jit(solution)/shard_map/ppermute | solution.py:60
  79.9 33.1 %collective-permute-start.25 = (bf16[128,3072]{1,0:T(8,128)(2,1)S(1)}, bf16[128,3072]{1,0:T(8,128)(2,1)}, u32[]{:S(2)}, u32[]{:S(2)}) collective-permute-start(bf16[128,3072]{1,0:T(8,128)(2,1)S(1)} %collective-permute-done.24.w2_ref), channel_id=1, source_target_pairs={{0,1},{1,0},{2,3},{3,2},{4,5},{5,4},{6,7},{7,6},{8,9},{9,8},{10,11... | collective-permute-start | bytes 2359304 | tf_op jit(solution)/shard_map/ppermute | solution.py:56
  80.6 1.2 copy-start.13
  81.9 1.0 copy-start.15
  88.8 1.3 copy-start.8
  90.2 1.0 copy-start.10
  91.2 1.6 copy-start.9
  92.8 1.2 copy-start.11
  94.0 11.5 %copy-start.16 = (bf16[1,32,3072]{2,1,0:T(8,128)(2,1)S(1)}, bf16[1,32,3072]{2,1,0:T(8,128)(2,1)}, u32[]{:S(2)}) copy-start(bf16[1,32,3072]{2,1,0:T(8,128)(2,1)} %param.8) | copy-start | bytes 589828
  98.7 14.3 %all-to-all-start.1 = ((bf16[8,272,128]{2,1,0:T(8,128)(2,1)}), bf16[8,272,128]{2,1,0:T(8,128)(2,1)S(1)}, u32[]{:S(2)}, u32[]{:S(2)}) async-start(bf16[8,272,128]{2,1,0:T(8,128)(2,1)} %far_attention.1), calls=%async_computation.1 | async-start | bytes 1114112 | tf_op jit(solution)/shard_map/all_to_all | solution.py:530
  105.5 60.6 %reduce-scatter.2.cloned.1.call-start = ((), (), s32[]{:S(2)}) async-start(), calls=%async_computation.5 | async-start | bytes 1769472 | tf_op jit(solution)/shard_map/reduce_scatter | solution.py:536
  119.2 14.4 %all-to-all-start.2 = ((bf16[8,16,128]{2,1,0:T(8,128)(2,1)}), bf16[8,16,128]{2,1,0:T(8,128)(2,1)S(1)}, u32[]{:S(2)}, u32[]{:S(2)}) async-start(bf16[8,16,128]{2,1,0:T(8,128)(2,1)} %broadcast_in_dim.59), calls=%async_computation.3 | async-start | bytes 65536 | tf_op jit(solution)/shard_map/all_to_all | solution.py:546
  134.3 19.3 %all-to-all-start.3 = ((bf16[32,16,128]{2,1,0:T(8,128)(2,1)}), bf16[32,16,128]{2,1,0:T(8,128)(2,1)S(1)}, u32[]{:S(2)}, u32[]{:S(2)}) async-start(bf16[32,16,128]{2,1,0:T(8,128)(2,1)} %broadcast_in_dim.61), calls=%async_computation.4 | async-start | bytes 262144 | tf_op jit(solution)/shard_map/all_to_all | solution.py:550
Sparse Core Ops, SparseCore 0:
  118.5 47.5 reduce-scatter.1

commit v3 on v1

--- a/solution.py
+++ b/solution.py
@@ -154,13 +154,15 @@
 
 
 def project_kernel(*refs):
-    blocks, (own_ref, oth_ref, mine_ref, theirs_ref, rows) = refs[:NZ], refs[NZ:]
+    blocks, (own_ref, oth_ref, q_ref, kv_ref, theirs_ref, rows) = refs[:NZ], refs[NZ:]
     for i, block in enumerate(blocks):
         rows[i * BLK : i * BLK + BLK, :] = block[...]
-    for w_ref, o_ref in ((oth_ref, theirs_ref), (own_ref, mine_ref)):
-        out = jnp.dot(rows[...], w_ref[...], preferred_element_type=jnp.float32)
-        o_ref[:, :HD] = (out[:, :HD] * EXP_SCALE).astype(jnp.bfloat16)
-        o_ref[:, HD:] = out[:, HD:].astype(jnp.bfloat16)
+    out = jnp.dot(rows[...], oth_ref[...], preferred_element_type=jnp.float32)
+    theirs_ref[:, :HD] = (out[:, :HD] * EXP_SCALE).astype(jnp.bfloat16)
+    theirs_ref[:, HD:] = out[:, HD:].astype(jnp.bfloat16)
+    out = jnp.dot(rows[...], own_ref[...], preferred_element_type=jnp.float32)
+    q_ref[...] = (out[:, :HD] * EXP_SCALE).astype(jnp.bfloat16)
+    kv_ref[...] = out[:, HD:].astype(jnp.bfloat16)
 
 
 def project(blocks, w_own, w_oth):
@@ -170,8 +172,8 @@
     return pl.pallas_call(
         project_kernel,
         in_specs=[vmem] * (len(blocks) + 2),
-        out_specs=[vmem, vmem],
-        out_shape=[jax.ShapeDtypeStruct((rows, cols), jnp.bfloat16)] * 2,
+        out_specs=[vmem, vmem, vmem],
+        out_shape=[jax.ShapeDtypeStruct((rows, n), jnp.bfloat16) for n in (HD, 2 * HD, cols)],
         scratch_shapes=[pltpu.VMEM((rows, width), jnp.bfloat16)],
         compiler_params=pltpu.CompilerParams(vmem_limit_bytes=16 * 2**20),
         cost_estimate=pl.CostEstimate(
@@ -456,20 +458,20 @@
     w_own = in_weight[0]
     own_blocks, other_blocks = gather_class(normed)
     w_oth = move_core(w_own)
-    mine_a, theirs_a = project(own_blocks, w_own, w_oth)
-    mine_b, theirs_b = project(other_blocks, w_own, w_oth)
-    triples = jnp.concatenate([mine_a, move_core(theirs_a), mine_b, move_core(theirs_b)], axis=0)
-    q = triples[:, :HD]
-    kv = triples[:, HD:]
+    q_a, kv_a, theirs_a = project(own_blocks, w_own, w_oth)
+    q_b, kv_b, theirs_b = project(other_blocks, w_own, w_oth)
+    theirs_a, theirs_b = move_core(theirs_a), move_core(theirs_b)
+    q = jnp.concatenate([q_a, theirs_a[:, :HD], q_b, theirs_b[:, :HD]], axis=0)
+    kv = jnp.concatenate([kv_a, theirs_a[:, HD:], kv_b, theirs_b[:, HD:]], axis=0)
 
     others = tuple(move_x(kv, d) for d in (1, NX - 1, 2))
     q_hi = move_hi(q)
 
-    matrix = latent_matrix(after(out_weight[0], mine_b), gate_row, latent_weight)
+    matrix = latent_matrix(after(out_weight[0], q_b), gate_row, latent_weight)
     part, acc, top = self_attention(place, q, kv, matrix)
     part = lax.all_to_all(part, "seq", 0, 0, tiled=True)
 
-    out_w = after(out_weight[0], mine_b)
+    out_w = after(out_weight[0], q_b)
     w_core, w_far = move_core(out_w), move_y(out_w)
     weights = (out_w, w_core, w_far, move_core(w_far))
 

time: 166 us -> 171 us (1.030)
  starting transfers between devices: 38.5 us -> 45.1 us
  waiting for transfers between devices: 54.5 us -> 51.7 us
    ppermute x9, starting transfers between devices: 9.66 us -> 17.3 us  [move_z(): return lax.ppermute(a, 'seq', seq_route(dz=d))]
    ppermute x6, waiting for transfers between devices: 13.3 us -> 7.5 us  [move_y(): return lax.ppermute(a, 'seq', seq_route(dy=1))]
    ppermute x9, waiting for transfers between devices: 10.3 us -> 15 us  [move_z(): return lax.ppermute(a, 'seq', seq_route(dz=d))]
    unnamed x29 -> x30, local copies, waits for them, and re-layouts: 3.34 us -> 4.01 us
  transfers between devices with their start and end apart: 29 -> 29, of which waited for: 12 -> 15; matrix products, arithmetic and copies ran while one was open for 4% -> 4% of each run, Pallas kernels for 13% -> 14%
where the time goes in v3:
time: 171 us; the launch traced here: 170 us
  waiting for transfers between devices  51.7 us (30%)
  starting transfers between devices  45.1 us (26%)
  Pallas kernels  28.8 us (17%)
  between operations  17 us (10%)
  blocking collectives  15.3 us (9%)
  local copies, waits for them, and re-layouts  7.18 us (4%)
  other arithmetic  3.01 us (2%)
  matrix products  1.95 us (1%)
    ppermute x9, starting transfers between devices, move_z(): return lax.ppermute(a, 'seq', seq_route(dz=d))  17.3 us
    all_to_all x1, blocking collectives, per_device(): part = lax.all_to_all(part, 'seq', 0, 0, tiled=True)  15.3 us
    ppermute x9, waiting for transfers between devices, move_z(): return lax.ppermute(a, 'seq', seq_route(dz=d))  15 us
    pallas_call x1, Pallas kernels, other_attention(): pl.pallas_call(other_kernel, grid_spec=pltpu.PrefetchScalarGridSpec(num_s...  12 us
    all_to_all x1, waiting for transfers between devices, per_device(): lax.all_to_all(jnp.broadcast_to(latents, (seq_count,) + latents.shape[1:]...  9.19 us
    all_to_all x1, waiting for transfers between devices, per_device(): lax.all_to_all(chunks, ('span', 'seq'), 0, 0, tiled=True, axis_index_grou...  8.09 us
    ppermute x6, waiting for transfers between devices, move_y(): return lax.ppermute(a, 'seq', seq_route(dy=1))  7.5 us
    reduce_scatter x1, waiting for transfers between devices, per_device(): lax.psum_scatter(partial, 'seq', scatter_dimension=0, tiled=True, axis_in...  6.94 us
  transfers between devices with their start and end apart: 29, of which 15 were waited for; matrix products, arithmetic and copies ran while one was open for 4% of the time, Pallas kernels for 14%

profile of v3, /device:TPU:10, one launch (start us, length us, event | category | flops | bytes accessed | tf_op | source)
XLA Modules:
  0.0 170.1 jit_solution(7925697949404061028)
XLA Ops:
  7.9 2.0 %normalize.1 = (bf16[32,3072]{1,0:T(8,128)(2,1)}, f32[1,3072]{1,0:T(1,128)}) custom-call(s32[1]{0:T(128)S(6)} %copy.34.level_ref, bf16[32,3072]{1,0:T(8,128)(2,1)} %bitcast.48, f32[3,16,3072]{2,1,0:T(8,128)} %bitcast.49), custom_call_target="tpu_custom_call" | custom-call | tf_op jit(solution)/shard_map/normalize/pallas_call | solution.py:114
  10.0 1.9 %collective-permute-start.2 = (bf16[32,3072]{1,0:T(8,128)(2,1)}, bf16[32,3072]{1,0:T(8,128)(2,1)S(1)}, u32[]{:S(2)}, u32[]{:S(2)}) collective-permute-start(bf16[32,3072]{1,0:T(8,128)(2,1)} %get-tuple-element.17.refs_0_), channel_id=1, source_target_pairs={{0,2},{1,3},{2,4},{3,5},{4,6},{5,7},{6,8},{7,9},{8,10},{9,11},{10,... | collective-permute-start | bytes 589832 | tf_op jit(solution)/shard_map/ppermute | solution.py:48
  11.9 3.9 %collective-permute-start = (bf16[32,3072]{1,0:T(8,128)(2,1)}, bf16[32,3072]{1,0:T(8,128)(2,1)S(1)}, u32[]{:S(2)}, u32[]{:S(2)}) collective-permute-start(bf16[32,3072]{1,0:T(8,128)(2,1)} %get-tuple-element.17.refs_0_), channel_id=1, source_target_pairs={{0,14},{1,15},{2,0},{3,1},{4,2},{5,3},{6,4},{7,5},{8,6},{9,7},{10,... | collective-permute-start | bytes 589832 | tf_op jit(solution)/shard_map/ppermute | solution.py:48
  15.8 5.8 %collective-permute-done.2.refs_4_ = bf16[32,3072]{1,0:T(8,128)(2,1)S(1)} collective-permute-done((bf16[32,3072]{1,0:T(8,128)(2,1)}, bf16[32,3072]{1,0:T(8,128)(2,1)S(1)}, u32[]{:S(2)}, u32[]{:S(2)}) %collective-permute-start.2) | collective-permute-done | bytes 196640 | tf_op jit(solution)/shard_map/ppermute | solution.py:48
  21.6 3.2 %collective-permute-start.1 = (bf16[32,3072]{1,0:T(8,128)(2,1)S(1)}, bf16[32,3072]{1,0:T(8,128)(2,1)S(1)}, u32[]{:S(2)}, u32[]{:S(2)}) collective-permute-start(bf16[32,3072]{1,0:T(8,128)(2,1)S(1)} %collective-permute-done.refs_1_), channel_id=1, source_target_pairs={{0,14},{1,15},{2,0},{3,1},{4,2},{5,3},{6,4},{7,5},{8,6},{9,7},{10,... | collective-permute-start | bytes 589832 | tf_op jit(solution)/shard_map/ppermute | solution.py:48
  24.8 4.7 %collective-permute-done.3.refs_3_ = bf16[32,3072]{1,0:T(8,128)(2,1)S(1)} collective-permute-done((bf16[32,3072]{1,0:T(8,128)(2,1)S(1)}, bf16[32,3072]{1,0:T(8,128)(2,1)S(1)}, u32[]{:S(2)}, u32[]{:S(2)}) %collective-permute-start.3) | collective-permute-done | bytes 196640 | tf_op jit(solution)/shard_map/ppermute | solution.py:48
  29.6 0.5 collective-permute-start.12
  30.0 3.2 %collective-permute-start.9 = (bf16[32,3072]{1,0:T(8,128)(2,1)S(1)}, bf16[32,3072]{1,0:T(8,128)(2,1)S(1)}, u32[]{:S(2)}, u32[]{:S(2)}) collective-permute-start(bf16[32,3072]{1,0:T(8,128)(2,1)S(1)} %collective-permute-done.1.refs_2_), channel_id=1, source_target_pairs={{0,14},{1,15},{2,0},{3,1},{4,2},{5,3},{6,4},{7,5},{8,6},{9,7},{10,... | collective-permute-start | bytes 589832 | tf_op jit(solution)/shard_map/ppermute | solution.py:48
  33.2 1.6 collective-permute-start.15
  34.8 1.8 %collective-permute-done.10.refs_2_ = bf16[32,3072]{1,0:T(8,128)(2,1)S(1)} collective-permute-done((bf16[32,3072]{1,0:T(8,128)(2,1)S(1)}, bf16[32,3072]{1,0:T(8,128)(2,1)S(1)}, u32[]{:S(2)}, u32[]{:S(2)}) %collective-permute-start.10) | collective-permute-done | bytes 196640 | tf_op jit(solution)/shard_map/ppermute | solution.py:48
  36.6 0.2 collective-permute-done.12.refs_3_
  36.8 3.7 %collective-permute-start.13 = (bf16[32,3072]{1,0:T(8,128)(2,1)S(1)}, bf16[32,3072]{1,0:T(8,128)(2,1)S(1)}, u32[]{:S(2)}, u32[]{:S(2)}) collective-permute-start(bf16[32,3072]{1,0:T(8,128)(2,1)S(1)} %collective-permute-done.12.refs_3_), channel_id=1, source_target_pairs={{0,14},{1,15},{2,0},{3,1},{4,2},{5,3},{6,4},{7,5},{8,6},{9,7},{10,... | collective-permute-start | bytes 589832 | tf_op jit(solution)/shard_map/ppermute | solution.py:48
  40.5 0.6 collective-permute-start.14
  41.1 1.3 collective-permute-start.16
  42.4 2.5 %collective-permute-done.11.refs_1_ = bf16[32,3072]{1,0:T(8,128)(2,1)S(1)} collective-permute-done((bf16[32,3072]{1,0:T(8,128)(2,1)S(1)}, bf16[32,3072]{1,0:T(8,128)(2,1)S(1)}, u32[]{:S(2)}, u32[]{:S(2)}) %collective-permute-start.11) | collective-permute-done | bytes 196640 | tf_op jit(solution)/shard_map/ppermute | solution.py:48
  44.9 0.2 collective-permute-start.4
  45.1 1.9 %collective-permute-start.5 = (bf16[32,3072]{1,0:T(8,128)(2,1)S(1)}, bf16[32,3072]{1,0:T(8,128)(2,1)S(1)}, u32[]{:S(2)}, u32[]{:S(2)}) collective-permute-start(bf16[32,3072]{1,0:T(8,128)(2,1)S(1)} %collective-permute-done.refs_1_), channel_id=1, source_target_pairs={{0,16},{1,17},{2,18},{3,19},{4,20},{5,21},{6,22},{7,23},{8,24},{9,... | collective-permute-start | bytes 589832 | tf_op jit(solution)/shard_map/ppermute | solution.py:52
  47.0 0.2 collective-permute-done.14.refs_5_
  47.2 0.7 collective-permute-start.6
  47.8 0.2 collective-permute-done.16.refs_6_
  48.0 1.7 copy-done.1
  49.7 1.8 %project.3 = (bf16[256,128]{1,0:T(8,128)(2,1)S(1)}, bf16[256,256]{1,0:T(8,128)(2,1)S(1)}, bf16[256,384]{1,0:T(8,128)(2,1)S(1)}) custom-call(bf16[32,3072]{1,0:T(8,128)(2,1)S(1)} %collective-permute-done.9.refs_0_, bf16[32,3072]{1,0:T(8,128)(2,1)S(1)} %collective-permute-done.11.refs_1_, bf16[32,3072]{1,0:T(8,128)(2,1)S(1)} %collective-permute-done.10.refs_2_, ...), custom_call_target="tpu_custom_call" | custom-call | flops 1207959552 | bytes 6291456 | tf_op jit(solution)/shard_map/project/pallas_call | solution.py:172
  51.6 1.4 collective-permute-done.4.refs_5_
  53.0 3.9 %collective-permute-done.5.refs_6_ = bf16[32,3072]{1,0:T(8,128)(2,1)S(1)} collective-permute-done((bf16[32,3072]{1,0:T(8,128)(2,1)S(1)}, bf16[32,3072]{1,0:T(8,128)(2,1)S(1)}, u32[]{:S(2)}, u32[]{:S(2)}) %collective-permute-start.5) | collective-permute-done | bytes 196640 | tf_op jit(solution)/shard_map/ppermute | solution.py:52
  56.9 2.1 %collective-permute-done.6.refs_7_ = bf16[32,3072]{1,0:T(8,128)(2,1)S(1)} collective-permute-done((bf16[32,3072]{1,0:T(8,128)(2,1)S(1)}, bf16[32,3072]{1,0:T(8,128)(2,1)S(1)}, u32[]{:S(2)}, u32[]{:S(2)}) %collective-permute-start.6) | collective-permute-done | bytes 196640 | tf_op jit(solution)/shard_map/ppermute | solution.py:52
  59.0 1.8 %project.2 = (bf16[256,128]{1,0:T(8,128)(2,1)S(1)}, bf16[256,256]{1,0:T(8,128)(2,1)S(1)}, bf16[256,384]{1,0:T(8,128)(2,1)S(1)}) custom-call(bf16[32,3072]{1,0:T(8,128)(2,1)S(1)} %copy-done.6, bf16[32,3072]{1,0:T(8,128)(2,1)S(1)} %collective-permute-done.refs_1_, bf16[32,3072]{1,0:T(8,128)(2,1)S(1)} %collective-permute-done.1.refs_2_, ...), custom_call_target="tpu_custom_call" | custom-call | flops 1207959552 | bytes 6291456 | tf_op jit(solution)/shard_map/project/pallas_call | solution.py:172
  60.9 0.4 collective-permute-start.23
  61.3 1.0 collective-permute-done.8
  62.3 0.7 copy-done.10
  63.1 1.6 collective-permute-start.19
  64.6 0.5 collective-permute-start.20
  65.2 2.1 %collective-permute-start.21 = (bf16[1024,256]{1,0:T(8,128)(2,1)S(1)}, bf16[1024,256]{1,0:T(8,128)(2,1)}, u32[]{:S(2)}, u32[]{:S(2)}) collective-permute-start(bf16[1024,256]{1,0:T(8,128)(2,1)S(1)} %pad_maximum_fusion.kv_ref.k0), channel_id=1, source_target_pairs={{0,128},{32,160},{64,192},{96,224},{128,0},{160,32},{192,64},{224,... | collective-permute-start | bytes 1572872 | tf_op jit(solution)/shard_map/ppermute | solution.py:60
  67.4 1.0 copy-done.4
  68.4 0.6 latent_matrix.1.m_ref
  69.0 0.8 slice.186
  69.8 2.4 %collective-permute-start.18 = (bf16[1024,128]{1,0:T(8,128)(2,1)S(1)}, bf16[1024,128]{1,0:T(8,128)(2,1)S(1)}, u32[]{:S(2)}, u32[]{:S(2)}) collective-permute-start(bf16[1024,128]{1,0:T(8,128)(2,1)S(1)} %pad_maximum_fusion.1.q_ref.qa_ref), channel_id=1, source_target_pairs={{0,32},{32,0},{64,96},{96,64},{128,160},{160,128},{192,224},{224,1... | collective-permute-start | bytes 786440 | tf_op jit(solution)/shard_map/ppermute | solution.py:64
  72.2 5.2 %self_attention.1 = (bf16[32,16,128]{2,1,0:T(8,128)(2,1)S(1)}, f32[1024,256]{1,0:T(8,128)S(1)}, f32[1024,128]{1,0:T(8,128)S(1)}) custom-call(s32[5]{0:T(128)S(1)} %stack.23.s_ref, bf16[1024,128]{1,0:T(8,128)(2,1)S(1)} %pad_maximum_fusion.1.q_ref.qa_ref, bf16[1024,256]{1,0:T(8,128)(2,1)S(1)} %pad_maximum_fusion.kv_ref.k0, bf16[256,64]{1,0:T(8,128)(2,1)S(1)} %latent_matrix.1.m_ref), custom_call_target="tpu_custom_call" | custom-call | flops 805306368 | bytes 1048576 | tf_op jit(solution)/shard_map/self_attention/pallas_call | solution.py:227
  77.4 15.3 %all_to_all.20 = bf16[32,16,128]{2,1,0:T(8,128)(2,1)S(1)} all-to-all(bf16[32,16,128]{2,1,0:T(8,128)(2,1)S(1)} %get-tuple-element.26), channel_id=1, replica_groups=mesh['span'=8,'seq'=32] {'seq'}, dimensions={0} | all-to-all | bytes 262144 | tf_op jit(solution)/shard_map/all_to_all | solution.py:472
  92.7 0.5 collective-permute-start.24
  93.2 12.0 %other_attention.1 = bf16[8,272,128]{2,1,0:T(8,128)(2,1)} custom-call(s32[8]{0:T(128)S(1)} %copy-done.8, s32[5]{0:T(128)S(1)} %stack.23.s_ref, bf16[1024,128]{1,0:T(8,128)(2,1)S(1)} %pad_maximum_fusion.1.q_ref.qa_ref, bf16[1024,128]{1,0:T(8,128)(2,1)S(1)} %collective-permute-done.18.qb_ref, f32[1024,256]{1,0:T(8,128)S(1)} %get-tuple-element.27.acc_in, ...), custom_call_target="tpu_custom_call" | custom-call | flops 4831838208 | bytes 4194304 | tf_op jit(solution)/shard_map/other_attention/pallas_call | solution.py:329
  105.2 5.0 %all-to-all-start.1 = ((bf16[8,272,128]{2,1,0:T(8,128)(2,1)}), bf16[8,272,128]{2,1,0:T(8,128)(2,1)S(1)}, u32[]{:S(2)}, u32[]{:S(2)}) async-start(bf16[8,272,128]{2,1,0:T(8,128)(2,1)} %other_attention.1), calls=%async_computation.1 | async-start | bytes 1114112 | tf_op jit(solution)/shard_map/all_to_all | solution.py:490
  110.2 1.2 fusion.4
  111.4 8.1 %all-to-all-done.1.in_ref = bf16[8,272,128]{2,1,0:T(8,128)(2,1)S(1)} async-done(((bf16[8,272,128]{2,1,0:T(8,128)(2,1)}), bf16[8,272,128]{2,1,0:T(8,128)(2,1)S(1)}, u32[]{:S(2)}, u32[]{:S(2)}) %all-to-all-start.1) | async-done | bytes 557088 | tf_op jit(solution)/shard_map/all_to_all | solution.py:490
  119.5 5.3 %join_heads.1 = bf16[256,3072]{1,0:T(8,128)(2,1)} custom-call(s32[5]{0:T(128)S(1)} %stack.23.s_ref, bf16[8,272,128]{2,1,0:T(8,128)(2,1)S(1)} %all-to-all-done.1.in_ref, bf16[128,3072]{1,0:T(8,128)(2,1)S(1)} %bitcast.45, bf16[128,3072]{1,0:T(8,128)(2,1)} %collective-permute-done.22.w1_ref, bf16[128,3072]{1,0:T(8,128)(2,1)S(1)} %collective-permute-done.23.w2_ref, ...), custom_call_target="tpu_custom_call" | custom-call | tf_op jit(solution)/shard_map/join_heads/pallas_call | solution.py:388
  125.0 0.6 broadcast_in_dim.59
  125.6 4.7 %all-to-all-start.2 = ((bf16[8,16,128]{2,1,0:T(8,128)(2,1)}), bf16[8,16,128]{2,1,0:T(8,128)(2,1)S(1)}, u32[]{:S(2)}, u32[]{:S(2)}) async-start(bf16[8,16,128]{2,1,0:T(8,128)(2,1)} %broadcast_in_dim.59), calls=%async_computation.3 | async-start | bytes 65536 | tf_op jit(solution)/shard_map/all_to_all | solution.py:506
  130.3 0.6 fusion.3
  132.9 3.7 %all-to-all-done.2 = bf16[8,16,128]{2,1,0:T(8,128)(2,1)S(1)} async-done(((bf16[8,16,128]{2,1,0:T(8,128)(2,1)}), bf16[8,16,128]{2,1,0:T(8,128)(2,1)S(1)}, u32[]{:S(2)}, u32[]{:S(2)}) %all-to-all-start.2) | async-done | bytes 32800 | tf_op jit(solution)/shard_map/all_to_all | solution.py:506
  136.6 0.7 broadcast_in_dim.61
  137.3 5.1 %all-to-all-start.3 = ((bf16[32,16,128]{2,1,0:T(8,128)(2,1)}), bf16[32,16,128]{2,1,0:T(8,128)(2,1)S(1)}, u32[]{:S(2)}, u32[]{:S(2)}) async-start(bf16[32,16,128]{2,1,0:T(8,128)(2,1)} %broadcast_in_dim.61), calls=%async_computation.4 | async-start | bytes 262144 | tf_op jit(solution)/shard_map/all_to_all | solution.py:510
  142.5 9.2 %all-to-all-done.3 = bf16[32,16,128]{2,1,0:T(8,128)(2,1)S(1)} async-done(((bf16[32,16,128]{2,1,0:T(8,128)(2,1)}), bf16[32,16,128]{2,1,0:T(8,128)(2,1)S(1)}, u32[]{:S(2)}, u32[]{:S(2)}) %all-to-all-start.3) | async-done | bytes 131104 | tf_op jit(solution)/shard_map/all_to_all | solution.py:510
  151.8 0.1 copy.32
  151.9 0.1 copy.33
  152.1 0.1 copy.21
  152.2 0.1 copy.29
  152.3 0.1 copy.30
  152.5 0.1 copy.19
  152.6 0.1 copy.26
  152.7 0.1 copy.27
  152.9 0.1 copy.17
  153.4 0.3 concatenate.35
  153.8 0.8 fusion
  154.6 6.9 %reduce-scatter.2.cloned.1.call-done = bf16[32,3072]{1,0:T(8,128)(2,1)} async-done(((bf16[256,3072]{1,0:T(8,128)(2,1)}), bf16[32,3072]{1,0:T(8,128)(2,1)}) %reduce-scatter.2.cloned.1.call-update) | async-done | bytes 196624 | tf_op jit(solution)/shard_map/reduce_scatter | solution.py:496
  161.6 1.7 fusion.1
  (69 shorter events, 1.5 us)
Async XLA Ops:
  7.2 146.6 %copy-start = (bf16[3,3,3,16,64]{4,3,2,1,0:T(8,128)(2,1)S(1)}, bf16[3,3,3,16,64]{4,3,2,1,0:T(8,128)(2,1)}, u32[]{:S(2)}) copy-start(bf16[3,3,3,16,64]{4,3,2,1,0:T(8,128)(2,1)} %param.15) | copy-start | bytes 165892
  7.2 40.8 %collective-permute-start.7 = (bf16[3072,384]{1,0:T(8,128)(2,1)}, bf16[3072,384]{1,0:T(8,128)(2,1)S(1)}, u32[]{:S(2)}, u32[]{:S(2)}) collective-permute-start(bf16[3072,384]{1,0:T(8,128)(2,1)} %bitcast.39), channel_id=1, source_target_pairs={{0,1},{1,0},{2,3},{3,2},{4,5},{5,4},{6,7},{7,6},{8,9},{9,8},{10,11... | collective-permute-start | bytes 7077896 | tf_op jit(solution)/shard_map/ppermute | solution.py:56
  10.0 11.6 %collective-permute-start.2 = (bf16[32,3072]{1,0:T(8,128)(2,1)}, bf16[32,3072]{1,0:T(8,128)(2,1)S(1)}, u32[]{:S(2)}, u32[]{:S(2)}) collective-permute-start(bf16[32,3072]{1,0:T(8,128)(2,1)} %get-tuple-element.17.refs_0_), channel_id=1, source_target_pairs={{0,2},{1,3},{2,4},{3,5},{4,6},{5,7},{6,8},{7,9},{8,10},{9,11},{10,... | collective-permute-start | bytes 589832 | tf_op jit(solution)/shard_map/ppermute | solution.py:48
  11.9 9.7 %collective-permute-start = (bf16[32,3072]{1,0:T(8,128)(2,1)}, bf16[32,3072]{1,0:T(8,128)(2,1)S(1)}, u32[]{:S(2)}, u32[]{:S(2)}) collective-permute-start(bf16[32,3072]{1,0:T(8,128)(2,1)} %get-tuple-element.17.refs_0_), channel_id=1, source_target_pairs={{0,14},{1,15},{2,0},{3,1},{4,2},{5,3},{6,4},{7,5},{8,6},{9,7},{10,... | collective-permute-start | bytes 589832 | tf_op jit(solution)/shard_map/ppermute | solution.py:48
  21.6 7.9 %collective-permute-start.3 = (bf16[32,3072]{1,0:T(8,128)(2,1)S(1)}, bf16[32,3072]{1,0:T(8,128)(2,1)S(1)}, u32[]{:S(2)}, u32[]{:S(2)}) collective-permute-start(bf16[32,3072]{1,0:T(8,128)(2,1)S(1)} %collective-permute-done.2.refs_4_), channel_id=1, source_target_pairs={{0,2},{1,3},{2,4},{3,5},{4,6},{5,7},{6,8},{7,9},{8,10},{9,11},{10,... | collective-permute-start | bytes 589832 | tf_op jit(solution)/shard_map/ppermute | solution.py:48
  21.6 7.9 %collective-permute-start.1 = (bf16[32,3072]{1,0:T(8,128)(2,1)S(1)}, bf16[32,3072]{1,0:T(8,128)(2,1)S(1)}, u32[]{:S(2)}, u32[]{:S(2)}) collective-permute-start(bf16[32,3072]{1,0:T(8,128)(2,1)S(1)} %collective-permute-done.refs_1_), channel_id=1, source_target_pairs={{0,14},{1,15},{2,0},{3,1},{4,2},{5,3},{6,4},{7,5},{8,6},{9,7},{10,... | collective-permute-start | bytes 589832 | tf_op jit(solution)/shard_map/ppermute | solution.py:48
  29.5 7.1 %collective-permute-start.10 = (bf16[32,3072]{1,0:T(8,128)(2,1)S(1)}, bf16[32,3072]{1,0:T(8,128)(2,1)S(1)}, u32[]{:S(2)}, u32[]{:S(2)}) collective-permute-start(bf16[32,3072]{1,0:T(8,128)(2,1)S(1)} %collective-permute-done.3.refs_3_), channel_id=1, source_target_pairs={{0,2},{1,3},{2,4},{3,5},{4,6},{5,7},{6,8},{7,9},{8,10},{9,11},{10,... | collective-permute-start | bytes 589832 | tf_op jit(solution)/shard_map/ppermute | solution.py:48
  29.6 7.2 %collective-permute-start.12 = (bf16[32,3072]{1,0:T(8,128)(2,1)S(1)}, bf16[32,3072]{1,0:T(8,128)(2,1)S(1)}, u32[]{:S(2)}, u32[]{:S(2)}) collective-permute-start(bf16[32,3072]{1,0:T(8,128)(2,1)S(1)} %collective-permute-done.1.refs_2_), channel_id=1, source_target_pairs={{0,16},{1,17},{2,18},{3,19},{4,20},{5,21},{6,22},{7,23},{8,24},{9,... | collective-permute-start | bytes 589832 | tf_op jit(solution)/shard_map/ppermute | solution.py:52
  30.0 10.5 %collective-permute-start.9 = (bf16[32,3072]{1,0:T(8,128)(2,1)S(1)}, bf16[32,3072]{1,0:T(8,128)(2,1)S(1)}, u32[]{:S(2)}, u32[]{:S(2)}) collective-permute-start(bf16[32,3072]{1,0:T(8,128)(2,1)S(1)} %collective-permute-done.1.refs_2_), channel_id=1, source_target_pairs={{0,14},{1,15},{2,0},{3,1},{4,2},{5,3},{6,4},{7,5},{8,6},{9,7},{10,... | collective-permute-start | bytes 589832 | tf_op jit(solution)/shard_map/ppermute | solution.py:48
  33.2 7.9 %collective-permute-start.15 = (bf16[32,3072]{1,0:T(8,128)(2,1)S(1)}, bf16[32,3072]{1,0:T(8,128)(2,1)S(1)}, u32[]{:S(2)}, u32[]{:S(2)}) collective-permute-start(bf16[32,3072]{1,0:T(8,128)(2,1)S(1)} %collective-permute-done.3.refs_3_), channel_id=1, source_target_pairs={{0,16},{1,17},{2,18},{3,19},{4,20},{5,21},{6,22},{7,23},{8,24},{9,... | collective-permute-start | bytes 589832 | tf_op jit(solution)/shard_map/ppermute | solution.py:52
  36.6 8.3 %collective-permute-start.11 = (bf16[32,3072]{1,0:T(8,128)(2,1)S(1)}, bf16[32,3072]{1,0:T(8,128)(2,1)S(1)}, u32[]{:S(2)}, u32[]{:S(2)}) collective-permute-start(bf16[32,3072]{1,0:T(8,128)(2,1)S(1)} %collective-permute-done.10.refs_2_), channel_id=1, source_target_pairs={{0,2},{1,3},{2,4},{3,5},{4,6},{5,7},{6,8},{7,9},{8,10},{9,11},{10,... | collective-permute-start | bytes 589832 | tf_op jit(solution)/shard_map/ppermute | solution.py:48
  36.8 8.3 %collective-permute-start.13 = (bf16[32,3072]{1,0:T(8,128)(2,1)S(1)}, bf16[32,3072]{1,0:T(8,128)(2,1)S(1)}, u32[]{:S(2)}, u32[]{:S(2)}) collective-permute-start(bf16[32,3072]{1,0:T(8,128)(2,1)S(1)} %collective-permute-done.12.refs_3_), channel_id=1, source_target_pairs={{0,14},{1,15},{2,0},{3,1},{4,2},{5,3},{6,4},{7,5},{8,6},{9,7},{10,... | collective-permute-start | bytes 589832 | tf_op jit(solution)/shard_map/ppermute | solution.py:48
  40.5 6.7 %collective-permute-start.14 = (bf16[32,3072]{1,0:T(8,128)(2,1)S(1)}, bf16[32,3072]{1,0:T(8,128)(2,1)S(1)}, u32[]{:S(2)}, u32[]{:S(2)}) collective-permute-start(bf16[32,3072]{1,0:T(8,128)(2,1)S(1)} %collective-permute-done.9.refs_0_), channel_id=1, source_target_pairs={{0,30},{1,31},{2,16},{3,17},{4,18},{5,19},{6,20},{7,21},{8,22},{9,... | collective-permute-start | bytes 589832 | tf_op jit(solution)/shard_map/ppermute | solution.py:92
  41.1 6.9 %collective-permute-start.16 = (bf16[32,3072]{1,0:T(8,128)(2,1)S(1)}, bf16[32,3072]{1,0:T(8,128)(2,1)S(1)}, u32[]{:S(2)}, u32[]{:S(2)}) collective-permute-start(bf16[32,3072]{1,0:T(8,128)(2,1)S(1)} %collective-permute-done.15.refs_7_), channel_id=1, source_target_pairs={{0,2},{1,3},{2,4},{3,5},{4,6},{5,7},{6,8},{7,9},{8,10},{9,11},{10,... | collective-permute-start | bytes 589832 | tf_op jit(solution)/shard_map/ppermute | solution.py:48
  44.9 8.1 %collective-permute-start.4 = (bf16[32,3072]{1,0:T(8,128)(2,1)}, bf16[32,3072]{1,0:T(8,128)(2,1)S(1)}, u32[]{:S(2)}, u32[]{:S(2)}) collective-permute-start(bf16[32,3072]{1,0:T(8,128)(2,1)} %get-tuple-element.17.refs_0_), channel_id=1, source_target_pairs={{0,16},{1,17},{2,18},{3,19},{4,20},{5,21},{6,22},{7,23},{8,24},{9,... | collective-permute-start | bytes 589832 | tf_op jit(solution)/shard_map/ppermute | solution.py:52
  45.1 11.7 %collective-permute-start.5 = (bf16[32,3072]{1,0:T(8,128)(2,1)S(1)}, bf16[32,3072]{1,0:T(8,128)(2,1)S(1)}, u32[]{:S(2)}, u32[]{:S(2)}) collective-permute-start(bf16[32,3072]{1,0:T(8,128)(2,1)S(1)} %collective-permute-done.refs_1_), channel_id=1, source_target_pairs={{0,16},{1,17},{2,18},{3,19},{4,20},{5,21},{6,22},{7,23},{8,24},{9,... | collective-permute-start | bytes 589832 | tf_op jit(solution)/shard_map/ppermute | solution.py:52
  47.2 11.8 %collective-permute-start.6 = (bf16[32,3072]{1,0:T(8,128)(2,1)S(1)}, bf16[32,3072]{1,0:T(8,128)(2,1)S(1)}, u32[]{:S(2)}, u32[]{:S(2)}) collective-permute-start(bf16[32,3072]{1,0:T(8,128)(2,1)S(1)} %collective-permute-done.2.refs_4_), channel_id=1, source_target_pairs={{0,16},{1,17},{2,18},{3,19},{4,20},{5,21},{6,22},{7,23},{8,24},{9,... | collective-permute-start | bytes 589832 | tf_op jit(solution)/shard_map/ppermute | solution.py:52
  48.0 1.7 copy-start.1
  49.7 9.3 %copy-start.2 = (bf16[1,3072,384]{2,1,0:T(8,128)(2,1)S(1)}, bf16[1,3072,384]{2,1,0:T(8,128)(2,1)}, u32[]{:S(2)}) copy-start(bf16[1,3072,384]{2,1,0:T(8,128)(2,1)} %param.12) | copy-start | bytes 7077892
  49.7 9.3 %copy-start.6 = (bf16[32,3072]{1,0:T(8,128)(2,1)S(1)}, bf16[32,3072]{1,0:T(8,128)(2,1)}, u32[]{:S(2)}) copy-start(bf16[32,3072]{1,0:T(8,128)(2,1)} %get-tuple-element.17.refs_0_) | copy-start | bytes 589828
  51.5 9.4 %copy-start.3 = (bf16[1,128,3072]{2,1,0:T(8,128)(2,1)S(1)}, bf16[1,128,3072]{2,1,0:T(8,128)(2,1)}, u32[]{:S(2)}) copy-start(bf16[1,128,3072]{2,1,0:T(8,128)(2,1)} %param.13) | copy-start | bytes 2359300
  51.5 15.9 %copy-start.7 = (f32[1,3072]{1,0:T(1,128)S(1)}, f32[1,3072]{1,0:T(1,128)}, u32[]{:S(2)}) copy-start(f32[1,3072]{1,0:T(1,128)} %get-tuple-element.16.gate_ref) | copy-start | bytes 36868
  51.5 9.7 %collective-permute-start.17 = (bf16[256,384]{1,0:T(8,128)(2,1)S(1)}, bf16[256,384]{1,0:T(8,128)(2,1)S(1)}, u32[]{:S(2)}, u32[]{:S(2)}) collective-permute-start(bf16[256,384]{1,0:T(8,128)(2,1)S(1)} %get-tuple-element.21), channel_id=1, source_target_pairs={{0,1},{1,0},{2,3},{3,2},{4,5},{5,4},{6,7},{7,6},{8,9},{9,8},{10,11... | collective-permute-start | bytes 589832 | tf_op jit(solution)/shard_map/ppermute | solution.py:56
  60.8 1.5 collective-permute-start.8
  60.9 31.8 %collective-permute-start.23 = (bf16[128,3072]{1,0:T(8,128)(2,1)S(1)}, bf16[128,3072]{1,0:T(8,128)(2,1)S(1)}, u32[]{:S(2)}, u32[]{:S(2)}) collective-permute-start(bf16[128,3072]{1,0:T(8,128)(2,1)S(1)} %bitcast.42), channel_id=1, source_target_pairs={{0,16},{1,17},{2,18},{3,19},{4,20},{5,21},{6,22},{7,23},{8,24},{9,... | collective-permute-start | bytes 2359304 | tf_op jit(solution)/shard_map/ppermute | solution.py:52
  61.3 3.4 %copy-start.11 = (bf16[256,384]{1,0:T(8,128)(2,1)}, bf16[256,384]{1,0:T(8,128)(2,1)S(1)}, u32[]{:S(2)}) copy-start(bf16[256,384]{1,0:T(8,128)(2,1)S(1)} %collective-permute-done.17) | copy-start | bytes 589828
  62.3 0.7 copy-start.10
  63.0 6.8 %slice-start = ((bf16[256,384]{1,0:T(8,128)(2,1)}), bf16[256,128]{1,0:T(8,128)(2,1)S(1)}, s32[]{:S(2)}) async-start(bf16[256,384]{1,0:T(8,128)(2,1)} %copy-done.10), calls=%async_computation.6 | async-start | bytes 131072 | tf_op jit(solution)/shard_map/slice | solution.py:464
  63.1 30.2 %collective-permute-start.19 = (bf16[1024,256]{1,0:T(8,128)(2,1)S(1)}, bf16[1024,256]{1,0:T(8,128)(2,1)S(1)}, u32[]{:S(2)}, u32[]{:S(2)}) collective-permute-start(bf16[1024,256]{1,0:T(8,128)(2,1)S(1)} %pad_maximum_fusion.kv_ref.k0), channel_id=1, source_target_pairs={{0,64},{32,96},{64,128},{96,160},{128,192},{160,224},{192,0},{224,... | collective-permute-start | bytes 1572872 | tf_op jit(solution)/shard_map/ppermute | solution.py:60
  64.6 28.6 %collective-permute-start.20 = (bf16[1024,256]{1,0:T(8,128)(2,1)S(1)}, bf16[1024,256]{1,0:T(8,128)(2,1)}, u32[]{:S(2)}, u32[]{:S(2)}) collective-permute-start(bf16[1024,256]{1,0:T(8,128)(2,1)S(1)} %pad_maximum_fusion.kv_ref.k0), channel_id=1, source_target_pairs={{0,192},{32,224},{64,0},{96,32},{128,64},{160,96},{192,128},{224,1... | collective-permute-start | bytes 1572872 | tf_op jit(solution)/shard_map/ppermute | solution.py:60
  65.2 28.1 %collective-permute-start.21 = (bf16[1024,256]{1,0:T(8,128)(2,1)S(1)}, bf16[1024,256]{1,0:T(8,128)(2,1)}, u32[]{:S(2)}, u32[]{:S(2)}) collective-permute-start(bf16[1024,256]{1,0:T(8,128)(2,1)S(1)} %pad_maximum_fusion.kv_ref.k0), channel_id=1, source_target_pairs={{0,128},{32,160},{64,192},{96,224},{128,0},{160,32},{192,64},{224,... | collective-permute-start | bytes 1572872 | tf_op jit(solution)/shard_map/ppermute | solution.py:60
  67.4 1.0 copy-start.4
  68.4 24.9 %copy-start.8 = (s32[8]{0:T(128)S(1)}, s32[8]{0:T(128)}, u32[]{:S(2)}) copy-start(s32[8]{0:T(128)} %order_ref.1) | copy-start | bytes 100
  69.8 22.9 %collective-permute-start.18 = (bf16[1024,128]{1,0:T(8,128)(2,1)S(1)}, bf16[1024,128]{1,0:T(8,128)(2,1)S(1)}, u32[]{:S(2)}, u32[]{:S(2)}) collective-permute-start(bf16[1024,128]{1,0:T(8,128)(2,1)S(1)} %pad_maximum_fusion.1.q_ref.qa_ref), channel_id=1, source_target_pairs={{0,32},{32,0},{64,96},{96,64},{128,160},{160,128},{192,224},{224,1... | collective-permute-start | bytes 786440 | tf_op jit(solution)/shard_map/ppermute | solution.py:64
  92.7 18.7 %collective-permute-start.22 = (bf16[128,3072]{1,0:T(8,128)(2,1)S(1)}, bf16[128,3072]{1,0:T(8,128)(2,1)}, u32[]{:S(2)}, u32[]{:S(2)}) collective-permute-start(bf16[128,3072]{1,0:T(8,128)(2,1)S(1)} %bitcast.44), channel_id=1, source_target_pairs={{0,1},{1,0},{2,3},{3,2},{4,5},{5,4},{6,7},{7,6},{8,9},{9,8},{10,11... | collective-permute-start | bytes 2359304 | tf_op jit(solution)/shard_map/ppermute | solution.py:56
  92.7 26.8 %collective-permute-start.24 = (bf16[128,3072]{1,0:T(8,128)(2,1)S(1)}, bf16[128,3072]{1,0:T(8,128)(2,1)}, u32[]{:S(2)}, u32[]{:S(2)}) collective-permute-start(bf16[128,3072]{1,0:T(8,128)(2,1)S(1)} %collective-permute-done.23.w2_ref), channel_id=1, source_target_pairs={{0,1},{1,0},{2,3},{3,2},{4,5},{5,4},{6,7},{7,6},{8,9},{9,8},{10,11... | collective-permute-start | bytes 2359304 | tf_op jit(solution)/shard_map/ppermute | solution.py:56
  93.2 17.0 %copy-start.5 = (bf16[3072,64]{0,1:T(8,128)(2,1)S(1)}, bf16[3072,64]{0,1:T(8,128)(2,1)}, u32[]{:S(2)}) copy-start(bf16[3072,64]{0,1:T(8,128)(2,1)} %param.14) | copy-start | bytes 1179652
  105.2 14.3 %all-to-all-start.1 = ((bf16[8,272,128]{2,1,0:T(8,128)(2,1)}), bf16[8,272,128]{2,1,0:T(8,128)(2,1)S(1)}, u32[]{:S(2)}, u32[]{:S(2)}) async-start(bf16[8,272,128]{2,1,0:T(8,128)(2,1)} %other_attention.1), calls=%async_computation.1 | async-start | bytes 1114112 | tf_op jit(solution)/shard_map/all_to_all | solution.py:490
  110.2 51.4 %reduce-scatter.2.cloned.1.call-start = ((), (), s32[]{:S(2)}) async-start(), calls=%async_computation.5 | async-start | bytes 1769472 | tf_op jit(solution)/shard_map/reduce_scatter | solution.py:496
  125.6 11.0 %all-to-all-start.2 = ((bf16[8,16,128]{2,1,0:T(8,128)(2,1)}), bf16[8,16,128]{2,1,0:T(8,128)(2,1)S(1)}, u32[]{:S(2)}, u32[]{:S(2)}) async-start(bf16[8,16,128]{2,1,0:T(8,128)(2,1)} %broadcast_in_dim.59), calls=%async_computation.3 | async-start | bytes 65536 | tf_op jit(solution)/shard_map/all_to_all | solution.py:506
  137.3 14.4 %all-to-all-start.3 = ((bf16[32,16,128]{2,1,0:T(8,128)(2,1)}), bf16[32,16,128]{2,1,0:T(8,128)(2,1)S(1)}, u32[]{:S(2)}, u32[]{:S(2)}) async-start(bf16[32,16,128]{2,1,0:T(8,128)(2,1)} %broadcast_in_dim.61), calls=%async_computation.4 | async-start | bytes 262144 | tf_op jit(solution)/shard_map/all_to_all | solution.py:510
  151.7 9.9 %copy-start.9 = (bf16[1,32,3072]{2,1,0:T(8,128)(2,1)S(1)}, bf16[1,32,3072]{2,1,0:T(8,128)(2,1)}, u32[]{:S(2)}) copy-start(bf16[1,32,3072]{2,1,0:T(8,128)(2,1)} %param.8) | copy-start | bytes 589828
Sparse Core Ops, SparseCore 0:
  124.9 36.5 reduce-scatter.1

commit v4 on v1

--- a/solution.py
+++ b/solution.py
@@ -83,13 +83,13 @@
 
 def gather_class(b):
     up1, dn1, y0 = move_z(b, 1), move_z(b, -1), move_y(b)
-    up2, dn2 = move_z(up1, 1), move_z(dn1, -1)
+    up2, dn2 = move_z(after(up1, y0), 1), move_z(dn1, -1)
     yu1, yd1 = move_y(up1), move_y(dn1)
     up3, dn3 = move_z(up2, 1), move_z(dn2, -1)
     yu2, yd2 = move_y(up2), move_y(dn2)
-    far = move_z(up3, 1)
+    far = move_z(after(up3, yu1), 1)
     yu3, yd3 = move_z(yu2, 1), move_z(yd2, -1)
-    yfar = lax.ppermute(dn3, "seq", seq_route(dy=1, dz=-1))
+    yfar = lax.ppermute(after(dn3, yd1), "seq", seq_route(dy=1, dz=-1))
     return (b, dn1, dn2, up2, up1, y0, yd1, yu1), (dn3, far, up3, yd2, yd3, yfar, yu3, yu2)
 
 

time: 166 us -> 171 us (1.030)
  starting transfers between devices: 38.5 us -> 55.7 us
  waiting for transfers between devices: 54.5 us -> 47.3 us
  Pallas kernels: 27.3 us -> 22.1 us
    ppermute x6, waiting for transfers between devices: 13.3 us -> 6.73 us  [move_y(): return lax.ppermute(a, 'seq', seq_route(dy=1))]
    ppermute x9, starting transfers between devices: 9.66 us -> 15.8 us  [move_z(): return lax.ppermute(a, 'seq', seq_route(dz=d))]
    pallas_call x1, Pallas kernels: 10.5 us -> 5.24 us  [other_attention(): pl.pallas_call(other_kernel, grid_spec=pltpu.PrefetchScalarGridSpec(num_s...]
    all_to_all x1, starting transfers between devices: 6.33 us -> 9.71 us  [per_device(): lax.all_to_all(chunks, ('span', 'seq'), 0, 0, tiled=True, axis_index_grou...]
    all_to_all x1, starting transfers between devices: 5.13 us -> 8.11 us  [per_device(): lax.all_to_all(jnp.broadcast_to(latents[None], (NX * NH,) + latents.shape...]
    ppermute x1, starting transfers between devices: 1.42 us -> 3.73 us  [gather_class(): yfar = lax.ppermute(after(dn3, yd1), 'seq', seq_route(dy=1, dz=-1))]
  transfers between devices with their start and end apart: 29 -> 29, of which waited for: 12 -> 10; matrix products, arithmetic and copies ran while one was open for 4% -> 4% of each run, Pallas kernels for 13% -> 10%
where the time goes in v4:
time: 171 us; the launch traced here: 169 us
  starting transfers between devices  55.7 us (33%)
  waiting for transfers between devices  47.3 us (28%)
  Pallas kernels  22.1 us (13%)
  between operations  17.1 us (10%)
  blocking collectives  15.9 us (9%)
  local copies, waits for them, and re-layouts  6.68 us (4%)
  other arithmetic  2.97 us (2%)
    all_to_all x1, blocking collectives, per_device(): part = lax.all_to_all(part, 'seq', 0, 0, tiled=True)  15.9 us
    ppermute x9, starting transfers between devices, move_z(): return lax.ppermute(a, 'seq', seq_route(dz=d))  15.8 us
    ppermute x9, waiting for transfers between devices, move_z(): return lax.ppermute(a, 'seq', seq_route(dz=d))  10.4 us
    all_to_all x1, waiting for transfers between devices, per_device(): lax.all_to_all(jnp.broadcast_to(latents, (seq_count,) + latents.shape[1:]...  10.3 us
    all_to_all x1, starting transfers between devices, per_device(): lax.all_to_all(chunks, ('span', 'seq'), 0, 0, tiled=True, axis_index_grou...  9.71 us
    all_to_all x1, waiting for transfers between devices, per_device(): lax.all_to_all(chunks, ('span', 'seq'), 0, 0, tiled=True, axis_index_grou...  9 us
    all_to_all x1, starting transfers between devices, per_device(): lax.all_to_all(jnp.broadcast_to(latents[None], (NX * NH,) + latents.shape...  8.11 us
    ppermute x6, waiting for transfers between devices, move_y(): return lax.ppermute(a, 'seq', seq_route(dy=1))  6.73 us
  transfers between devices with their start and end apart: 29, of which 10 were waited for; matrix products, arithmetic and copies ran while one was open for 4% of the time, Pallas kernels for 10%

profile of v4, /device:TPU:10, one launch (start us, length us, event | category | flops | bytes accessed | tf_op | source)
XLA Modules:
  0.0 168.7 jit_solution(16434754776595147455)
XLA Ops:
  7.2 0.1 collective-permute-start.7
  7.9 2.0 %normalize.1 = (bf16[32,3072]{1,0:T(8,128)(2,1)}, f32[1,3072]{1,0:T(1,128)}) custom-call(s32[1]{0:T(128)S(6)} %copy.37.level_ref, bf16[32,3072]{1,0:T(8,128)(2,1)} %bitcast.48, f32[3,16,3072]{2,1,0:T(8,128)} %bitcast.49), custom_call_target="tpu_custom_call" | custom-call | tf_op jit(solution)/shard_map/normalize/pallas_call | solution.py:114
  10.0 1.9 %collective-permute-start.2 = (bf16[32,3072]{1,0:T(8,128)(2,1)}, bf16[32,3072]{1,0:T(8,128)(2,1)S(1)}, u32[]{:S(2)}, u32[]{:S(2)}) collective-permute-start(bf16[32,3072]{1,0:T(8,128)(2,1)} %get-tuple-element.18.refs_0_), channel_id=1, source_target_pairs={{0,2},{1,3},{2,4},{3,5},{4,6},{5,7},{6,8},{7,9},{8,10},{9,11},{10,... | collective-permute-start | bytes 589832 | tf_op jit(solution)/shard_map/ppermute | solution.py:48
  11.9 0.4 collective-permute-start.3
  12.3 3.9 %collective-permute-start = (bf16[32,3072]{1,0:T(8,128)(2,1)}, bf16[32,3072]{1,0:T(8,128)(2,1)S(1)}, u32[]{:S(2)}, u32[]{:S(2)}) collective-permute-start(bf16[32,3072]{1,0:T(8,128)(2,1)} %get-tuple-element.18.refs_0_), channel_id=1, source_target_pairs={{0,14},{1,15},{2,0},{3,1},{4,2},{5,3},{6,4},{7,5},{8,6},{9,7},{10,... | collective-permute-start | bytes 589832 | tf_op jit(solution)/shard_map/ppermute | solution.py:48
  16.3 5.3 %collective-permute-done.2.refs_4_ = bf16[32,3072]{1,0:T(8,128)(2,1)S(1)} collective-permute-done((bf16[32,3072]{1,0:T(8,128)(2,1)}, bf16[32,3072]{1,0:T(8,128)(2,1)S(1)}, u32[]{:S(2)}, u32[]{:S(2)}) %collective-permute-start.2) | collective-permute-done | bytes 196640 | tf_op jit(solution)/shard_map/ppermute | solution.py:48
  21.6 3.2 %collective-permute-start.1 = (bf16[32,3072]{1,0:T(8,128)(2,1)S(1)}, bf16[32,3072]{1,0:T(8,128)(2,1)S(1)}, u32[]{:S(2)}, u32[]{:S(2)}) collective-permute-start(bf16[32,3072]{1,0:T(8,128)(2,1)S(1)} %collective-permute-done.refs_1_), channel_id=1, source_target_pairs={{0,14},{1,15},{2,0},{3,1},{4,2},{5,3},{6,4},{7,5},{8,6},{9,7},{10,... | collective-permute-start | bytes 589832 | tf_op jit(solution)/shard_map/ppermute | solution.py:48
  24.8 1.5 collective-permute-start.6
  26.3 3.2 %collective-permute-done.4.refs_3_ = bf16[32,3072]{1,0:T(8,128)(2,1)S(1)} collective-permute-done((bf16[32,3072]{1,0:T(8,128)(2,1)S(1)}, bf16[32,3072]{1,0:T(8,128)(2,1)S(1)}, u32[]{:S(2)}, u32[]{:S(2)}) %collective-permute-start.4) | collective-permute-done | bytes 196640 | tf_op jit(solution)/shard_map/ppermute | solution.py:48
  29.6 0.5 collective-permute-start.5
  30.0 3.2 %collective-permute-start.9 = (bf16[32,3072]{1,0:T(8,128)(2,1)S(1)}, bf16[32,3072]{1,0:T(8,128)(2,1)S(1)}, u32[]{:S(2)}, u32[]{:S(2)}) collective-permute-start(bf16[32,3072]{1,0:T(8,128)(2,1)S(1)} %collective-permute-done.1.refs_2_), channel_id=1, source_target_pairs={{0,14},{1,15},{2,0},{3,1},{4,2},{5,3},{6,4},{7,5},{8,6},{9,7},{10,... | collective-permute-start | bytes 589832 | tf_op jit(solution)/shard_map/ppermute | solution.py:48
  33.2 1.6 collective-permute-start.15
  34.8 1.8 %collective-permute-done.10.refs_2_ = bf16[32,3072]{1,0:T(8,128)(2,1)S(1)} collective-permute-done((bf16[32,3072]{1,0:T(8,128)(2,1)S(1)}, bf16[32,3072]{1,0:T(8,128)(2,1)S(1)}, u32[]{:S(2)}, u32[]{:S(2)}) %collective-permute-start.10) | collective-permute-done | bytes 196640 | tf_op jit(solution)/shard_map/ppermute | solution.py:48
  36.6 0.4 collective-permute-start.12
  37.1 0.5 collective-permute-start.11
  37.6 3.7 %collective-permute-start.14 = (bf16[32,3072]{1,0:T(8,128)(2,1)S(1)}, bf16[32,3072]{1,0:T(8,128)(2,1)S(1)}, u32[]{:S(2)}, u32[]{:S(2)}) collective-permute-start(bf16[32,3072]{1,0:T(8,128)(2,1)S(1)} %collective-permute-done.9.refs_0_), channel_id=1, source_target_pairs={{0,30},{1,31},{2,16},{3,17},{4,18},{5,19},{6,20},{7,21},{8,22},{9,... | collective-permute-start | bytes 589832 | tf_op jit(solution)/shard_map/ppermute | solution.py:92
  41.3 4.0 %collective-permute-done.15.refs_7_ = bf16[32,3072]{1,0:T(8,128)(2,1)S(1)} collective-permute-done((bf16[32,3072]{1,0:T(8,128)(2,1)S(1)}, bf16[32,3072]{1,0:T(8,128)(2,1)S(1)}, u32[]{:S(2)}, u32[]{:S(2)}) %collective-permute-start.15) | collective-permute-done | bytes 196640 | tf_op jit(solution)/shard_map/ppermute | solution.py:52
  45.3 2.8 %collective-permute-done.12.refs_3_ = bf16[32,3072]{1,0:T(8,128)(2,1)S(1)} collective-permute-done((bf16[32,3072]{1,0:T(8,128)(2,1)S(1)}, bf16[32,3072]{1,0:T(8,128)(2,1)S(1)}, u32[]{:S(2)}, u32[]{:S(2)}) %collective-permute-start.12) | collective-permute-done | bytes 196640 | tf_op jit(solution)/shard_map/ppermute | solution.py:52
  48.1 3.0 %collective-permute-start.13 = (bf16[32,3072]{1,0:T(8,128)(2,1)S(1)}, bf16[32,3072]{1,0:T(8,128)(2,1)S(1)}, u32[]{:S(2)}, u32[]{:S(2)}) collective-permute-start(bf16[32,3072]{1,0:T(8,128)(2,1)S(1)} %collective-permute-done.12.refs_3_), channel_id=1, source_target_pairs={{0,14},{1,15},{2,0},{3,1},{4,2},{5,3},{6,4},{7,5},{8,6},{9,7},{10,... | collective-permute-start | bytes 589832 | tf_op jit(solution)/shard_map/ppermute | solution.py:48
  51.0 1.7 copy-done.1
  52.7 0.9 copy-done.5
  53.6 1.8 %project.2 = (bf16[256,384]{1,0:T(8,128)(2,1)S(1)}, bf16[256,384]{1,0:T(8,128)(2,1)S(1)}) custom-call(bf16[32,3072]{1,0:T(8,128)(2,1)S(1)} %copy-done.5, bf16[32,3072]{1,0:T(8,128)(2,1)S(1)} %collective-permute-done.refs_1_, bf16[32,3072]{1,0:T(8,128)(2,1)S(1)} %collective-permute-done.1.refs_2_, bf16[32,3072]{1,0:T(8,128)(2,1)S(1)} %collective-permute-done.4.refs_3_, ...), custom_call_target="tpu_custom_call" | custom-call | flops 1207959552 | bytes 6291456 | tf_op jit(solution)/shard_map/project/pallas_call | solution.py:170
  55.4 0.1 collective-permute-start.8
  55.6 1.8 %project.3 = (bf16[256,384]{1,0:T(8,128)(2,1)S(1)}, bf16[256,384]{1,0:T(8,128)(2,1)S(1)}) custom-call(bf16[32,3072]{1,0:T(8,128)(2,1)S(1)} %collective-permute-done.9.refs_0_, bf16[32,3072]{1,0:T(8,128)(2,1)S(1)} %collective-permute-done.11.refs_1_, bf16[32,3072]{1,0:T(8,128)(2,1)S(1)} %collective-permute-done.10.refs_2_, ...), custom_call_target="tpu_custom_call" | custom-call | flops 1207959552 | bytes 6291456 | tf_op jit(solution)/shard_map/project/pallas_call | solution.py:170
  57.4 0.6 collective-permute-start.17
  58.0 0.4 collective-permute-start.23
  58.6 0.5 collective-permute-done.17
  59.2 1.6 collective-permute-start.19
  60.7 0.5 collective-permute-start.20
  61.3 2.1 %collective-permute-start.21 = (bf16[1024,256]{1,0:T(8,128)(2,1)S(1)}, bf16[1024,256]{1,0:T(8,128)(2,1)}, u32[]{:S(2)}, u32[]{:S(2)}) collective-permute-start(bf16[1024,256]{1,0:T(8,128)(2,1)S(1)} %slice.178.kv_ref.k0), channel_id=1, source_target_pairs={{0,128},{32,160},{64,192},{96,224},{128,0},{160,32},{192,64},{224,... | collective-permute-start | bytes 1572872 | tf_op jit(solution)/shard_map/ppermute | solution.py:60
  63.5 0.6 latent_matrix.1.m_ref
  64.1 1.0 slice.177.q_ref.qa_ref
  65.0 2.4 %collective-permute-start.18 = (bf16[1024,128]{1,0:T(8,128)(2,1)S(1)}, bf16[1024,128]{1,0:T(8,128)(2,1)S(1)}, u32[]{:S(2)}, u32[]{:S(2)}) collective-permute-start(bf16[1024,128]{1,0:T(8,128)(2,1)S(1)} %slice.177.q_ref.qa_ref), channel_id=1, source_target_pairs={{0,32},{32,0},{64,96},{96,64},{128,160},{160,128},{192,224},{224,1... | collective-permute-start | bytes 786440 | tf_op jit(solution)/shard_map/ppermute | solution.py:64
  67.4 5.2 %self_attention.1 = (bf16[32,16,128]{2,1,0:T(8,128)(2,1)S(1)}, f32[1024,256]{1,0:T(8,128)S(1)}, f32[1024,128]{1,0:T(8,128)S(1)}) custom-call(s32[5]{0:T(128)S(1)} %stack.23.s_ref, bf16[1024,128]{1,0:T(8,128)(2,1)S(1)} %slice.177.q_ref.qa_ref, bf16[1024,256]{1,0:T(8,128)(2,1)S(1)} %slice.178.kv_ref.k0, bf16[256,64]{1,0:T(8,128)(2,1)S(1)} %latent_matrix.1.m_ref), custom_call_target="tpu_custom_call" | custom-call | flops 805306368 | bytes 1048576 | tf_op jit(solution)/shard_map/self_attention/pallas_call | solution.py:225
  72.7 15.9 %all_to_all.20 = bf16[32,16,128]{2,1,0:T(8,128)(2,1)S(1)} all-to-all(bf16[32,16,128]{2,1,0:T(8,128)(2,1)S(1)} %get-tuple-element.28), channel_id=1, replica_groups=mesh['span'=8,'seq'=32] {'seq'}, dimensions={0} | all-to-all | bytes 262144 | tf_op jit(solution)/shard_map/all_to_all | solution.py:470
  88.6 0.5 collective-permute-start.24
  89.1 5.2 %other_attention.1 = bf16[8,272,128]{2,1,0:T(8,128)(2,1)} custom-call(s32[8]{0:T(128)S(1)} %copy-done.7, s32[5]{0:T(128)S(1)} %stack.23.s_ref, bf16[1024,128]{1,0:T(8,128)(2,1)S(1)} %slice.177.q_ref.qa_ref, bf16[1024,128]{1,0:T(8,128)(2,1)S(1)} %collective-permute-done.18.qb_ref, f32[1024,256]{1,0:T(8,128)S(1)} %get-tuple-element.29.acc_in, ...), custom_call_target="tpu_custom_call" | custom-call | flops 4831838208 | bytes 4194304 | tf_op jit(solution)/shard_map/other_attention/pallas_call | solution.py:327
  94.4 9.7 %all-to-all-start.1 = ((bf16[8,272,128]{2,1,0:T(8,128)(2,1)}), bf16[8,272,128]{2,1,0:T(8,128)(2,1)S(1)}, u32[]{:S(2)}, u32[]{:S(2)}) async-start(bf16[8,272,128]{2,1,0:T(8,128)(2,1)} %other_attention.1), calls=%async_computation.1 | async-start | bytes 1114112 | tf_op jit(solution)/shard_map/all_to_all | solution.py:488
  104.1 0.2 fusion.4
  104.3 9.0 %all-to-all-done.1.in_ref = bf16[8,272,128]{2,1,0:T(8,128)(2,1)S(1)} async-done(((bf16[8,272,128]{2,1,0:T(8,128)(2,1)}), bf16[8,272,128]{2,1,0:T(8,128)(2,1)S(1)}, u32[]{:S(2)}, u32[]{:S(2)}) %all-to-all-start.1) | async-done | bytes 557088 | tf_op jit(solution)/shard_map/all_to_all | solution.py:488
  113.3 5.4 %join_heads.1 = bf16[256,3072]{1,0:T(8,128)(2,1)} custom-call(s32[5]{0:T(128)S(1)} %stack.23.s_ref, bf16[8,272,128]{2,1,0:T(8,128)(2,1)S(1)} %all-to-all-done.1.in_ref, bf16[128,3072]{1,0:T(8,128)(2,1)S(1)} %bitcast.45, bf16[128,3072]{1,0:T(8,128)(2,1)} %collective-permute-done.22.w1_ref, bf16[128,3072]{1,0:T(8,128)(2,1)S(1)} %collective-permute-done.23.w2_ref, ...), custom_call_target="tpu_custom_call" | custom-call | tf_op jit(solution)/shard_map/join_heads/pallas_call | solution.py:386
  118.8 0.6 broadcast_in_dim.59
  119.5 8.1 %all-to-all-start.2 = ((bf16[8,16,128]{2,1,0:T(8,128)(2,1)}), bf16[8,16,128]{2,1,0:T(8,128)(2,1)S(1)}, u32[]{:S(2)}, u32[]{:S(2)}) async-start(bf16[8,16,128]{2,1,0:T(8,128)(2,1)} %broadcast_in_dim.59), calls=%async_computation.3 | async-start | bytes 65536 | tf_op jit(solution)/shard_map/all_to_all | solution.py:504
  127.6 0.6 fusion.3
  130.2 3.7 %all-to-all-done.2 = bf16[8,16,128]{2,1,0:T(8,128)(2,1)S(1)} async-done(((bf16[8,16,128]{2,1,0:T(8,128)(2,1)}), bf16[8,16,128]{2,1,0:T(8,128)(2,1)S(1)}, u32[]{:S(2)}, u32[]{:S(2)}) %all-to-all-start.2) | async-done | bytes 32800 | tf_op jit(solution)/shard_map/all_to_all | solution.py:504
  133.8 0.7 broadcast_in_dim.61
  134.5 5.6 %all-to-all-start.3 = ((bf16[32,16,128]{2,1,0:T(8,128)(2,1)}), bf16[32,16,128]{2,1,0:T(8,128)(2,1)S(1)}, u32[]{:S(2)}, u32[]{:S(2)}) async-start(bf16[32,16,128]{2,1,0:T(8,128)(2,1)} %broadcast_in_dim.61), calls=%async_computation.4 | async-start | bytes 262144 | tf_op jit(solution)/shard_map/all_to_all | solution.py:508
  140.2 10.3 %all-to-all-done.3 = bf16[32,16,128]{2,1,0:T(8,128)(2,1)S(1)} async-done(((bf16[32,16,128]{2,1,0:T(8,128)(2,1)}), bf16[32,16,128]{2,1,0:T(8,128)(2,1)S(1)}, u32[]{:S(2)}, u32[]{:S(2)}) %all-to-all-start.3) | async-done | bytes 131104 | tf_op jit(solution)/shard_map/all_to_all | solution.py:508
  150.7 0.1 copy.32
  150.8 0.1 copy.33
  150.9 0.1 pad_maximum_fusion.3
  151.0 0.1 copy.21
  151.1 0.1 copy.29
  151.2 0.1 copy.30
  151.3 0.1 pad_maximum_fusion.2
  151.4 0.1 copy.19
  151.6 0.1 copy.26
  151.7 0.1 copy.27
  151.8 0.1 pad_maximum_fusion.1
  151.9 0.1 copy.17
  152.4 0.4 concatenate.31
  152.8 0.8 fusion
  153.6 6.7 %reduce-scatter.2.cloned.1.call-done = bf16[32,3072]{1,0:T(8,128)(2,1)} async-done(((bf16[256,3072]{1,0:T(8,128)(2,1)}), bf16[32,3072]{1,0:T(8,128)(2,1)}) %reduce-scatter.2.cloned.1.call-update) | async-done | bytes 196624 | tf_op jit(solution)/shard_map/reduce_scatter | solution.py:494
  160.2 1.7 fusion.1
  (64 shorter events, 1.0 us)
Async XLA Ops:
  7.2 145.6 %copy-start = (bf16[3,3,3,16,64]{4,3,2,1,0:T(8,128)(2,1)S(1)}, bf16[3,3,3,16,64]{4,3,2,1,0:T(8,128)(2,1)}, u32[]{:S(2)}) copy-start(bf16[3,3,3,16,64]{4,3,2,1,0:T(8,128)(2,1)} %param.15) | copy-start | bytes 165892
  7.2 43.8 %collective-permute-start.7 = (bf16[3072,384]{1,0:T(8,128)(2,1)}, bf16[3072,384]{1,0:T(8,128)(2,1)S(1)}, u32[]{:S(2)}, u32[]{:S(2)}) collective-permute-start(bf16[3072,384]{1,0:T(8,128)(2,1)} %bitcast.39), channel_id=1, source_target_pairs={{0,1},{1,0},{2,3},{3,2},{4,5},{5,4},{6,7},{7,6},{8,9},{9,8},{10,11... | collective-permute-start | bytes 7077896 | tf_op jit(solution)/shard_map/ppermute | solution.py:56
  10.0 11.6 %collective-permute-start.2 = (bf16[32,3072]{1,0:T(8,128)(2,1)}, bf16[32,3072]{1,0:T(8,128)(2,1)S(1)}, u32[]{:S(2)}, u32[]{:S(2)}) collective-permute-start(bf16[32,3072]{1,0:T(8,128)(2,1)} %get-tuple-element.18.refs_0_), channel_id=1, source_target_pairs={{0,2},{1,3},{2,4},{3,5},{4,6},{5,7},{6,8},{7,9},{8,10},{9,11},{10,... | collective-permute-start | bytes 589832 | tf_op jit(solution)/shard_map/ppermute | solution.py:48
  11.9 9.7 %collective-permute-start.3 = (bf16[32,3072]{1,0:T(8,128)(2,1)}, bf16[32,3072]{1,0:T(8,128)(2,1)S(1)}, u32[]{:S(2)}, u32[]{:S(2)}) collective-permute-start(bf16[32,3072]{1,0:T(8,128)(2,1)} %get-tuple-element.18.refs_0_), channel_id=1, source_target_pairs={{0,16},{1,17},{2,18},{3,19},{4,20},{5,21},{6,22},{7,23},{8,24},{9,... | collective-permute-start | bytes 589832 | tf_op jit(solution)/shard_map/ppermute | solution.py:52
  12.3 9.3 %collective-permute-start = (bf16[32,3072]{1,0:T(8,128)(2,1)}, bf16[32,3072]{1,0:T(8,128)(2,1)S(1)}, u32[]{:S(2)}, u32[]{:S(2)}) collective-permute-start(bf16[32,3072]{1,0:T(8,128)(2,1)} %get-tuple-element.18.refs_0_), channel_id=1, source_target_pairs={{0,14},{1,15},{2,0},{3,1},{4,2},{5,3},{6,4},{7,5},{8,6},{9,7},{10,... | collective-permute-start | bytes 589832 | tf_op jit(solution)/shard_map/ppermute | solution.py:48
  21.6 7.9 %collective-permute-start.4 = (bf16[32,3072]{1,0:T(8,128)(2,1)S(1)}, bf16[32,3072]{1,0:T(8,128)(2,1)S(1)}, u32[]{:S(2)}, u32[]{:S(2)}) collective-permute-start(bf16[32,3072]{1,0:T(8,128)(2,1)S(1)} %collective-permute-done.2.refs_4_), channel_id=1, source_target_pairs={{0,2},{1,3},{2,4},{3,5},{4,6},{5,7},{6,8},{7,9},{8,10},{9,11},{10,... | collective-permute-start | bytes 589832 | tf_op jit(solution)/shard_map/ppermute | solution.py:48
  21.6 8.4 %collective-permute-start.1 = (bf16[32,3072]{1,0:T(8,128)(2,1)S(1)}, bf16[32,3072]{1,0:T(8,128)(2,1)S(1)}, u32[]{:S(2)}, u32[]{:S(2)}) collective-permute-start(bf16[32,3072]{1,0:T(8,128)(2,1)S(1)} %collective-permute-done.refs_1_), channel_id=1, source_target_pairs={{0,14},{1,15},{2,0},{3,1},{4,2},{5,3},{6,4},{7,5},{8,6},{9,7},{10,... | collective-permute-start | bytes 589832 | tf_op jit(solution)/shard_map/ppermute | solution.py:48
  24.8 8.4 %collective-permute-start.6 = (bf16[32,3072]{1,0:T(8,128)(2,1)S(1)}, bf16[32,3072]{1,0:T(8,128)(2,1)S(1)}, u32[]{:S(2)}, u32[]{:S(2)}) collective-permute-start(bf16[32,3072]{1,0:T(8,128)(2,1)S(1)} %collective-permute-done.2.refs_4_), channel_id=1, source_target_pairs={{0,16},{1,17},{2,18},{3,19},{4,20},{5,21},{6,22},{7,23},{8,24},{9,... | collective-permute-start | bytes 589832 | tf_op jit(solution)/shard_map/ppermute | solution.py:52
  29.5 7.1 %collective-permute-start.10 = (bf16[32,3072]{1,0:T(8,128)(2,1)S(1)}, bf16[32,3072]{1,0:T(8,128)(2,1)S(1)}, u32[]{:S(2)}, u32[]{:S(2)}) collective-permute-start(bf16[32,3072]{1,0:T(8,128)(2,1)S(1)} %collective-permute-done.4.refs_3_), channel_id=1, source_target_pairs={{0,2},{1,3},{2,4},{3,5},{4,6},{5,7},{6,8},{7,9},{8,10},{9,11},{10,... | collective-permute-start | bytes 589832 | tf_op jit(solution)/shard_map/ppermute | solution.py:48
  29.6 7.5 %collective-permute-start.5 = (bf16[32,3072]{1,0:T(8,128)(2,1)S(1)}, bf16[32,3072]{1,0:T(8,128)(2,1)S(1)}, u32[]{:S(2)}, u32[]{:S(2)}) collective-permute-start(bf16[32,3072]{1,0:T(8,128)(2,1)S(1)} %collective-permute-done.refs_1_), channel_id=1, source_target_pairs={{0,16},{1,17},{2,18},{3,19},{4,20},{5,21},{6,22},{7,23},{8,24},{9,... | collective-permute-start | bytes 589832 | tf_op jit(solution)/shard_map/ppermute | solution.py:52
  30.0 7.6 %collective-permute-start.9 = (bf16[32,3072]{1,0:T(8,128)(2,1)S(1)}, bf16[32,3072]{1,0:T(8,128)(2,1)S(1)}, u32[]{:S(2)}, u32[]{:S(2)}) collective-permute-start(bf16[32,3072]{1,0:T(8,128)(2,1)S(1)} %collective-permute-done.1.refs_2_), channel_id=1, source_target_pairs={{0,14},{1,15},{2,0},{3,1},{4,2},{5,3},{6,4},{7,5},{8,6},{9,7},{10,... | collective-permute-start | bytes 589832 | tf_op jit(solution)/shard_map/ppermute | solution.py:48
  33.2 12.1 %collective-permute-start.15 = (bf16[32,3072]{1,0:T(8,128)(2,1)S(1)}, bf16[32,3072]{1,0:T(8,128)(2,1)S(1)}, u32[]{:S(2)}, u32[]{:S(2)}) collective-permute-start(bf16[32,3072]{1,0:T(8,128)(2,1)S(1)} %collective-permute-done.4.refs_3_), channel_id=1, source_target_pairs={{0,16},{1,17},{2,18},{3,19},{4,20},{5,21},{6,22},{7,23},{8,24},{9,... | collective-permute-start | bytes 589832 | tf_op jit(solution)/shard_map/ppermute | solution.py:52
  36.6 11.4 %collective-permute-start.12 = (bf16[32,3072]{1,0:T(8,128)(2,1)S(1)}, bf16[32,3072]{1,0:T(8,128)(2,1)S(1)}, u32[]{:S(2)}, u32[]{:S(2)}) collective-permute-start(bf16[32,3072]{1,0:T(8,128)(2,1)S(1)} %collective-permute-done.1.refs_2_), channel_id=1, source_target_pairs={{0,16},{1,17},{2,18},{3,19},{4,20},{5,21},{6,22},{7,23},{8,24},{9,... | collective-permute-start | bytes 589832 | tf_op jit(solution)/shard_map/ppermute | solution.py:52
  37.1 18.5 %collective-permute-start.11 = (bf16[32,3072]{1,0:T(8,128)(2,1)S(1)}, bf16[32,3072]{1,0:T(8,128)(2,1)S(1)}, u32[]{:S(2)}, u32[]{:S(2)}) collective-permute-start(bf16[32,3072]{1,0:T(8,128)(2,1)S(1)} %collective-permute-done.10.refs_2_), channel_id=1, source_target_pairs={{0,2},{1,3},{2,4},{3,5},{4,6},{5,7},{6,8},{7,9},{8,10},{9,11},{10,... | collective-permute-start | bytes 589832 | tf_op jit(solution)/shard_map/ppermute | solution.py:48
  37.6 17.9 %collective-permute-start.14 = (bf16[32,3072]{1,0:T(8,128)(2,1)S(1)}, bf16[32,3072]{1,0:T(8,128)(2,1)S(1)}, u32[]{:S(2)}, u32[]{:S(2)}) collective-permute-start(bf16[32,3072]{1,0:T(8,128)(2,1)S(1)} %collective-permute-done.9.refs_0_), channel_id=1, source_target_pairs={{0,30},{1,31},{2,16},{3,17},{4,18},{5,19},{6,20},{7,21},{8,22},{9,... | collective-permute-start | bytes 589832 | tf_op jit(solution)/shard_map/ppermute | solution.py:92
  45.3 10.3 %collective-permute-start.16 = (bf16[32,3072]{1,0:T(8,128)(2,1)S(1)}, bf16[32,3072]{1,0:T(8,128)(2,1)S(1)}, u32[]{:S(2)}, u32[]{:S(2)}) collective-permute-start(bf16[32,3072]{1,0:T(8,128)(2,1)S(1)} %collective-permute-done.15.refs_7_), channel_id=1, source_target_pairs={{0,2},{1,3},{2,4},{3,5},{4,6},{5,7},{6,8},{7,9},{8,10},{9,11},{10,... | collective-permute-start | bytes 589832 | tf_op jit(solution)/shard_map/ppermute | solution.py:48
  48.1 7.5 %collective-permute-start.13 = (bf16[32,3072]{1,0:T(8,128)(2,1)S(1)}, bf16[32,3072]{1,0:T(8,128)(2,1)S(1)}, u32[]{:S(2)}, u32[]{:S(2)}) collective-permute-start(bf16[32,3072]{1,0:T(8,128)(2,1)S(1)} %collective-permute-done.12.refs_3_), channel_id=1, source_target_pairs={{0,14},{1,15},{2,0},{3,1},{4,2},{5,3},{6,4},{7,5},{8,6},{9,7},{10,... | collective-permute-start | bytes 589832 | tf_op jit(solution)/shard_map/ppermute | solution.py:48
  51.0 1.7 copy-start.1
  52.7 0.9 copy-start.5
  53.6 2.0 %copy-start.2 = (bf16[1,3072,384]{2,1,0:T(8,128)(2,1)S(1)}, bf16[1,3072,384]{2,1,0:T(8,128)(2,1)}, u32[]{:S(2)}) copy-start(bf16[1,3072,384]{2,1,0:T(8,128)(2,1)} %param.12) | copy-start | bytes 7077892
  55.4 2.6 %copy-start.3 = (bf16[1,128,3072]{2,1,0:T(8,128)(2,1)S(1)}, bf16[1,128,3072]{2,1,0:T(8,128)(2,1)}, u32[]{:S(2)}) copy-start(bf16[1,128,3072]{2,1,0:T(8,128)(2,1)} %param.13) | copy-start | bytes 2359300
  55.4 3.0 %collective-permute-start.8 = (bf16[256,384]{1,0:T(8,128)(2,1)S(1)}, bf16[256,384]{1,0:T(8,128)(2,1)S(1)}, u32[]{:S(2)}, u32[]{:S(2)}) collective-permute-start(bf16[256,384]{1,0:T(8,128)(2,1)S(1)} %get-tuple-element.21), channel_id=1, source_target_pairs={{0,1},{1,0},{2,3},{3,2},{4,5},{5,4},{6,7},{7,6},{8,9},{9,8},{10,11... | collective-permute-start | bytes 589832 | tf_op jit(solution)/shard_map/ppermute | solution.py:56
  57.4 6.1 %copy-start.4 = (bf16[3072,64]{0,1:T(8,128)(2,1)S(1)}, bf16[3072,64]{0,1:T(8,128)(2,1)}, u32[]{:S(2)}) copy-start(bf16[3072,64]{0,1:T(8,128)(2,1)} %param.14) | copy-start | bytes 1179652
  57.4 6.1 %copy-start.6 = (f32[1,3072]{1,0:T(1,128)S(1)}, f32[1,3072]{1,0:T(1,128)}, u32[]{:S(2)}) copy-start(f32[1,3072]{1,0:T(1,128)} %get-tuple-element.17.gate_ref) | copy-start | bytes 36868
  57.4 1.6 collective-permute-start.17
  58.0 30.6 %collective-permute-start.23 = (bf16[128,3072]{1,0:T(8,128)(2,1)S(1)}, bf16[128,3072]{1,0:T(8,128)(2,1)S(1)}, u32[]{:S(2)}, u32[]{:S(2)}) collective-permute-start(bf16[128,3072]{1,0:T(8,128)(2,1)S(1)} %bitcast.42), channel_id=1, source_target_pairs={{0,16},{1,17},{2,18},{3,19},{4,20},{5,21},{6,22},{7,23},{8,24},{9,... | collective-permute-start | bytes 2359304 | tf_op jit(solution)/shard_map/ppermute | solution.py:52
  59.1 1.6 copy-start.9
  59.2 29.9 %collective-permute-start.19 = (bf16[1024,256]{1,0:T(8,128)(2,1)S(1)}, bf16[1024,256]{1,0:T(8,128)(2,1)}, u32[]{:S(2)}, u32[]{:S(2)}) collective-permute-start(bf16[1024,256]{1,0:T(8,128)(2,1)S(1)} %slice.178.kv_ref.k0), channel_id=1, source_target_pairs={{0,64},{32,96},{64,128},{96,160},{128,192},{160,224},{192,0},{224,... | collective-permute-start | bytes 1572872 | tf_op jit(solution)/shard_map/ppermute | solution.py:60
  60.7 28.3 %collective-permute-start.20 = (bf16[1024,256]{1,0:T(8,128)(2,1)S(1)}, bf16[1024,256]{1,0:T(8,128)(2,1)}, u32[]{:S(2)}, u32[]{:S(2)}) collective-permute-start(bf16[1024,256]{1,0:T(8,128)(2,1)S(1)} %slice.178.kv_ref.k0), channel_id=1, source_target_pairs={{0,192},{32,224},{64,0},{96,32},{128,64},{160,96},{192,128},{224,1... | collective-permute-start | bytes 1572872 | tf_op jit(solution)/shard_map/ppermute | solution.py:60
  61.3 27.8 %collective-permute-start.21 = (bf16[1024,256]{1,0:T(8,128)(2,1)S(1)}, bf16[1024,256]{1,0:T(8,128)(2,1)}, u32[]{:S(2)}, u32[]{:S(2)}) collective-permute-start(bf16[1024,256]{1,0:T(8,128)(2,1)S(1)} %slice.178.kv_ref.k0), channel_id=1, source_target_pairs={{0,128},{32,160},{64,192},{96,224},{128,0},{160,32},{192,64},{224,... | collective-permute-start | bytes 1572872 | tf_op jit(solution)/shard_map/ppermute | solution.py:60
  63.5 25.6 %copy-start.7 = (s32[8]{0:T(128)S(1)}, s32[8]{0:T(128)}, u32[]{:S(2)}) copy-start(s32[8]{0:T(128)} %order_ref.1) | copy-start | bytes 100
  65.0 23.5 %collective-permute-start.18 = (bf16[1024,128]{1,0:T(8,128)(2,1)S(1)}, bf16[1024,128]{1,0:T(8,128)(2,1)S(1)}, u32[]{:S(2)}, u32[]{:S(2)}) collective-permute-start(bf16[1024,128]{1,0:T(8,128)(2,1)S(1)} %slice.177.q_ref.qa_ref), channel_id=1, source_target_pairs={{0,32},{32,0},{64,96},{96,64},{128,160},{160,128},{192,224},{224,1... | collective-permute-start | bytes 786440 | tf_op jit(solution)/shard_map/ppermute | solution.py:64
  88.6 15.7 %collective-permute-start.22 = (bf16[128,3072]{1,0:T(8,128)(2,1)S(1)}, bf16[128,3072]{1,0:T(8,128)(2,1)}, u32[]{:S(2)}, u32[]{:S(2)}) collective-permute-start(bf16[128,3072]{1,0:T(8,128)(2,1)S(1)} %bitcast.44), channel_id=1, source_target_pairs={{0,1},{1,0},{2,3},{3,2},{4,5},{5,4},{6,7},{7,6},{8,9},{9,8},{10,11... | collective-permute-start | bytes 2359304 | tf_op jit(solution)/shard_map/ppermute | solution.py:56
  88.6 24.7 %collective-permute-start.24 = (bf16[128,3072]{1,0:T(8,128)(2,1)S(1)}, bf16[128,3072]{1,0:T(8,128)(2,1)}, u32[]{:S(2)}, u32[]{:S(2)}) collective-permute-start(bf16[128,3072]{1,0:T(8,128)(2,1)S(1)} %collective-permute-done.23.w2_ref), channel_id=1, source_target_pairs={{0,1},{1,0},{2,3},{3,2},{4,5},{5,4},{6,7},{7,6},{8,9},{9,8},{10,11... | collective-permute-start | bytes 2359304 | tf_op jit(solution)/shard_map/ppermute | solution.py:56
  89.1 15.0 %copy-start.8 = (bf16[1,32,3072]{2,1,0:T(8,128)(2,1)S(1)}, bf16[1,32,3072]{2,1,0:T(8,128)(2,1)}, u32[]{:S(2)}) copy-start(bf16[1,32,3072]{2,1,0:T(8,128)(2,1)} %param.8) | copy-start | bytes 589828
  94.4 19.0 %all-to-all-start.1 = ((bf16[8,272,128]{2,1,0:T(8,128)(2,1)}), bf16[8,272,128]{2,1,0:T(8,128)(2,1)S(1)}, u32[]{:S(2)}, u32[]{:S(2)}) async-start(bf16[8,272,128]{2,1,0:T(8,128)(2,1)} %other_attention.1), calls=%async_computation.1 | async-start | bytes 1114112 | tf_op jit(solution)/shard_map/all_to_all | solution.py:488
  104.1 56.1 %reduce-scatter.2.cloned.1.call-start = ((), (), s32[]{:S(2)}) async-start(), calls=%async_computation.5 | async-start | bytes 1769472 | tf_op jit(solution)/shard_map/reduce_scatter | solution.py:494
  119.5 14.4 %all-to-all-start.2 = ((bf16[8,16,128]{2,1,0:T(8,128)(2,1)}), bf16[8,16,128]{2,1,0:T(8,128)(2,1)S(1)}, u32[]{:S(2)}, u32[]{:S(2)}) async-start(bf16[8,16,128]{2,1,0:T(8,128)(2,1)} %broadcast_in_dim.59), calls=%async_computation.3 | async-start | bytes 65536 | tf_op jit(solution)/shard_map/all_to_all | solution.py:504
  134.5 16.0 %all-to-all-start.3 = ((bf16[32,16,128]{2,1,0:T(8,128)(2,1)}), bf16[32,16,128]{2,1,0:T(8,128)(2,1)S(1)}, u32[]{:S(2)}, u32[]{:S(2)}) async-start(bf16[32,16,128]{2,1,0:T(8,128)(2,1)} %broadcast_in_dim.61), calls=%async_computation.4 | async-start | bytes 262144 | tf_op jit(solution)/shard_map/all_to_all | solution.py:508
Sparse Core Ops, SparseCore 0:
  118.8 41.3 reduce-scatter.1

commit v5 on v1

--- a/solution.py
+++ b/solution.py
@@ -473,8 +473,8 @@
     w_core, w_far = move_core(out_w), move_y(out_w)
     weights = (out_w, w_core, w_far, move_core(w_far))
 
-    acc = after(acc, part)
     chunks = other_attention(span_order, place, q, q_hi, acc, top, (kv, *others))
+    chunks = after(chunks, part)
     groups = [
         [
             span_at(i, hh) * seq_count + seq_at(yy, j, cc)

time: 166 us -> 168 us (1.012)
  blocking collectives: 15.9 us -> 0 us
  starting transfers between devices: 38.5 us -> 48.7 us
  waiting for transfers between devices: 54.5 us -> 58.5 us
  local copies, waits for them, and re-layouts: 6.68 us -> 9.77 us
    all_to_all x1 -> x0, blocking collectives: 15.9 us -> none  [per_device(): part = lax.all_to_all(part, 'seq', 0, 0, tiled=True)]
    all_to_all x0 -> x1, starting transfers between devices: none -> 7.04 us  [per_device(): part = lax.all_to_all(part, 'seq', 0, 0, tiled=True)]
    unnamed x29 -> x35, local copies, waits for them, and re-layouts: 3.34 us -> 7.39 us
    ppermute x1, waiting for transfers between devices: 0.01 us -> 3.16 us  [move_hi(): return lax.ppermute(a, 'span', span_route(dh=1))]
    all_to_all x1, starting transfers between devices: 6.33 us -> 8.52 us  [per_device(): lax.all_to_all(chunks, ('span', 'seq'), 0, 0, tiled=True, axis_index_grou...]
    all_to_all x1, starting transfers between devices: 5.04 us -> 6.98 us  [per_device(): lax.all_to_all(jnp.broadcast_to(latents, (seq_count,) + latents.shape[1:]...]
  transfers between devices with their start and end apart: 29 -> 30, of which waited for: 12 -> 14; matrix products, arithmetic and copies ran while one was open for 4% -> 4% of each run, Pallas kernels for 13% -> 13%
where the time goes in v5:
time: 168 us; the launch traced here: 167 us
  waiting for transfers between devices  58.5 us (35%)
  starting transfers between devices  48.7 us (29%)
  Pallas kernels  27.9 us (17%)
  between operations  17.1 us (10%)
  local copies, waits for them, and re-layouts  9.77 us (6%)
  other arithmetic  3.86 us (2%)
    ppermute x6, waiting for transfers between devices, move_y(): return lax.ppermute(a, 'seq', seq_route(dy=1))  13.3 us
    pallas_call x1, Pallas kernels, other_attention(): pl.pallas_call(other_kernel, grid_spec=pltpu.PrefetchScalarGridSpec(num_s...  10.4 us
    ppermute x9, waiting for transfers between devices, move_z(): return lax.ppermute(a, 'seq', seq_route(dz=d))  10.3 us
    all_to_all x1, waiting for transfers between devices, per_device(): lax.all_to_all(jnp.broadcast_to(latents, (seq_count,) + latents.shape[1:]...  10 us
    ppermute x9, starting transfers between devices, move_z(): return lax.ppermute(a, 'seq', seq_route(dz=d))  9.66 us
    all_to_all x1, waiting for transfers between devices, per_device(): lax.all_to_all(chunks, ('span', 'seq'), 0, 0, tiled=True, axis_index_grou...  9 us
    all_to_all x1, starting transfers between devices, per_device(): lax.all_to_all(chunks, ('span', 'seq'), 0, 0, tiled=True, axis_index_grou...  8.52 us
    unnamed x35, local copies, waits for them, and re-layouts  7.39 us
  transfers between devices with their start and end apart: 30, of which 14 were waited for; matrix products, arithmetic and copies ran while one was open for 4% of the time, Pallas kernels for 13%

profile of v5, /device:TPU:10, one launch (start us, length us, event | category | flops | bytes accessed | tf_op | source)
XLA Modules:
  0.0 166.9 jit_solution(9478364175841471659)
XLA Ops:
  7.2 0.1 collective-permute-start.7
  7.9 2.0 %normalize.1 = (bf16[32,3072]{1,0:T(8,128)(2,1)}, f32[1,3072]{1,0:T(1,128)}) custom-call(s32[1]{0:T(128)S(6)} %copy.37.level_ref, bf16[32,3072]{1,0:T(8,128)(2,1)} %bitcast.48, f32[3,16,3072]{2,1,0:T(8,128)} %bitcast.49), custom_call_target="tpu_custom_call" | custom-call | tf_op jit(solution)/shard_map/normalize/pallas_call | solution.py:114
  10.0 1.9 %collective-permute-start.2 = (bf16[32,3072]{1,0:T(8,128)(2,1)}, bf16[32,3072]{1,0:T(8,128)(2,1)S(1)}, u32[]{:S(2)}, u32[]{:S(2)}) collective-permute-start(bf16[32,3072]{1,0:T(8,128)(2,1)} %get-tuple-element.15.refs_0_), channel_id=1, source_target_pairs={{0,2},{1,3},{2,4},{3,5},{4,6},{5,7},{6,8},{7,9},{8,10},{9,11},{10,... | collective-permute-start | bytes 589832 | tf_op jit(solution)/shard_map/ppermute | solution.py:48
  11.9 3.9 %collective-permute-start = (bf16[32,3072]{1,0:T(8,128)(2,1)}, bf16[32,3072]{1,0:T(8,128)(2,1)S(1)}, u32[]{:S(2)}, u32[]{:S(2)}) collective-permute-start(bf16[32,3072]{1,0:T(8,128)(2,1)} %get-tuple-element.15.refs_0_), channel_id=1, source_target_pairs={{0,14},{1,15},{2,0},{3,1},{4,2},{5,3},{6,4},{7,5},{8,6},{9,7},{10,... | collective-permute-start | bytes 589832 | tf_op jit(solution)/shard_map/ppermute | solution.py:48
  15.8 0.4 collective-permute-start.4
  16.3 5.3 %collective-permute-done.2.refs_4_ = bf16[32,3072]{1,0:T(8,128)(2,1)S(1)} collective-permute-done((bf16[32,3072]{1,0:T(8,128)(2,1)}, bf16[32,3072]{1,0:T(8,128)(2,1)S(1)}, u32[]{:S(2)}, u32[]{:S(2)}) %collective-permute-start.2) | collective-permute-done | bytes 196640 | tf_op jit(solution)/shard_map/ppermute | solution.py:48
  21.6 3.2 %collective-permute-start.1 = (bf16[32,3072]{1,0:T(8,128)(2,1)S(1)}, bf16[32,3072]{1,0:T(8,128)(2,1)S(1)}, u32[]{:S(2)}, u32[]{:S(2)}) collective-permute-start(bf16[32,3072]{1,0:T(8,128)(2,1)S(1)} %collective-permute-done.refs_1_), channel_id=1, source_target_pairs={{0,14},{1,15},{2,0},{3,1},{4,2},{5,3},{6,4},{7,5},{8,6},{9,7},{10,... | collective-permute-start | bytes 589832 | tf_op jit(solution)/shard_map/ppermute | solution.py:48
  24.8 0.4 collective-permute-start.5
  25.3 1.6 collective-permute-start.6
  26.9 2.7 %collective-permute-done.3.refs_3_ = bf16[32,3072]{1,0:T(8,128)(2,1)S(1)} collective-permute-done((bf16[32,3072]{1,0:T(8,128)(2,1)S(1)}, bf16[32,3072]{1,0:T(8,128)(2,1)S(1)}, u32[]{:S(2)}, u32[]{:S(2)}) %collective-permute-start.3) | collective-permute-done | bytes 196640 | tf_op jit(solution)/shard_map/ppermute | solution.py:48
  29.6 0.5 collective-permute-start.12
  30.0 2.7 %collective-permute-done.5.refs_6_ = bf16[32,3072]{1,0:T(8,128)(2,1)S(1)} collective-permute-done((bf16[32,3072]{1,0:T(8,128)(2,1)S(1)}, bf16[32,3072]{1,0:T(8,128)(2,1)S(1)}, u32[]{:S(2)}, u32[]{:S(2)}) %collective-permute-start.5) | collective-permute-done | bytes 196640 | tf_op jit(solution)/shard_map/ppermute | solution.py:52
  32.7 0.6 collective-permute-start.9
  33.2 3.7 %collective-permute-done.6.refs_7_ = bf16[32,3072]{1,0:T(8,128)(2,1)S(1)} collective-permute-done((bf16[32,3072]{1,0:T(8,128)(2,1)S(1)}, bf16[32,3072]{1,0:T(8,128)(2,1)S(1)}, u32[]{:S(2)}, u32[]{:S(2)}) %collective-permute-start.6) | collective-permute-done | bytes 196640 | tf_op jit(solution)/shard_map/ppermute | solution.py:52
  36.9 0.4 collective-permute-start.15
  37.4 3.8 %collective-permute-done.12.refs_3_ = bf16[32,3072]{1,0:T(8,128)(2,1)S(1)} collective-permute-done((bf16[32,3072]{1,0:T(8,128)(2,1)S(1)}, bf16[32,3072]{1,0:T(8,128)(2,1)S(1)}, u32[]{:S(2)}, u32[]{:S(2)}) %collective-permute-start.12) | collective-permute-done | bytes 196640 | tf_op jit(solution)/shard_map/ppermute | solution.py:52
  41.1 1.4 collective-permute-start.14
  42.5 3.2 %collective-permute-done.15.refs_7_ = bf16[32,3072]{1,0:T(8,128)(2,1)S(1)} collective-permute-done((bf16[32,3072]{1,0:T(8,128)(2,1)S(1)}, bf16[32,3072]{1,0:T(8,128)(2,1)S(1)}, u32[]{:S(2)}, u32[]{:S(2)}) %collective-permute-start.15) | collective-permute-done | bytes 196640 | tf_op jit(solution)/shard_map/ppermute | solution.py:52
  45.8 1.7 copy-done.1
  47.4 0.9 copy-done.5
  48.4 1.8 %project.2 = (bf16[256,384]{1,0:T(8,128)(2,1)S(1)}, bf16[256,384]{1,0:T(8,128)(2,1)S(1)}) custom-call(bf16[32,3072]{1,0:T(8,128)(2,1)S(1)} %copy-done.5, bf16[32,3072]{1,0:T(8,128)(2,1)S(1)} %collective-permute-done.refs_1_, bf16[32,3072]{1,0:T(8,128)(2,1)S(1)} %collective-permute-done.1.refs_2_, bf16[32,3072]{1,0:T(8,128)(2,1)S(1)} %collective-permute-done.3.refs_3_, ...), custom_call_target="tpu_custom_call" | custom-call | flops 1207959552 | bytes 6291456 | tf_op jit(solution)/shard_map/project/pallas_call | solution.py:170
  50.3 2.3 %collective-permute-done.16.refs_6_ = bf16[32,3072]{1,0:T(8,128)(2,1)S(1)} collective-permute-done((bf16[32,3072]{1,0:T(8,128)(2,1)S(1)}, bf16[32,3072]{1,0:T(8,128)(2,1)S(1)}, u32[]{:S(2)}, u32[]{:S(2)}) %collective-permute-start.16) | collective-permute-done | bytes 196640 | tf_op jit(solution)/shard_map/ppermute | solution.py:48
  52.6 1.8 %project.3 = (bf16[256,384]{1,0:T(8,128)(2,1)S(1)}, bf16[256,384]{1,0:T(8,128)(2,1)S(1)}) custom-call(bf16[32,3072]{1,0:T(8,128)(2,1)S(1)} %collective-permute-done.9.refs_0_, bf16[32,3072]{1,0:T(8,128)(2,1)S(1)} %collective-permute-done.11.refs_1_, bf16[32,3072]{1,0:T(8,128)(2,1)S(1)} %collective-permute-done.10.refs_2_, ...), custom_call_target="tpu_custom_call" | custom-call | flops 1207959552 | bytes 6291456 | tf_op jit(solution)/shard_map/project/pallas_call | solution.py:170
  54.8 1.2 collective-permute-done.17
  56.1 1.6 collective-permute-start.19
  57.7 0.5 collective-permute-start.20
  58.2 2.1 %collective-permute-start.21 = (bf16[1024,256]{1,0:T(8,128)(2,1)S(1)}, bf16[1024,256]{1,0:T(8,128)(2,1)}, u32[]{:S(2)}, u32[]{:S(2)}) collective-permute-start(bf16[1024,256]{1,0:T(8,128)(2,1)S(1)} %slice.178.kv_ref.k0), channel_id=1, source_target_pairs={{0,128},{32,160},{64,192},{96,224},{128,0},{160,32},{192,64},{224,... | collective-permute-start | bytes 1572872 | tf_op jit(solution)/shard_map/ppermute | solution.py:60
  60.4 2.4 %collective-permute-start.18 = (bf16[1024,128]{1,0:T(8,128)(2,1)S(1)}, bf16[1024,128]{1,0:T(8,128)(2,1)S(1)}, u32[]{:S(2)}, u32[]{:S(2)}) collective-permute-start(bf16[1024,128]{1,0:T(8,128)(2,1)S(1)} %slice.177.q_ref.qa_ref), channel_id=1, source_target_pairs={{0,32},{32,0},{64,96},{96,64},{128,160},{160,128},{192,224},{224,1... | collective-permute-start | bytes 786440 | tf_op jit(solution)/shard_map/ppermute | solution.py:64
  62.8 0.6 latent_matrix.1.m_ref
  63.4 5.9 %self_attention.1 = (bf16[32,16,128]{2,1,0:T(8,128)(2,1)}, f32[1024,256]{1,0:T(8,128)S(1)}, f32[1024,128]{1,0:T(8,128)S(1)}) custom-call(s32[5]{0:T(128)S(1)} %stack.23.s_ref, bf16[1024,128]{1,0:T(8,128)(2,1)S(1)} %slice.177.q_ref.qa_ref, bf16[1024,256]{1,0:T(8,128)(2,1)S(1)} %slice.178.kv_ref.k0, bf16[256,64]{1,0:T(8,128)(2,1)S(1)} %latent_matrix.1.m_ref), custom_call_target="tpu_custom_call" | custom-call | flops 805306368 | bytes 1048576 | tf_op jit(solution)/shard_map/self_attention/pallas_call | solution.py:225
  69.3 1.0 copy-done.8
  70.3 0.8 copy-done.10
  71.1 7.0 %all-to-all-start = ((bf16[32,16,128]{2,1,0:T(8,128)(2,1)}), bf16[32,16,128]{2,1,0:T(8,128)(2,1)}, u32[]{:S(2)}, u32[]{:S(2)}) async-start(bf16[32,16,128]{2,1,0:T(8,128)(2,1)} %get-tuple-element.23), calls=%async_computation | async-start | bytes 262144 | tf_op jit(solution)/shard_map/all_to_all | solution.py:470
  78.1 3.2 %collective-permute-done.18.qb_ref = bf16[1024,128]{1,0:T(8,128)(2,1)S(1)} collective-permute-done((bf16[1024,128]{1,0:T(8,128)(2,1)S(1)}, bf16[1024,128]{1,0:T(8,128)(2,1)S(1)}, u32[]{:S(2)}, u32[]{:S(2)}) %collective-permute-start.18) | collective-permute-done | bytes 262176 | tf_op jit(solution)/shard_map/ppermute | solution.py:64
  81.3 0.5 collective-permute-start.24
  81.8 1.5 collective-permute-done.21.k3
  83.3 1.2 copy-done.9
  84.6 1.0 copy-done.11
  85.6 10.4 %other_attention.1 = bf16[8,272,128]{2,1,0:T(8,128)(2,1)} custom-call(s32[8]{0:T(128)S(1)} %copy-done.7, s32[5]{0:T(128)S(1)} %stack.23.s_ref, bf16[1024,128]{1,0:T(8,128)(2,1)S(1)} %slice.177.q_ref.qa_ref, bf16[1024,128]{1,0:T(8,128)(2,1)S(1)} %collective-permute-done.18.qb_ref, f32[1024,256]{1,0:T(8,128)S(1)} %copy-done.9, f32[1024,128]{1,0:T(8,128)S(1)} %copy-done.11, ...), custom_call_target="tpu_custom_call" | custom-call | flops 4831838208 | bytes 4194304 | tf_op jit(solution)/shard_map/other_attention/pallas_call | solution.py:327
  96.0 8.5 %all-to-all-start.1 = ((bf16[8,272,128]{2,1,0:T(8,128)(2,1)}), bf16[8,272,128]{2,1,0:T(8,128)(2,1)S(1)}, u32[]{:S(2)}, u32[]{:S(2)}) async-start(bf16[8,272,128]{2,1,0:T(8,128)(2,1)} %other_attention.1), calls=%async_computation.1 | async-start | bytes 1114112 | tf_op jit(solution)/shard_map/all_to_all | solution.py:488
  104.5 0.2 fusion.4
  104.8 9.0 %all-to-all-done.1.in_ref = bf16[8,272,128]{2,1,0:T(8,128)(2,1)S(1)} async-done(((bf16[8,272,128]{2,1,0:T(8,128)(2,1)}), bf16[8,272,128]{2,1,0:T(8,128)(2,1)S(1)}, u32[]{:S(2)}, u32[]{:S(2)}) %all-to-all-start.1) | async-done | bytes 557088 | tf_op jit(solution)/shard_map/all_to_all | solution.py:488
  113.8 5.4 %join_heads.1 = bf16[256,3072]{1,0:T(8,128)(2,1)} custom-call(s32[5]{0:T(128)S(1)} %stack.23.s_ref, bf16[8,272,128]{2,1,0:T(8,128)(2,1)S(1)} %all-to-all-done.1.in_ref, bf16[128,3072]{1,0:T(8,128)(2,1)S(1)} %bitcast.45, bf16[128,3072]{1,0:T(8,128)(2,1)} %collective-permute-done.22.w1_ref, bf16[128,3072]{1,0:T(8,128)(2,1)S(1)} %collective-permute-done.23.w2_ref, ...), custom_call_target="tpu_custom_call" | custom-call | tf_op jit(solution)/shard_map/join_heads/pallas_call | solution.py:386
  119.2 0.9 convert_reduce_fusion
  120.2 0.6 broadcast_in_dim.59
  120.9 4.2 %all-to-all-start.2 = ((bf16[8,16,128]{2,1,0:T(8,128)(2,1)}), bf16[8,16,128]{2,1,0:T(8,128)(2,1)S(1)}, u32[]{:S(2)}, u32[]{:S(2)}) async-start(bf16[8,16,128]{2,1,0:T(8,128)(2,1)} %broadcast_in_dim.59), calls=%async_computation.3 | async-start | bytes 65536 | tf_op jit(solution)/shard_map/all_to_all | solution.py:504
  125.1 0.6 fusion.3
  127.6 3.7 %all-to-all-done.2 = bf16[8,16,128]{2,1,0:T(8,128)(2,1)S(1)} async-done(((bf16[8,16,128]{2,1,0:T(8,128)(2,1)}), bf16[8,16,128]{2,1,0:T(8,128)(2,1)S(1)}, u32[]{:S(2)}, u32[]{:S(2)}) %all-to-all-start.2) | async-done | bytes 32800 | tf_op jit(solution)/shard_map/all_to_all | solution.py:504
  131.3 0.7 broadcast_in_dim.61
  132.0 7.0 %all-to-all-start.3 = ((bf16[32,16,128]{2,1,0:T(8,128)(2,1)}), bf16[32,16,128]{2,1,0:T(8,128)(2,1)S(1)}, u32[]{:S(2)}, u32[]{:S(2)}) async-start(bf16[32,16,128]{2,1,0:T(8,128)(2,1)} %broadcast_in_dim.61), calls=%async_computation.4 | async-start | bytes 262144 | tf_op jit(solution)/shard_map/all_to_all | solution.py:508
  139.1 10.0 %all-to-all-done.3 = bf16[32,16,128]{2,1,0:T(8,128)(2,1)S(1)} async-done(((bf16[32,16,128]{2,1,0:T(8,128)(2,1)}), bf16[32,16,128]{2,1,0:T(8,128)(2,1)S(1)}, u32[]{:S(2)}, u32[]{:S(2)}) %all-to-all-start.3) | async-done | bytes 131104 | tf_op jit(solution)/shard_map/all_to_all | solution.py:508
  149.3 0.1 copy.32
  149.4 0.1 copy.33
  149.6 0.1 copy.21
  149.7 0.1 copy.29
  149.8 0.1 copy.30
  150.0 0.1 copy.19
  150.1 0.1 copy.26
  150.2 0.1 copy.27
  150.4 0.1 copy.17
  150.9 0.3 concatenate.31
  151.3 0.8 fusion
  152.1 6.3 %reduce-scatter.2.cloned.1.call-done = bf16[32,3072]{1,0:T(8,128)(2,1)} async-done(((bf16[256,3072]{1,0:T(8,128)(2,1)}), bf16[32,3072]{1,0:T(8,128)(2,1)}) %reduce-scatter.2.cloned.1.call-update) | async-done | bytes 196624 | tf_op jit(solution)/shard_map/reduce_scatter | solution.py:494
  158.4 1.7 fusion.1
  (71 shorter events, 1.5 us)
Async XLA Ops:
  7.2 144.1 %copy-start = (bf16[3,3,3,16,64]{4,3,2,1,0:T(8,128)(2,1)S(1)}, bf16[3,3,3,16,64]{4,3,2,1,0:T(8,128)(2,1)}, u32[]{:S(2)}) copy-start(bf16[3,3,3,16,64]{4,3,2,1,0:T(8,128)(2,1)} %param.15) | copy-start | bytes 165892
  7.2 38.6 %collective-permute-start.7 = (bf16[3072,384]{1,0:T(8,128)(2,1)}, bf16[3072,384]{1,0:T(8,128)(2,1)S(1)}, u32[]{:S(2)}, u32[]{:S(2)}) collective-permute-start(bf16[3072,384]{1,0:T(8,128)(2,1)} %bitcast.39), channel_id=1, source_target_pairs={{0,1},{1,0},{2,3},{3,2},{4,5},{5,4},{6,7},{7,6},{8,9},{9,8},{10,11... | collective-permute-start | bytes 7077896 | tf_op jit(solution)/shard_map/ppermute | solution.py:56
  10.0 11.6 %collective-permute-start.2 = (bf16[32,3072]{1,0:T(8,128)(2,1)}, bf16[32,3072]{1,0:T(8,128)(2,1)S(1)}, u32[]{:S(2)}, u32[]{:S(2)}) collective-permute-start(bf16[32,3072]{1,0:T(8,128)(2,1)} %get-tuple-element.15.refs_0_), channel_id=1, source_target_pairs={{0,2},{1,3},{2,4},{3,5},{4,6},{5,7},{6,8},{7,9},{8,10},{9,11},{10,... | collective-permute-start | bytes 589832 | tf_op jit(solution)/shard_map/ppermute | solution.py:48
  11.9 9.7 %collective-permute-start = (bf16[32,3072]{1,0:T(8,128)(2,1)}, bf16[32,3072]{1,0:T(8,128)(2,1)S(1)}, u32[]{:S(2)}, u32[]{:S(2)}) collective-permute-start(bf16[32,3072]{1,0:T(8,128)(2,1)} %get-tuple-element.15.refs_0_), channel_id=1, source_target_pairs={{0,14},{1,15},{2,0},{3,1},{4,2},{5,3},{6,4},{7,5},{8,6},{9,7},{10,... | collective-permute-start | bytes 589832 | tf_op jit(solution)/shard_map/ppermute | solution.py:48
  15.8 9.5 %collective-permute-start.4 = (bf16[32,3072]{1,0:T(8,128)(2,1)}, bf16[32,3072]{1,0:T(8,128)(2,1)S(1)}, u32[]{:S(2)}, u32[]{:S(2)}) collective-permute-start(bf16[32,3072]{1,0:T(8,128)(2,1)} %get-tuple-element.15.refs_0_), channel_id=1, source_target_pairs={{0,16},{1,17},{2,18},{3,19},{4,20},{5,21},{6,22},{7,23},{8,24},{9,... | collective-permute-start | bytes 589832 | tf_op jit(solution)/shard_map/ppermute | solution.py:52
  21.6 7.9 %collective-permute-start.3 = (bf16[32,3072]{1,0:T(8,128)(2,1)S(1)}, bf16[32,3072]{1,0:T(8,128)(2,1)S(1)}, u32[]{:S(2)}, u32[]{:S(2)}) collective-permute-start(bf16[32,3072]{1,0:T(8,128)(2,1)S(1)} %collective-permute-done.2.refs_4_), channel_id=1, source_target_pairs={{0,2},{1,3},{2,4},{3,5},{4,6},{5,7},{6,8},{7,9},{8,10},{9,11},{10,... | collective-permute-start | bytes 589832 | tf_op jit(solution)/shard_map/ppermute | solution.py:48
  21.6 7.9 %collective-permute-start.1 = (bf16[32,3072]{1,0:T(8,128)(2,1)S(1)}, bf16[32,3072]{1,0:T(8,128)(2,1)S(1)}, u32[]{:S(2)}, u32[]{:S(2)}) collective-permute-start(bf16[32,3072]{1,0:T(8,128)(2,1)S(1)} %collective-permute-done.refs_1_), channel_id=1, source_target_pairs={{0,14},{1,15},{2,0},{3,1},{4,2},{5,3},{6,4},{7,5},{8,6},{9,7},{10,... | collective-permute-start | bytes 589832 | tf_op jit(solution)/shard_map/ppermute | solution.py:48
  24.8 7.8 %collective-permute-start.5 = (bf16[32,3072]{1,0:T(8,128)(2,1)S(1)}, bf16[32,3072]{1,0:T(8,128)(2,1)S(1)}, u32[]{:S(2)}, u32[]{:S(2)}) collective-permute-start(bf16[32,3072]{1,0:T(8,128)(2,1)S(1)} %collective-permute-done.refs_1_), channel_id=1, source_target_pairs={{0,16},{1,17},{2,18},{3,19},{4,20},{5,21},{6,22},{7,23},{8,24},{9,... | collective-permute-start | bytes 589832 | tf_op jit(solution)/shard_map/ppermute | solution.py:52
  25.3 11.6 %collective-permute-start.6 = (bf16[32,3072]{1,0:T(8,128)(2,1)S(1)}, bf16[32,3072]{1,0:T(8,128)(2,1)S(1)}, u32[]{:S(2)}, u32[]{:S(2)}) collective-permute-start(bf16[32,3072]{1,0:T(8,128)(2,1)S(1)} %collective-permute-done.2.refs_4_), channel_id=1, source_target_pairs={{0,16},{1,17},{2,18},{3,19},{4,20},{5,21},{6,22},{7,23},{8,24},{9,... | collective-permute-start | bytes 589832 | tf_op jit(solution)/shard_map/ppermute | solution.py:52
  29.5 7.8 %collective-permute-start.10 = (bf16[32,3072]{1,0:T(8,128)(2,1)S(1)}, bf16[32,3072]{1,0:T(8,128)(2,1)S(1)}, u32[]{:S(2)}, u32[]{:S(2)}) collective-permute-start(bf16[32,3072]{1,0:T(8,128)(2,1)S(1)} %collective-permute-done.3.refs_3_), channel_id=1, source_target_pairs={{0,2},{1,3},{2,4},{3,5},{4,6},{5,7},{6,8},{7,9},{8,10},{9,11},{10,... | collective-permute-start | bytes 589832 | tf_op jit(solution)/shard_map/ppermute | solution.py:48
  29.6 11.6 %collective-permute-start.12 = (bf16[32,3072]{1,0:T(8,128)(2,1)S(1)}, bf16[32,3072]{1,0:T(8,128)(2,1)S(1)}, u32[]{:S(2)}, u32[]{:S(2)}) collective-permute-start(bf16[32,3072]{1,0:T(8,128)(2,1)S(1)} %collective-permute-done.1.refs_2_), channel_id=1, source_target_pairs={{0,16},{1,17},{2,18},{3,19},{4,20},{5,21},{6,22},{7,23},{8,24},{9,... | collective-permute-start | bytes 589832 | tf_op jit(solution)/shard_map/ppermute | solution.py:52
  32.7 8.4 %collective-permute-start.9 = (bf16[32,3072]{1,0:T(8,128)(2,1)S(1)}, bf16[32,3072]{1,0:T(8,128)(2,1)S(1)}, u32[]{:S(2)}, u32[]{:S(2)}) collective-permute-start(bf16[32,3072]{1,0:T(8,128)(2,1)S(1)} %collective-permute-done.1.refs_2_), channel_id=1, source_target_pairs={{0,14},{1,15},{2,0},{3,1},{4,2},{5,3},{6,4},{7,5},{8,6},{9,7},{10,... | collective-permute-start | bytes 589832 | tf_op jit(solution)/shard_map/ppermute | solution.py:48
  36.9 8.9 %collective-permute-start.15 = (bf16[32,3072]{1,0:T(8,128)(2,1)S(1)}, bf16[32,3072]{1,0:T(8,128)(2,1)S(1)}, u32[]{:S(2)}, u32[]{:S(2)}) collective-permute-start(bf16[32,3072]{1,0:T(8,128)(2,1)S(1)} %collective-permute-done.3.refs_3_), channel_id=1, source_target_pairs={{0,16},{1,17},{2,18},{3,19},{4,20},{5,21},{6,22},{7,23},{8,24},{9,... | collective-permute-start | bytes 589832 | tf_op jit(solution)/shard_map/ppermute | solution.py:52
  37.4 12.9 %collective-permute-start.11 = (bf16[32,3072]{1,0:T(8,128)(2,1)S(1)}, bf16[32,3072]{1,0:T(8,128)(2,1)S(1)}, u32[]{:S(2)}, u32[]{:S(2)}) collective-permute-start(bf16[32,3072]{1,0:T(8,128)(2,1)S(1)} %collective-permute-done.10.refs_2_), channel_id=1, source_target_pairs={{0,2},{1,3},{2,4},{3,5},{4,6},{5,7},{6,8},{7,9},{8,10},{9,11},{10,... | collective-permute-start | bytes 589832 | tf_op jit(solution)/shard_map/ppermute | solution.py:48
  41.1 9.2 %collective-permute-start.13 = (bf16[32,3072]{1,0:T(8,128)(2,1)S(1)}, bf16[32,3072]{1,0:T(8,128)(2,1)S(1)}, u32[]{:S(2)}, u32[]{:S(2)}) collective-permute-start(bf16[32,3072]{1,0:T(8,128)(2,1)S(1)} %collective-permute-done.12.refs_3_), channel_id=1, source_target_pairs={{0,14},{1,15},{2,0},{3,1},{4,2},{5,3},{6,4},{7,5},{8,6},{9,7},{10,... | collective-permute-start | bytes 589832 | tf_op jit(solution)/shard_map/ppermute | solution.py:48
  41.1 9.2 %collective-permute-start.14 = (bf16[32,3072]{1,0:T(8,128)(2,1)S(1)}, bf16[32,3072]{1,0:T(8,128)(2,1)S(1)}, u32[]{:S(2)}, u32[]{:S(2)}) collective-permute-start(bf16[32,3072]{1,0:T(8,128)(2,1)S(1)} %collective-permute-done.9.refs_0_), channel_id=1, source_target_pairs={{0,30},{1,31},{2,16},{3,17},{4,18},{5,19},{6,20},{7,21},{8,22},{9,... | collective-permute-start | bytes 589832 | tf_op jit(solution)/shard_map/ppermute | solution.py:92
  45.8 6.9 %collective-permute-start.16 = (bf16[32,3072]{1,0:T(8,128)(2,1)S(1)}, bf16[32,3072]{1,0:T(8,128)(2,1)S(1)}, u32[]{:S(2)}, u32[]{:S(2)}) collective-permute-start(bf16[32,3072]{1,0:T(8,128)(2,1)S(1)} %collective-permute-done.15.refs_7_), channel_id=1, source_target_pairs={{0,2},{1,3},{2,4},{3,5},{4,6},{5,7},{6,8},{7,9},{8,10},{9,11},{10,... | collective-permute-start | bytes 589832 | tf_op jit(solution)/shard_map/ppermute | solution.py:48
  45.8 1.7 copy-start.1
  47.4 0.9 copy-start.5
  48.4 4.3 %copy-start.2 = (bf16[1,3072,384]{2,1,0:T(8,128)(2,1)S(1)}, bf16[1,3072,384]{2,1,0:T(8,128)(2,1)}, u32[]{:S(2)}) copy-start(bf16[1,3072,384]{2,1,0:T(8,128)(2,1)} %param.12) | copy-start | bytes 7077892
  50.2 4.4 %copy-start.3 = (bf16[1,128,3072]{2,1,0:T(8,128)(2,1)S(1)}, bf16[1,128,3072]{2,1,0:T(8,128)(2,1)}, u32[]{:S(2)}) copy-start(bf16[1,128,3072]{2,1,0:T(8,128)(2,1)} %param.13) | copy-start | bytes 2359300
  50.2 4.5 %collective-permute-start.8 = (bf16[256,384]{1,0:T(8,128)(2,1)S(1)}, bf16[256,384]{1,0:T(8,128)(2,1)S(1)}, u32[]{:S(2)}, u32[]{:S(2)}) collective-permute-start(bf16[256,384]{1,0:T(8,128)(2,1)S(1)} %get-tuple-element.17), channel_id=1, source_target_pairs={{0,1},{1,0},{2,3},{3,2},{4,5},{5,4},{6,7},{7,6},{8,9},{9,8},{10,11... | collective-permute-start | bytes 589832 | tf_op jit(solution)/shard_map/ppermute | solution.py:56
  54.5 8.4 %copy-start.4 = (bf16[3072,64]{0,1:T(8,128)(2,1)S(1)}, bf16[3072,64]{0,1:T(8,128)(2,1)}, u32[]{:S(2)}) copy-start(bf16[3072,64]{0,1:T(8,128)(2,1)} %param.14) | copy-start | bytes 1179652
  54.5 8.4 %copy-start.6 = (f32[1,3072]{1,0:T(1,128)S(1)}, f32[1,3072]{1,0:T(1,128)}, u32[]{:S(2)}) copy-start(f32[1,3072]{1,0:T(1,128)} %get-tuple-element.14.gate_ref) | copy-start | bytes 36868
  54.5 1.5 collective-permute-start.17
  54.6 26.7 %collective-permute-start.23 = (bf16[128,3072]{1,0:T(8,128)(2,1)S(1)}, bf16[128,3072]{1,0:T(8,128)(2,1)S(1)}, u32[]{:S(2)}, u32[]{:S(2)}) collective-permute-start(bf16[128,3072]{1,0:T(8,128)(2,1)S(1)} %bitcast.42), channel_id=1, source_target_pairs={{0,16},{1,17},{2,18},{3,19},{4,20},{5,21},{6,22},{7,23},{8,24},{9,... | collective-permute-start | bytes 2359304 | tf_op jit(solution)/shard_map/ppermute | solution.py:52
  56.1 25.7 %collective-permute-start.19 = (bf16[1024,256]{1,0:T(8,128)(2,1)S(1)}, bf16[1024,256]{1,0:T(8,128)(2,1)}, u32[]{:S(2)}, u32[]{:S(2)}) collective-permute-start(bf16[1024,256]{1,0:T(8,128)(2,1)S(1)} %slice.178.kv_ref.k0), channel_id=1, source_target_pairs={{0,64},{32,96},{64,128},{96,160},{128,192},{160,224},{192,0},{224,... | collective-permute-start | bytes 1572872 | tf_op jit(solution)/shard_map/ppermute | solution.py:60
  57.7 24.1 %collective-permute-start.20 = (bf16[1024,256]{1,0:T(8,128)(2,1)S(1)}, bf16[1024,256]{1,0:T(8,128)(2,1)}, u32[]{:S(2)}, u32[]{:S(2)}) collective-permute-start(bf16[1024,256]{1,0:T(8,128)(2,1)S(1)} %slice.178.kv_ref.k0), channel_id=1, source_target_pairs={{0,192},{32,224},{64,0},{96,32},{128,64},{160,96},{192,128},{224,1... | collective-permute-start | bytes 1572872 | tf_op jit(solution)/shard_map/ppermute | solution.py:60
  58.2 25.1 %collective-permute-start.21 = (bf16[1024,256]{1,0:T(8,128)(2,1)S(1)}, bf16[1024,256]{1,0:T(8,128)(2,1)}, u32[]{:S(2)}, u32[]{:S(2)}) collective-permute-start(bf16[1024,256]{1,0:T(8,128)(2,1)S(1)} %slice.178.kv_ref.k0), channel_id=1, source_target_pairs={{0,128},{32,160},{64,192},{96,224},{128,0},{160,32},{192,64},{224,... | collective-permute-start | bytes 1572872 | tf_op jit(solution)/shard_map/ppermute | solution.py:60
  60.3 23.0 %copy-start.7 = (s32[8]{0:T(128)S(1)}, s32[8]{0:T(128)}, u32[]{:S(2)}) copy-start(s32[8]{0:T(128)} %order_ref.1) | copy-start | bytes 100
  60.4 20.9 %collective-permute-start.18 = (bf16[1024,128]{1,0:T(8,128)(2,1)S(1)}, bf16[1024,128]{1,0:T(8,128)(2,1)S(1)}, u32[]{:S(2)}, u32[]{:S(2)}) collective-permute-start(bf16[1024,128]{1,0:T(8,128)(2,1)S(1)} %slice.177.q_ref.qa_ref), channel_id=1, source_target_pairs={{0,32},{32,0},{64,96},{96,64},{128,160},{160,128},{192,224},{224,1... | collective-permute-start | bytes 786440 | tf_op jit(solution)/shard_map/ppermute | solution.py:64
  69.3 1.0 copy-start.8
  70.3 0.8 copy-start.10
  71.1 24.9 %all-to-all-start = ((bf16[32,16,128]{2,1,0:T(8,128)(2,1)}), bf16[32,16,128]{2,1,0:T(8,128)(2,1)}, u32[]{:S(2)}, u32[]{:S(2)}) async-start(bf16[32,16,128]{2,1,0:T(8,128)(2,1)} %get-tuple-element.23), calls=%async_computation | async-start | bytes 262144 | tf_op jit(solution)/shard_map/all_to_all | solution.py:470
  81.3 23.5 %collective-permute-start.22 = (bf16[128,3072]{1,0:T(8,128)(2,1)S(1)}, bf16[128,3072]{1,0:T(8,128)(2,1)}, u32[]{:S(2)}, u32[]{:S(2)}) collective-permute-start(bf16[128,3072]{1,0:T(8,128)(2,1)S(1)} %bitcast.44), channel_id=1, source_target_pairs={{0,1},{1,0},{2,3},{3,2},{4,5},{5,4},{6,7},{7,6},{8,9},{9,8},{10,11... | collective-permute-start | bytes 2359304 | tf_op jit(solution)/shard_map/ppermute | solution.py:56
  81.3 32.5 %collective-permute-start.24 = (bf16[128,3072]{1,0:T(8,128)(2,1)S(1)}, bf16[128,3072]{1,0:T(8,128)(2,1)}, u32[]{:S(2)}, u32[]{:S(2)}) collective-permute-start(bf16[128,3072]{1,0:T(8,128)(2,1)S(1)} %collective-permute-done.23.w2_ref), channel_id=1, source_target_pairs={{0,1},{1,0},{2,3},{3,2},{4,5},{5,4},{6,7},{7,6},{8,9},{9,8},{10,11... | collective-permute-start | bytes 2359304 | tf_op jit(solution)/shard_map/ppermute | solution.py:56
  83.3 1.2 copy-start.9
  84.6 1.0 copy-start.11
  85.6 18.9 %copy-start.12 = (bf16[1,32,3072]{2,1,0:T(8,128)(2,1)S(1)}, bf16[1,32,3072]{2,1,0:T(8,128)(2,1)}, u32[]{:S(2)}) copy-start(bf16[1,32,3072]{2,1,0:T(8,128)(2,1)} %param.8) | copy-start | bytes 589828
  96.0 17.8 %all-to-all-start.1 = ((bf16[8,272,128]{2,1,0:T(8,128)(2,1)}), bf16[8,272,128]{2,1,0:T(8,128)(2,1)S(1)}, u32[]{:S(2)}, u32[]{:S(2)}) async-start(bf16[8,272,128]{2,1,0:T(8,128)(2,1)} %other_attention.1), calls=%async_computation.1 | async-start | bytes 1114112 | tf_op jit(solution)/shard_map/all_to_all | solution.py:488
  104.5 53.8 %reduce-scatter.2.cloned.1.call-start = ((), (), s32[]{:S(2)}) async-start(), calls=%async_computation.5 | async-start | bytes 1769472 | tf_op jit(solution)/shard_map/reduce_scatter | solution.py:494
  120.9 10.5 %all-to-all-start.2 = ((bf16[8,16,128]{2,1,0:T(8,128)(2,1)}), bf16[8,16,128]{2,1,0:T(8,128)(2,1)S(1)}, u32[]{:S(2)}, u32[]{:S(2)}) async-start(bf16[8,16,128]{2,1,0:T(8,128)(2,1)} %broadcast_in_dim.59), calls=%async_computation.3 | async-start | bytes 65536 | tf_op jit(solution)/shard_map/all_to_all | solution.py:504
  132.0 17.1 %all-to-all-start.3 = ((bf16[32,16,128]{2,1,0:T(8,128)(2,1)}), bf16[32,16,128]{2,1,0:T(8,128)(2,1)S(1)}, u32[]{:S(2)}, u32[]{:S(2)}) async-start(bf16[32,16,128]{2,1,0:T(8,128)(2,1)} %broadcast_in_dim.61), calls=%async_computation.4 | async-start | bytes 262144 | tf_op jit(solution)/shard_map/all_to_all | solution.py:508
Sparse Core Ops, SparseCore 0:
  119.3 38.9 reduce-scatter.1
